TPU v7x, 256 devices: a whole 4x4x8 slice. The times are simulated.
256 devices in a mesh: dp: 64 (over z, y, core), group: 4 (over x).
Axes of the slice: x: 4, y: 4, z: 8, core: 2. Of those that a mesh axis runs over, the one named last changes fastest.
Arguments:
- cotangent: bfloat16 [32768, 512], P('dp', 'group'), may hold values from -6 to 6
- saved_inputs: bfloat16 [3, 32768, 512], P(None, 'dp'), may hold values from -6 to 6
- weights: bfloat16 [3, 512, 512], replicated, may hold values from -0.25 to 0.25
- edge_values: bfloat16 [8192, 128, 128], P('dp'), may hold values from -0.25 to 0.25
- edge_rows: int32 [8192], P('dp'), may hold values from 0 to 3
- edge_cols: int32 [8192], P('dp'), may hold values from 0 to 255, as said below
- edge_counts: int32 [64], P('dp'), may hold values from 96 to 128, as said below
- block_owner: int32 [256], replicated, may hold values from 0 to 255, as said below
Outputs:
- input_grad: bfloat16 [32768, 512], P('dp', 'group')
- weight_grad: float32 [3, 512, 512], P(None, None, 'group')
Inputs may be any that keep to these rules, and one draw needn't show every extreme that they name: `edge_cols`: column block ids; among the live edge slots of one dp index, those whose blocks are stored on any one dp index reach at most 2 different column blocks, and some dp index is reached with 2 blocks by the live edges of every dp index. `edge_counts`: number of live slots at the head of each dp index's edge slots; the others are empty. Some dp index has all of its slots live. `block_owner`: each storage position appears once.
All inputs are finite; a program needn't handle non-finite values.
Results may differ from a plain program's by a relative error of at most 0.03.
Values may be sent and summed in bfloat16 or wider, within the bound.
No kernel may reach another device: no remote copies, remote signals or barrier semaphores. Data moves between devices by JAX's collectives and lax.ppermute only.
A program may use at most 128 MiB of HBM per device.

v0:
```python
import math

import jax
import jax.numpy as jnp
from jax import lax
from jax.experimental import pallas as pl
from jax.experimental.pallas import tpu as pltpu
from jax.sharding import PartitionSpec as P

BLK = 128
HOPS = 3
NZ, NY, NC = 8, 4, 2
NX = 4
NB = 4
SLOTS = NZ * NY * NB
EDGES = 256
UNROLL = 8
ITEMS = 264
HALF = 64

bf16 = jnp.bfloat16
f32 = jnp.float32
MB = 1 << 20


def index_of(z, y, c):
    return ((z % NZ) * NY + (y % NY)) * NC + c


def shift(dz=0, dy=0, dc=0):
    return [
        (index_of(z, y, c), index_of(z + dz, y + dy, c ^ dc))
        for z in range(NZ)
        for y in range(NY)
        for c in range(NC)
    ]


Y_GROUPS = [[index_of(z, y, c) for y in range(NY)] for z in range(NZ) for c in range(NC)]
Z_GROUPS = [[index_of(z, y, c) for z in range(NZ)] for y in range(NY) for c in range(NC)]


YZ_GROUPS = [[index_of(z, y, c) for z in range(NZ) for y in range(NY)] for c in range(NC)]
PAIR = (2, NY // 2, NB, HALF, BLK)
SUM_Y_COST = 1
SUMS = 512 // (NZ * NY)
ROWS = NB * HALF + 2 * SUMS
STIE = 4


def cost(us):
    return pl.CostEstimate(flops=0, bytes_accessed=int(us * 3_300_000), transcendentals=0)


def silu_slope(value):
    sigma = jax.nn.sigmoid(value)
    return sigma * (1.0 + value * (1.0 - sigma))


def vmem():
    return pl.BlockSpec(memory_space=pltpu.VMEM)


def params(limit):
    return pltpu.CompilerParams(vmem_limit_bytes=limit)


def factor_kernel(member, x_ref, w_ref, d_ref):
    for r in range(NB):
        z = jnp.dot(x_ref[0, r * BLK : (r + 1) * BLK, :], w_ref[0], preferred_element_type=f32)
        d_ref[r] = silu_slope(z.T)


def factors(member, saved, weights, hop):
    return pl.pallas_call(
        factor_kernel,
        out_shape=jax.ShapeDtypeStruct((NB, BLK, BLK), f32),
        grid_spec=pltpu.PrefetchScalarGridSpec(
            num_scalar_prefetch=1,
            grid=(1,),
            in_specs=[
                pl.BlockSpec((1, 512, 512), lambda i, m: (hop, 0, 0)),
                pl.BlockSpec((1, 512, BLK), lambda i, m: (hop, 0, m[0])),
            ],
            out_specs=pl.BlockSpec((NB, BLK, BLK), lambda i, m: (0, 0, 0)),
        ),
        compiler_params=params(60 * MB),
        name="factors",
    )(member, saved, weights)


def first_kernel(member, x_ref, w_ref, cot_ref, grad_ref, slope_ref):
    for r in range(NB):
        rows = slice(r * BLK, (r + 1) * BLK)
        z = jnp.dot(x_ref[0, rows, :], w_ref[0], preferred_element_type=f32)
        grad = cot_ref[rows, :].astype(f32).T
        grad_ref[r] = grad
        slope_ref[r] = (grad * silu_slope(z.T)).astype(bf16)


def first_slopes(member, saved, weights, cotangent):
    hop = HOPS - 1
    whole = pl.BlockSpec((NB, BLK, BLK), lambda i, m: (0, 0, 0))
    return pl.pallas_call(
        first_kernel,
        out_shape=(
            jax.ShapeDtypeStruct((NB, BLK, BLK), f32),
            jax.ShapeDtypeStruct((NB, BLK, BLK), bf16),
        ),
        grid_spec=pltpu.PrefetchScalarGridSpec(
            num_scalar_prefetch=1,
            grid=(1,),
            in_specs=[
                pl.BlockSpec((1, 512, 512), lambda i, m: (hop, 0, 0)),
                pl.BlockSpec((1, 512, BLK), lambda i, m: (hop, 0, m[0])),
                pl.BlockSpec((512, BLK), lambda i, m: (0, 0)),
            ],
            out_specs=(whole, whole),
        ),
        compiler_params=params(60 * MB),
        name="first_slopes",
    )(member, saved, weights, cotangent)


def upstream_kernel(member, w_ref, s0, s1, s2, s3, u_ref):
    me = member[0]
    parts = []
    for d in range(NX):
        start = pl.multiple_of(lax.rem(me - d + NX, NX) * BLK, BLK)
        parts.append(w_ref[:, pl.ds(start, BLK)])
    lhs = jnp.concatenate(parts, axis=1)
    for r in range(NB):
        rhs = jnp.concatenate([s[r] for s in (s0, s1, s2, s3)], axis=0)
        u_ref[r] = jnp.dot(lhs, rhs, preferred_element_type=f32).astype(bf16)


def upstream_of(member, rows, pieces):
    whole = pl.BlockSpec((NB, BLK, BLK), lambda i, m: (0, 0, 0))
    return pl.pallas_call(
        upstream_kernel,
        out_shape=jax.ShapeDtypeStruct((NB, BLK, BLK), bf16),
        grid_spec=pltpu.PrefetchScalarGridSpec(
            num_scalar_prefetch=1,
            grid=(1,),
            in_specs=[pl.BlockSpec((BLK, 512), lambda i, m: (0, 0))] + [whole] * NX,
            out_specs=whole,
        ),
        compiler_params=params(16 * MB),
        name="upstream",
    )(member, rows, *pieces)


def split(x):
    high = x.astype(bf16)
    return high, (x - high.astype(f32)).astype(bf16)


def joined(x):
    return x[:SUMS].astype(f32) + x[SUMS:].astype(f32)


def weight_kernel(x_ref, s_ref, out_ref, *, scale):
    lhs = jnp.concatenate([s_ref[r] for r in range(NB)], axis=1)
    part = jnp.dot(lhs, x_ref[0], preferred_element_type=f32).T * scale
    high, low = split(part)
    for z in range(NZ):
        for y in range(NY):
            start = (z * NY + y) * SUMS
            out_ref[y, z, :SUMS] = high[start : start + SUMS]
            out_ref[y, z, SUMS:] = low[start : start + SUMS]


def weight_part(saved, slopes, hop, scale):
    shape = (NY, NZ, 2 * SUMS, BLK)
    return pl.pallas_call(
        lambda *refs: weight_kernel(*refs, scale=scale),
        out_shape=jax.ShapeDtypeStruct(shape, bf16),
        grid=(1,),
        in_specs=[
            pl.BlockSpec((1, 512, 512), lambda i: (hop, 0, 0)),
            pl.BlockSpec((NB, BLK, BLK), lambda i: (0, 0, 0)),
        ],
        out_specs=pl.BlockSpec(shape, lambda i: (0, 0, 0, 0)),
        compiler_params=params(60 * MB),
        cost_estimate=cost(1),
        name="weight_part",
    )(saved, slopes)


def spread_kernel(a_ref, b_ref, out_ref):
    total = (a_ref[...] + b_ref[...]).astype(bf16)
    for i in range(NZ * NY):
        out_ref[i] = total


def spread(mine):
    theirs = lax.ppermute(mine, "dp", shift(dc=1))
    shape = (NZ * NY,) + mine.shape
    return pl.pallas_call(
        spread_kernel,
        out_shape=jax.ShapeDtypeStruct(shape, bf16),
        grid=(1,),
        in_specs=[pl.BlockSpec(mine.shape, lambda i: (0, 0))] * 2,
        out_specs=pl.BlockSpec(shape, lambda i: (0, 0, 0)),
        compiler_params=params(60 * MB),
        cost_estimate=cost(0.5),
        name="spread",
    )(mine, theirs)


def collect(copies):
    whole = lax.all_to_all(copies, "dp", 0, 0, axis_index_groups=YZ_GROUPS, tiled=True)
    whole = whole.reshape(NZ * NY, HOPS, SUMS, BLK).transpose(1, 0, 2, 3)
    return whole.reshape(HOPS, 512, BLK).astype(f32)


def message_kernel(table, own_ref, sib_ref, a_own, a_sib, weight_ref, out_a, *rest):
    out_b = rest[:NZ]
    edges, acc, up, stage, stage_b, sems, out_sems, out_b_sems = rest[NZ:]
    copies = [
        pltpu.make_async_copy(a_own, edges.at[pl.ds(0, EDGES // 2)], sems.at[0]),
        pltpu.make_async_copy(a_sib, edges.at[pl.ds(EDGES // 2, EDGES // 2)], sems.at[1]),
    ]
    copies[0].start()
    up[0:NB] = own_ref[...]
    up[NB : 2 * NB] = sib_ref[...]
    up[2 * NB] = jnp.zeros((BLK, BLK), bf16)

    @pl.loop(0, SLOTS // 4)
    def _(i):
        acc[pl.ds(i * 4, 4)] = jnp.zeros((4, BLK, BLK), f32)

    n_items, n_own = table[5 * ITEMS], table[5 * ITEMS + 3]

    def add_items(i):
        sums = []
        for j in range(UNROLL):
            at = i * UNROLL + j
            lhs = jnp.concatenate([up[table[3 * ITEMS + at]], up[table[4 * ITEMS + at]]], axis=1)
            rhs = jnp.concatenate([edges[table[ITEMS + at]], edges[table[2 * ITEMS + at]]], axis=0)
            sums.append(jnp.dot(lhs, rhs, preferred_element_type=f32))
        for j in range(UNROLL):
            slot = table[i * UNROLL + j]
            acc[slot] = acc[slot] + sums[j]

    early = n_own // UNROLL
    copies[0].wait()
    copies[1].start()
    weight_copy = pltpu.make_async_copy(
        weight_ref, out_a.at[:, :, pl.ds(NB * HALF, 2 * SUMS)], sems.at[2]
    )
    weight_copy.start()
    pl.loop(0, early)(add_items)
    copies[1].wait()
    pl.loop(early, (n_items + UNROLL - 1) // UNROLL)(add_items)

    z, y = table[5 * ITEMS + 1], table[5 * ITEMS + 2]
    sends = []
    for dz in range(NZ):
        for dy in range(NY):
            place = dz * 2 + dy // 2
            for b in range(NB):
                total = acc[(dz * NY + dy) * NB + b].astype(bf16)
                stage[dz, dy, b * HALF : (b + 1) * HALF] = total[:HALF]
                stage_b[(place + 1) // 2 % NZ, (place + 1) % 2, dy % 2, b] = total[HALF:]
            send = pltpu.make_async_copy(
                stage.at[dz, dy],
                out_a.at[lax.rem(y + dy, NY), lax.rem(z + dz, NZ), pl.ds(0, NB * HALF)],
                out_sems.at[dz * NY + dy],
            )
            send.start()
            sends.append(send)
        ready = [dz] if dz else []
        if dz == NZ - 1:
            ready.append(0)
        for pair in ready:
            send = pltpu.make_async_copy(stage_b.at[pair], out_b[pair], out_b_sems.at[pair])
            send.start()
            sends.append(send)
    for send in sends:
        send.wait()
    weight_copy.wait()


def messages_of(table, own, sibling, a_own, a_sib, weight):
    hbm = pl.BlockSpec(memory_space=pltpu.HBM)
    return pl.pallas_call(
        message_kernel,
        out_shape=(jax.ShapeDtypeStruct((NY, NZ, ROWS, BLK), bf16),)
        + (jax.ShapeDtypeStruct(PAIR, bf16),) * NZ,
        in_specs=[pl.BlockSpec(memory_space=pltpu.SMEM), vmem(), vmem(), hbm, hbm, hbm],
        out_specs=(hbm,) * (NZ + 1),
        scratch_shapes=[
            pltpu.VMEM((EDGES, BLK, BLK), bf16),
            pltpu.VMEM((SLOTS + 1, BLK, BLK), f32),
            pltpu.VMEM((2 * NB + 1, BLK, BLK), bf16),
            pltpu.VMEM((NZ, NY, NB * HALF, BLK), bf16),
            pltpu.VMEM((NZ,) + PAIR, bf16),
            pltpu.SemaphoreType.DMA((3,)),
            pltpu.SemaphoreType.DMA((NZ * NY,)),
            pltpu.SemaphoreType.DMA((NZ,)),
        ],
        compiler_params=params(60 * MB),
        cost_estimate=cost(6),
        name="messages",
    )(table, own, sibling, a_own, a_sib, weight)


def arrivals(from_z, from_y, r):
    rows = slice(r * HALF, (r + 1) * HALF)
    first = from_z[0, rows].astype(f32)
    for i in range(1, NZ):
        first += from_z[i, rows].astype(f32)
    second = from_y[0][r].astype(f32)
    for part in from_y[1:]:
        second += part[r].astype(f32)
    return jnp.concatenate([first, second], axis=0)


def weight_sums(from_z):
    total = joined(from_z[0, NB * HALF :])
    for i in range(1, NZ):
        total += joined(from_z[i, NB * HALF :])
    return total


def update_kernel(from_z, *refs):
    from_y, (grad_ref, d_ref, new_ref, slope_ref, sums_ref) = refs[:NY], refs[NY:]
    for r in range(NB):
        grad = grad_ref[r] + arrivals(from_z, from_y, r)
        new_ref[r] = grad
        slope_ref[r] = (grad * d_ref[r]).astype(bf16)
    sums_ref[...] = weight_sums(from_z)


def update(from_z, from_y, grad, factor):
    return pl.pallas_call(
        update_kernel,
        out_shape=(
            jax.ShapeDtypeStruct((NB, BLK, BLK), f32),
            jax.ShapeDtypeStruct((NB, BLK, BLK), bf16),
            jax.ShapeDtypeStruct((SUMS, BLK), f32),
        ),
        in_specs=[vmem()] * (NY + 3),
        out_specs=(vmem(),) * 3,
        compiler_params=params(16 * MB),
        cost_estimate=cost(1),
        name="update",
    )(from_z, *from_y, grad, factor)


def last_kernel(from_z, *refs):
    from_y, (grad_ref, out_ref) = refs[:NY], refs[NY:]
    for r in range(NB):
        grad = grad_ref[r] + arrivals(from_z, from_y, r)
        out_ref[r * BLK : (r + 1) * BLK, :] = grad.T.astype(bf16)


def last_update(from_z, from_y, grad):
    return pl.pallas_call(
        last_kernel,
        out_shape=jax.ShapeDtypeStruct((NB * BLK, BLK), bf16),
        in_specs=[vmem()] * (NY + 2),
        out_specs=vmem(),
        compiler_params=params(16 * MB),
        cost_estimate=cost(1),
        name="last_update",
    )(from_z, *from_y, grad)


def last_sums_kernel(from_z, out_ref):
    out_ref[...] = weight_sums(from_z)


def last_sums(from_z):
    return pl.pallas_call(
        last_sums_kernel,
        out_shape=jax.ShapeDtypeStruct((SUMS, BLK), f32),
        grid=(1,),
        in_specs=[pl.BlockSpec((NZ, ROWS, BLK), lambda i: (0, 0, 0))],
        out_specs=pl.BlockSpec((SUMS, BLK), lambda i: (0, 0)),
        compiler_params=params(16 * MB),
        cost_estimate=cost(0.5),
        name="last_sums",
    )(from_z)


def plus(a, b):
    return (a.astype(f32) + b.astype(f32)).astype(bf16)


def fetch(held, sems, *sources):
    copies = [
        pltpu.make_async_copy(q, held.at[i], sems.at[i]) for i, q in enumerate(sources)
    ]
    for copy in copies:
        copy.start()
    for copy in copies:
        copy.wait()


def step_kernel(q_up, q_down, got_up, got_down, up, down, held, sems):
    fetch(held, sems, q_up, q_down)
    up[...] = plus(held[0], got_up[...])
    down[...] = plus(held[1], got_down[...])


def final_kernel(q_up, q_down, got_up, got_down, up, down, keep, held, sems):
    fetch(held, sems, q_up, q_down)
    up[...] = plus(held[0, 1], got_up[1])
    down[...] = plus(held[1, 0], got_down[0])
    keep[0] = held[1, 1].astype(f32) + got_down[1].astype(f32)
    keep[1] = held[0, 0].astype(f32) + got_up[0].astype(f32)


def step(q_up, q_down, got_up, got_down, final):
    hbm = pl.BlockSpec(memory_space=pltpu.HBM)
    sent = jax.ShapeDtypeStruct(PAIR[1:] if final else PAIR, bf16)
    kept = (jax.ShapeDtypeStruct(PAIR, f32),) if final else ()
    return pl.pallas_call(
        final_kernel if final else step_kernel,
        out_shape=(sent, sent) + kept,
        in_specs=[hbm, hbm, vmem(), vmem()],
        out_specs=(vmem(),) * (3 if final else 2),
        scratch_shapes=[pltpu.VMEM((2,) + PAIR, bf16), pltpu.SemaphoreType.DMA((2,))],
        compiler_params=params(4 * MB),
        cost_estimate=cost(0.5),
        name="final_step" if final else "step",
    )(q_up, q_down, got_up, got_down)


def ring_end_kernel(keep, last_up, last_down, *out):
    for i, last in enumerate((last_up, last_down)):
        total = keep[i] + last[...].astype(f32)
        for j in range(NY // 2):
            at = out[i * (NY // 2) + j]
            at[...] = total[j].astype(at.dtype)


def ring_end(keep, last_up, last_down):
    shape = (NB, HALF, BLK)
    return pl.pallas_call(
        ring_end_kernel,
        out_shape=(jax.ShapeDtypeStruct(shape, f32),)
        + (jax.ShapeDtypeStruct(shape, bf16),) * (NY - 1),
        in_specs=[vmem()] * 3,
        out_specs=(vmem(),) * NY,
        compiler_params=params(4 * MB),
        cost_estimate=cost(0.5),
        name="ring_end",
    )(keep, last_up, last_down)


def ring(q, tie):
    ahead, back = shift(dz=1), shift(dz=-1)
    up, down = q[NZ // 2], q[NZ // 2 + 1]
    keep = None
    for k in range(1, NZ // 2):
        got_up = lax.ppermute(up, "dp", ahead)
        got_down = lax.ppermute(down, "dp", back)
        got_up, got_down = tie(k, got_up, got_down)
        args = (q[NZ // 2 - k], q[(NZ // 2 + 1 + k) % NZ], got_up, got_down)
        up, down, *keep = step(*args, k == NZ // 2 - 1)
    last_up = lax.ppermute(up, "dp", ahead)
    last_down = lax.ppermute(down, "dp", back)
    last_up, last_down = tie(NZ // 2, last_up, last_down)
    return ring_end(*keep, last_up, last_down)


def sum_y_kernel(x_ref, out_ref, held, made, sems, out_sems):
    copies, sends = [], []
    for i in range(NZ // 2):
        two = pl.ds(2 * i, 2)
        copies.append(pltpu.make_async_copy(x_ref.at[:, two], held.at[:, two], sems.at[i]))
        sends.append(pltpu.make_async_copy(made.at[two], out_ref.at[two], out_sems.at[i]))
    for copy in copies:
        copy.start()
    for i in range(NZ // 2):
        two = slice(2 * i, 2 * i + 2)
        copies[i].wait()
        total = held[0, two].astype(f32)
        for j in range(1, NY):
            total += held[j, two].astype(f32)
        made[two] = total.astype(bf16)
        for j in (2 * i, 2 * i + 1):
            part = joined(held[0, j, NB * HALF :])
            for k in range(1, NY):
                part += joined(held[k, j, NB * HALF :])
            high, low = split(part)
            made[j, NB * HALF : NB * HALF + SUMS] = high
            made[j, NB * HALF + SUMS :] = low
        sends[i].start()
    for send in sends:
        send.wait()


def sum_y(x):
    hbm = pl.BlockSpec(memory_space=pltpu.HBM)
    return pl.pallas_call(
        sum_y_kernel,
        out_shape=jax.ShapeDtypeStruct(x.shape[1:], bf16),
        in_specs=[hbm],
        out_specs=hbm,
        scratch_shapes=[
            pltpu.VMEM(x.shape, bf16),
            pltpu.VMEM(x.shape[1:], bf16),
            pltpu.SemaphoreType.DMA((NZ // 2,)),
            pltpu.SemaphoreType.DMA((NZ // 2,)),
        ],
        compiler_params=params(60 * MB),
        cost_estimate=cost(SUM_Y_COST),
        name="sum_y",
    )(x)


def exchange(out_a, out_b):
    by_y = lax.all_to_all(out_a, "dp", 0, 0, axis_index_groups=Y_GROUPS, tiled=True)
    made = {"sums": sum_y(by_y)}

    def tie(k, up, down):
        if k == STIE:
            up, down, made["sums"] = lax.optimization_barrier((up, down, made["sums"]))
        return up, down

    own, *others = ring(out_b, tie)
    from_z = lax.all_to_all(made["sums"], "dp", 0, 0, axis_index_groups=Z_GROUPS, tiled=True)
    from_y = [own] + [lax.ppermute(x, "dp", shift(dy=d + 1)) for d, x in enumerate(others)]
    return from_z, from_y


def routing(edge_rows, edge_cols, edge_counts, block_owner, z, y, c):
    live = jnp.arange(EDGES // 2, dtype=jnp.int32) < edge_counts[0]
    code = jnp.where(live, block_owner[edge_cols], -1)
    mine = jnp.stack([code, edge_rows])
    theirs = lax.ppermute(mine, "dp", shift(dc=1))
    code = jnp.concatenate([mine[0], theirs[0]])
    rows = jnp.concatenate([mine[1], theirs[1] + NB])
    dev = code // NB
    used = (code >= 0) & (dev % NC == c)
    y_to, z_to = (dev // NC) % NY, dev // (NC * NY)
    slot = jnp.where(used, ((z_to - z + NZ) % NZ * NY + (y_to - y + NY) % NY) * NB + code % NB, SLOTS)
    ids = jnp.arange(EDGES, dtype=jnp.int32)
    key = jnp.where(used, slot + SLOTS * (ids // (EDGES // 2)), 2 * SLOTS)
    keys = jnp.arange(2 * SLOTS, dtype=jnp.int32)
    same = (key[:, None] == key[None, :]) & (ids[None, :] < ids[:, None])
    rank = jnp.sum(same.astype(jnp.int32), axis=1)
    hit = (key[:, None] == keys[None, :]).astype(jnp.int32)
    pairs = (jnp.sum(hit, axis=0) + 1) // 2
    base = jnp.sum(jnp.where(keys[None, :] < keys[:, None], pairs[None, :], 0), axis=1)
    item = jnp.where(used, jnp.sum(hit * base[None, :], axis=1) + rank // 2, -1)
    side = rank % 2
    place = jnp.arange(ITEMS, dtype=jnp.int32)
    at = [
        (place[:, None] == item[None, :]) & (side[None, :] == s) for s in range(2)
    ]

    def pick(mask, values, default):
        return jnp.sum(jnp.where(mask, values[None, :] - default, 0), axis=1) + default

    return jnp.concatenate(
        [
            pick(at[0], slot, SLOTS),
            pick(at[0], ids, 0),
            pick(at[1], ids, 0),
            pick(at[0], rows, 2 * NB),
            pick(at[1], rows, 2 * NB),
            jnp.stack([jnp.sum(pairs), z, y, jnp.sum(pairs[:SLOTS])]),
        ]
    ).astype(jnp.int32)


def on_device(
    cotangent, saved_inputs, weights, edge_values, edge_rows, edge_cols, edge_counts, block_owner
):
    scale = 1.0 / math.sqrt(saved_inputs.shape[1] * lax.axis_size("dp"))
    dp = lax.axis_index("dp")
    z, y, c = dp // (NY * NC), dp // NC % NY, dp % NC
    group = lax.axis_index("group")
    member = jnp.full((1,), group, jnp.int32)

    edges_sib = lax.ppermute(edge_values, "dp", shift(dc=1))
    table = routing(edge_rows, edge_cols, edge_counts, block_owner, z, y, c)
    grad, slopes = first_slopes(member, saved_inputs, weights, cotangent)
    factor = [factors(member, saved_inputs, weights, h) for h in range(HOPS - 1)]

    my_rows = [
        lax.dynamic_slice(weights, (h, group * BLK, 0), (1, BLK, 512))[0] for h in range(HOPS)
    ]
    sums = [None] * HOPS
    for hop in reversed(range(HOPS)):
        pieces = [slopes] + [
            lax.ppermute(slopes, "group", [(i, (i + d) % NX) for i in range(NX)])
            for d in range(1, NX)
        ]
        weight = weight_part(saved_inputs, slopes, hop, scale)
        own = upstream_of(member, my_rows[hop], pieces)
        sibling = lax.ppermute(own, "dp", shift(dc=1))
        out_a, *out_b = messages_of(table, own, sibling, edge_values, edges_sib, weight)
        from_z, from_y = exchange(out_a, out_b)
        if hop:
            grad, slopes, sums[hop] = update(from_z, from_y, grad, factor[hop - 1])
    result = last_update(from_z, from_y, grad)
    sums[0] = last_sums(from_z)
    return result, collect(spread(jnp.concatenate(sums, axis=0)))


def solution(mesh):
    in_specs = (
        P("dp", "group"),
        P(None, "dp", None),
        P(),
        P("dp", None, None),
        P("dp"),
        P("dp"),
        P("dp"),
        P(),
    )
    out_specs = (P("dp", "group"), P(None, None, "group"))
    return jax.shard_map(
        on_device, mesh=mesh, in_specs=in_specs, out_specs=out_specs, check_vma=False
    )
```

profile of v0, /device:TPU:1, one launch (start us, length us, event | category | flops | bytes accessed | tf_op | source)
XLA Modules:
  0.0 299.5 jit_solution(9131681207990086990)
XLA Ops:
  0.7 3.3 %collective-permute-start.5 = (bf16[128,128,128]{2,1,0:T(8,128)(2,1)}, bf16[128,128,128]{2,1,0:T(8,128)(2,1)}, u32[]{:S(2)}, u32[]{:S(2)}) collective-permute-start(bf16[128,128,128]{2,1,0:T(8,128)(2,1)} %a_own.5), channel_id=1, source_target_pairs={{0,4},{4,0},{8,12},{12,8},{16,20},{20,16},{24,28},{28,24},{32,36},... | collective-permute-start | bytes 12582920 | tf_op jit(solution)/shard_map/ppermute | solution.py:581
  4.0 2.2 first_slopes.1
  6.2 1.9 collective-permute-start.2
  9.9 1.3 gather_fusion
  13.3 2.1 weight_part.3.weight_ref
  18.2 2.0 concatenate.102.table
  20.9 12.6 %messages.3 = (bf16[4,8,288,128]{3,2,1,0:T(8,128)(2,1)}, bf16[2,2,4,64,128]{4,3,2,1,0:T(8,128)(2,1)}, bf16[2,2,4,64,128]{4,3,2,1,0:T(8,128)(2,1)}, bf16[2,2,4,64...) custom-call(s32[1324]{0:T(1024)} %concatenate.102.table, ...), custom_call_target="tpu_custom_call" | custom-call | bytes 19800000 | tf_op jit(solution)/shard_map/messages/pallas_call | solution.py:287
  33.6 4.7 %all-to-all-start = ((bf16[4,8,288,128]{3,2,1,0:T(8,128)(2,1)}), bf16[4,8,288,128]{3,2,1,0:T(8,128)(2,1)}, u32[]{:S(2)}, u32[]{:S(2)}) async-start(bf16[4,8,288,128]{3,2,1,0:T(8,128)(2,1)} %get-tuple-element.94), calls=%async_computation | async-start | bytes 4718592 | tf_op jit(solution)/shard_map/all_to_all | solution.py:517
  38.3 1.7 collective-permute-start.6
  40.0 4.0 %collective-permute-start.7 = (bf16[2,2,4,64,128]{4,3,2,1,0:T(8,128)(2,1)S(1)}, bf16[2,2,4,64,128]{4,3,2,1,0:T(8,128)(2,1)S(1)}, u32[]{:S(2)}, u32[]{:S(2)}) collective-permute-start(bf16[2,2,4,64,128]{4,3,2,1,0:T(8,128)(2,1)S(1)} %copy-done.35), channel_id=1, source_target_pairs={{0,224},{4,228},{8,232},{12,236},{16,240},{20,244},{24,248},{28,25... | collective-permute-start | bytes 786440 | tf_op jit(solution)/shard_map/ppermute | solution.py:460
  44.0 6.3 %collective-permute-done.6.got_up = bf16[2,2,4,64,128]{4,3,2,1,0:T(8,128)(2,1)S(1)} collective-permute-done((bf16[2,2,4,64,128]{4,3,2,1,0:T(8,128)(2,1)S(1)}, bf16[2,2,4,64,128]{4,3,2,1,0:T(8,128)(2,1)S(1)}, u32[]{:S(2)}, u32[]{:S(2)}) %collective-permute-start.6) | collective-permute-done | bytes 262176 | tf_op jit(solution)/shard_map/ppermute | solution.py:459
  50.7 2.7 collective-permute-start.9
  53.3 5.6 %collective-permute-done.8.got_up = bf16[2,2,4,64,128]{4,3,2,1,0:T(8,128)(2,1)S(1)} collective-permute-done((bf16[2,2,4,64,128]{4,3,2,1,0:T(8,128)(2,1)S(1)}, bf16[2,2,4,64,128]{4,3,2,1,0:T(8,128)(2,1)S(1)}, u32[]{:S(2)}, u32[]{:S(2)}) %collective-permute-start.8) | collective-permute-done | bytes 262176 | tf_op jit(solution)/shard_map/ppermute | solution.py:459
  60.1 2.0 collective-permute-start.11
  62.1 4.5 %collective-permute-done.10.got_up = bf16[2,2,4,64,128]{4,3,2,1,0:T(8,128)(2,1)S(1)} collective-permute-done((bf16[2,2,4,64,128]{4,3,2,1,0:T(8,128)(2,1)S(1)}, bf16[2,2,4,64,128]{4,3,2,1,0:T(8,128)(2,1)S(1)}, u32[]{:S(2)}, u32[]{:S(2)}) %collective-permute-start.10) | collective-permute-done | bytes 262176 | tf_op jit(solution)/shard_map/ppermute | solution.py:459
  67.8 1.9 collective-permute-start.13
  69.7 2.4 sum_y.3
  72.1 5.6 %all-to-all-start.1 = ((bf16[8,288,128]{2,1,0:T(8,128)(2,1)}), bf16[8,288,128]{2,1,0:T(8,128)(2,1)S(1)}, u32[]{:S(2)}, u32[]{:S(2)}) async-start(bf16[8,288,128]{2,1,0:T(8,128)(2,1)} %sum_y.3), calls=%async_computation.1 | async-start | bytes 1179648 | tf_op jit(solution)/shard_map/all_to_all | solution.py:526
  78.2 2.0 collective-permute-start.15
  80.7 2.1 factors.2.refs_5_
  83.5 10.4 %all-to-all-done.1.from_z = bf16[8,288,128]{2,1,0:T(8,128)(2,1)S(1)} async-done(((bf16[8,288,128]{2,1,0:T(8,128)(2,1)}), bf16[8,288,128]{2,1,0:T(8,128)(2,1)S(1)}, u32[]{:S(2)}, u32[]{:S(2)}) %all-to-all-start.1) | async-done | bytes 589856 | tf_op jit(solution)/shard_map/all_to_all | solution.py:526
  96.2 1.7 collective-permute-start.19
  97.9 3.6 %collective-permute-done.17.s1 = bf16[4,128,128]{2,1,0:T(8,128)(2,1)S(1)} collective-permute-done((bf16[4,128,128]{2,1,0:T(8,128)(2,1)S(1)}, bf16[4,128,128]{2,1,0:T(8,128)(2,1)S(1)}, u32[]{:S(2)}, u32[]{:S(2)}) %collective-permute-start.17) | collective-permute-done | bytes 131104 | tf_op jit(solution)/shard_map/ppermute | solution.py:592
  102.4 5.2 %collective-permute-start.20 = (bf16[4,128,128]{2,1,0:T(8,128)(2,1)S(1)}, bf16[4,128,128]{2,1,0:T(8,128)(2,1)S(1)}, u32[]{:S(2)}, u32[]{:S(2)}) collective-permute-start(bf16[4,128,128]{2,1,0:T(8,128)(2,1)S(1)} %upstream.4.own_ref), channel_id=1, source_target_pairs={{0,4},{4,0},{8,12},{12,8},{16,20},{20,16},{24,28},{28,24},{32,36},... | collective-permute-start | bytes 393224 | tf_op jit(solution)/shard_map/ppermute | solution.py:597
  107.6 2.1 weight_part.4.weight_ref
  110.4 12.6 %messages.4 = (bf16[4,8,288,128]{3,2,1,0:T(8,128)(2,1)}, bf16[2,2,4,64,128]{4,3,2,1,0:T(8,128)(2,1)}, bf16[2,2,4,64,128]{4,3,2,1,0:T(8,128)(2,1)}, bf16[2,2,4,64...) custom-call(s32[1324]{0:T(1024)} %concatenate.102.table, ...), custom_call_target="tpu_custom_call" | custom-call | bytes 19800000 | tf_op jit(solution)/shard_map/messages/pallas_call | solution.py:287
  123.1 4.7 %all-to-all-start.2 = ((bf16[4,8,288,128]{3,2,1,0:T(8,128)(2,1)}), bf16[4,8,288,128]{3,2,1,0:T(8,128)(2,1)}, u32[]{:S(2)}, u32[]{:S(2)}) async-start(bf16[4,8,288,128]{3,2,1,0:T(8,128)(2,1)} %get-tuple-element.119), calls=%async_computation.2 | async-start | bytes 4718592 | tf_op jit(solution)/shard_map/all_to_all | solution.py:517
  128.1 2.4 collective-permute-start.22
  130.5 6.6 %collective-permute-done.21.got_up = bf16[2,2,4,64,128]{4,3,2,1,0:T(8,128)(2,1)S(1)} collective-permute-done((bf16[2,2,4,64,128]{4,3,2,1,0:T(8,128)(2,1)S(1)}, bf16[2,2,4,64,128]{4,3,2,1,0:T(8,128)(2,1)S(1)}, u32[]{:S(2)}, u32[]{:S(2)}) %collective-permute-start.21) | collective-permute-done | bytes 262176 | tf_op jit(solution)/shard_map/ppermute | solution.py:459
  137.4 11.4 %collective-permute-start.24 = (bf16[2,2,4,64,128]{4,3,2,1,0:T(8,128)(2,1)S(1)}, bf16[2,2,4,64,128]{4,3,2,1,0:T(8,128)(2,1)S(1)}, u32[]{:S(2)}, u32[]{:S(2)}) collective-permute-start(bf16[2,2,4,64,128]{4,3,2,1,0:T(8,128)(2,1)S(1)} %get-tuple-element.114), channel_id=1, source_target_pairs={{0,224},{4,228},{8,232},{12,236},{16,240},{20,244},{24,248},{28,25... | collective-permute-start | bytes 786440 | tf_op jit(solution)/shard_map/ppermute | solution.py:460
  148.8 4.9 %collective-permute-done.24.got_down = bf16[2,2,4,64,128]{4,3,2,1,0:T(8,128)(2,1)S(1)} collective-permute-done((bf16[2,2,4,64,128]{4,3,2,1,0:T(8,128)(2,1)S(1)}, bf16[2,2,4,64,128]{4,3,2,1,0:T(8,128)(2,1)S(1)}, u32[]{:S(2)}, u32[]{:S(2)}) %collective-permute-start.24) | collective-permute-done | bytes 262176 | tf_op jit(solution)/shard_map/ppermute | solution.py:460
  154.0 3.2 %collective-permute-start.26 = (bf16[2,2,4,64,128]{4,3,2,1,0:T(8,128)(2,1)S(1)}, bf16[2,2,4,64,128]{4,3,2,1,0:T(8,128)(2,1)S(1)}, u32[]{:S(2)}, u32[]{:S(2)}) collective-permute-start(bf16[2,2,4,64,128]{4,3,2,1,0:T(8,128)(2,1)S(1)} %get-tuple-element.116), channel_id=1, source_target_pairs={{0,224},{4,228},{8,232},{12,236},{16,240},{20,244},{24,248},{28,25... | collective-permute-start | bytes 786440 | tf_op jit(solution)/shard_map/ppermute | solution.py:460
  157.2 4.6 %collective-permute-done.25.got_up = bf16[2,2,4,64,128]{4,3,2,1,0:T(8,128)(2,1)S(1)} collective-permute-done((bf16[2,2,4,64,128]{4,3,2,1,0:T(8,128)(2,1)S(1)}, bf16[2,2,4,64,128]{4,3,2,1,0:T(8,128)(2,1)S(1)}, u32[]{:S(2)}, u32[]{:S(2)}) %collective-permute-start.25) | collective-permute-done | bytes 262176 | tf_op jit(solution)/shard_map/ppermute | solution.py:459
  162.1 2.7 collective-permute-start.28
  164.7 2.4 sum_y.4
  167.2 3.9 %all-to-all-start.3 = ((bf16[8,288,128]{2,1,0:T(8,128)(2,1)}), bf16[8,288,128]{2,1,0:T(8,128)(2,1)S(1)}, u32[]{:S(2)}, u32[]{:S(2)}) async-start(bf16[8,288,128]{2,1,0:T(8,128)(2,1)} %sum_y.4), calls=%async_computation.3 | async-start | bytes 1179648 | tf_op jit(solution)/shard_map/all_to_all | solution.py:526
  171.2 2.7 collective-permute-start.30
  174.8 2.1 factors.3.refs_5_
  177.1 8.7 %all-to-all-done.3.from_z = bf16[8,288,128]{2,1,0:T(8,128)(2,1)S(1)} async-done(((bf16[8,288,128]{2,1,0:T(8,128)(2,1)}), bf16[8,288,128]{2,1,0:T(8,128)(2,1)S(1)}, u32[]{:S(2)}, u32[]{:S(2)}) %all-to-all-start.3) | async-done | bytes 589856 | tf_op jit(solution)/shard_map/all_to_all | solution.py:526
  187.6 2.9 collective-permute-start.33
  190.5 1.4 collective-permute-done.32.s1
  192.0 2.3 collective-permute-done.33.s2
  194.7 6.9 %collective-permute-start.35 = (bf16[4,128,128]{2,1,0:T(8,128)(2,1)S(1)}, bf16[4,128,128]{2,1,0:T(8,128)(2,1)S(1)}, u32[]{:S(2)}, u32[]{:S(2)}) collective-permute-start(bf16[4,128,128]{2,1,0:T(8,128)(2,1)S(1)} %upstream.5.own_ref), channel_id=1, source_target_pairs={{0,4},{4,0},{8,12},{12,8},{16,20},{20,16},{24,28},{28,24},{32,36},... | collective-permute-start | bytes 393224 | tf_op jit(solution)/shard_map/ppermute | solution.py:597
  201.6 2.1 weight_part.5.weight_ref
  204.3 12.6 %messages.5 = (bf16[4,8,288,128]{3,2,1,0:T(8,128)(2,1)}, bf16[2,2,4,64,128]{4,3,2,1,0:T(8,128)(2,1)}, bf16[2,2,4,64,128]{4,3,2,1,0:T(8,128)(2,1)}, bf16[2,2,4,64...) custom-call(s32[1324]{0:T(1024)} %concatenate.102.table, ...), custom_call_target="tpu_custom_call" | custom-call | bytes 19800000 | tf_op jit(solution)/shard_map/messages/pallas_call | solution.py:287
  217.0 4.6 %all-to-all-start.4 = ((bf16[4,8,288,128]{3,2,1,0:T(8,128)(2,1)}), bf16[4,8,288,128]{3,2,1,0:T(8,128)(2,1)}, u32[]{:S(2)}, u32[]{:S(2)}) async-start(bf16[4,8,288,128]{3,2,1,0:T(8,128)(2,1)} %get-tuple-element.144), calls=%async_computation.4 | async-start | bytes 4718592 | tf_op jit(solution)/shard_map/all_to_all | solution.py:517
  222.0 2.6 collective-permute-start.37
  224.6 6.4 %collective-permute-done.36.got_up = bf16[2,2,4,64,128]{4,3,2,1,0:T(8,128)(2,1)S(1)} collective-permute-done((bf16[2,2,4,64,128]{4,3,2,1,0:T(8,128)(2,1)S(1)}, bf16[2,2,4,64,128]{4,3,2,1,0:T(8,128)(2,1)S(1)}, u32[]{:S(2)}, u32[]{:S(2)}) %collective-permute-start.36) | collective-permute-done | bytes 262176 | tf_op jit(solution)/shard_map/ppermute | solution.py:459
  231.3 2.7 collective-permute-start.39
  234.0 5.8 %collective-permute-done.38.got_up = bf16[2,2,4,64,128]{4,3,2,1,0:T(8,128)(2,1)S(1)} collective-permute-done((bf16[2,2,4,64,128]{4,3,2,1,0:T(8,128)(2,1)S(1)}, bf16[2,2,4,64,128]{4,3,2,1,0:T(8,128)(2,1)S(1)}, u32[]{:S(2)}, u32[]{:S(2)}) %collective-permute-start.38) | collective-permute-done | bytes 262176 | tf_op jit(solution)/shard_map/ppermute | solution.py:459
  240.1 2.7 collective-permute-start.41
  242.7 5.0 %collective-permute-done.40.got_up = bf16[2,2,4,64,128]{4,3,2,1,0:T(8,128)(2,1)S(1)} collective-permute-done((bf16[2,2,4,64,128]{4,3,2,1,0:T(8,128)(2,1)S(1)}, bf16[2,2,4,64,128]{4,3,2,1,0:T(8,128)(2,1)S(1)}, u32[]{:S(2)}, u32[]{:S(2)}) %collective-permute-start.40) | collective-permute-done | bytes 262176 | tf_op jit(solution)/shard_map/ppermute | solution.py:459
  248.0 2.7 collective-permute-start.43
  251.0 2.4 sum_y.5
  253.4 17.8 %all_to_all.35.from_z = bf16[8,288,128]{2,1,0:T(8,128)(2,1)S(1)} all-to-all(bf16[8,288,128]{2,1,0:T(8,128)(2,1)} %sum_y.5), channel_id=1, replica_groups={{0,32,64,96,128,160,192,224},{4,36,68,100,132,164,196,228},{8,40,72,104..., dimensions={0} | all-to-all | bytes 1179648 | tf_op jit(solution)/shard_map/all_to_all | solution.py:526
  271.3 5.7 %collective-permute-start.47 = (f32[48,128]{1,0:T(8,128)S(1)}, f32[48,128]{1,0:T(8,128)S(1)}, u32[]{:S(2)}, u32[]{:S(2)}) collective-permute-start(f32[48,128]{1,0:T(8,128)S(1)} %pad_maximum_fusion.a_ref), channel_id=1, source_target_pairs={{0,4},{4,0},{8,12},{12,8},{16,20},{20,16},{24,28},{28,24},{32,36},... | collective-permute-start | bytes 73736 | tf_op jit(solution)/shard_map/ppermute | solution.py:197
  278.4 1.5 spread.1
  280.0 3.9 %all-to-all-start.6 = ((bf16[32,48,128]{2,1,0:T(8,128)(2,1)}), bf16[32,48,128]{2,1,0:T(8,128)(2,1)S(1)}, u32[]{:S(2)}, u32[]{:S(2)}) async-start(bf16[32,48,128]{2,1,0:T(8,128)(2,1)} %spread.1), calls=%async_computation.6 | async-start | bytes 786432 | tf_op jit(solution)/shard_map/all_to_all | solution.py:212
  283.9 1.2 collective-permute-start.44
  285.1 2.4 collective-permute-start.45
  287.5 1.2 collective-permute-start.46
  289.2 2.7 collective-permute-done.45.refs_2_
  291.9 1.4 collective-permute-done.46.refs_3_
  294.1 4.1 %all-to-all-done.6 = bf16[32,48,128]{2,1,0:T(8,128)(2,1)S(1)} async-done(((bf16[32,48,128]{2,1,0:T(8,128)(2,1)}), bf16[32,48,128]{2,1,0:T(8,128)(2,1)S(1)}, u32[]{:S(2)}, u32[]{:S(2)}) %all-to-all-start.6) | async-done | bytes 393248 | tf_op jit(solution)/shard_map/all_to_all | solution.py:212
  (185 shorter events, 25.5 us)
Async XLA Ops:
  0.7 19.6 %collective-permute-start.5 = (bf16[128,128,128]{2,1,0:T(8,128)(2,1)}, bf16[128,128,128]{2,1,0:T(8,128)(2,1)}, u32[]{:S(2)}, u32[]{:S(2)}) collective-permute-start(bf16[128,128,128]{2,1,0:T(8,128)(2,1)} %a_own.5), channel_id=1, source_target_pairs={{0,4},{4,0},{8,12},{12,8},{16,20},{20,16},{24,28},{28,24},{32,36},... | collective-permute-start | bytes 12582920 | tf_op jit(solution)/shard_map/ppermute | solution.py:581
  6.2 10.9 %collective-permute-start.1 = (bf16[4,128,128]{2,1,0:T(8,128)(2,1)}, bf16[4,128,128]{2,1,0:T(8,128)(2,1)S(1)}, u32[]{:S(2)}, u32[]{:S(2)}) collective-permute-start(bf16[4,128,128]{2,1,0:T(8,128)(2,1)} %get-tuple-element.79.s0.refs_1_), channel_id=1, source_target_pairs={{0,1},{1,2},{2,3},{3,0},{4,5},{5,6},{6,7},{7,4},{8,9},{9,10},{10,1... | collective-permute-start | bytes 393224 | tf_op jit(solution)/shard_map/ppermute | solution.py:592
  6.2 10.9 %collective-permute-start.2 = (bf16[4,128,128]{2,1,0:T(8,128)(2,1)}, bf16[4,128,128]{2,1,0:T(8,128)(2,1)S(1)}, u32[]{:S(2)}, u32[]{:S(2)}) collective-permute-start(bf16[4,128,128]{2,1,0:T(8,128)(2,1)} %get-tuple-element.79.s0.refs_1_), channel_id=1, source_target_pairs={{0,2},{1,3},{2,0},{3,1},{4,6},{5,7},{6,4},{7,5},{8,10},{9,11},{10,... | collective-permute-start | bytes 393224 | tf_op jit(solution)/shard_map/ppermute | solution.py:592
  8.1 9.0 %collective-permute-start.3 = (bf16[4,128,128]{2,1,0:T(8,128)(2,1)}, bf16[4,128,128]{2,1,0:T(8,128)(2,1)S(1)}, u32[]{:S(2)}, u32[]{:S(2)}) collective-permute-start(bf16[4,128,128]{2,1,0:T(8,128)(2,1)} %get-tuple-element.79.s0.refs_1_), channel_id=1, source_target_pairs={{0,3},{1,0},{2,1},{3,2},{4,7},{5,4},{6,5},{7,6},{8,11},{9,8},{10,9... | collective-permute-start | bytes 393224 | tf_op jit(solution)/shard_map/ppermute | solution.py:592
  11.2 4.1 %collective-permute-start = (s32[2,128]{1,0:T(2,128)S(1)}, s32[2,128]{1,0:T(2,128)S(1)}, u32[]{:S(2)}, u32[]{:S(2)}) collective-permute-start(s32[2,128]{1,0:T(2,128)S(1)} %pad_add_fusion), channel_id=1, source_target_pairs={{0,4},{4,0},{8,12},{12,8},{16,20},{20,16},{24,28},{28,24},{32,36},... | collective-permute-start | bytes 3080 | tf_op jit(solution)/shard_map/ppermute | solution.py:535
  17.4 2.8 collective-permute-start.4
  33.5 25.4 %copy-start.18 = (bf16[2,2,4,64,128]{4,3,2,1,0:T(8,128)(2,1)S(1)}, bf16[2,2,4,64,128]{4,3,2,1,0:T(8,128)(2,1)}, u32[]{:S(2)}) copy-start(bf16[2,2,4,64,128]{4,3,2,1,0:T(8,128)(2,1)} %get-tuple-element.82.q_up) | copy-start | bytes 786436
  33.5 25.4 %copy-start.19 = (bf16[2,2,4,64,128]{4,3,2,1,0:T(8,128)(2,1)S(1)}, bf16[2,2,4,64,128]{4,3,2,1,0:T(8,128)(2,1)}, u32[]{:S(2)}) copy-start(bf16[2,2,4,64,128]{4,3,2,1,0:T(8,128)(2,1)} %get-tuple-element.83.q_down) | copy-start | bytes 786436
  33.5 33.1 %copy-start.12 = (bf16[2,2,4,64,128]{4,3,2,1,0:T(8,128)(2,1)S(1)}, bf16[2,2,4,64,128]{4,3,2,1,0:T(8,128)(2,1)}, u32[]{:S(2)}) copy-start(bf16[2,2,4,64,128]{4,3,2,1,0:T(8,128)(2,1)} %get-tuple-element.81.q_down) | copy-start | bytes 786436
  33.6 33.1 %copy-start.13 = (bf16[2,2,4,64,128]{4,3,2,1,0:T(8,128)(2,1)S(1)}, bf16[2,2,4,64,128]{4,3,2,1,0:T(8,128)(2,1)}, u32[]{:S(2)}) copy-start(bf16[2,2,4,64,128]{4,3,2,1,0:T(8,128)(2,1)} %get-tuple-element.80.q_up) | copy-start | bytes 786436
  33.6 36.1 %all-to-all-start = ((bf16[4,8,288,128]{3,2,1,0:T(8,128)(2,1)}), bf16[4,8,288,128]{3,2,1,0:T(8,128)(2,1)}, u32[]{:S(2)}, u32[]{:S(2)}) async-start(bf16[4,8,288,128]{3,2,1,0:T(8,128)(2,1)} %get-tuple-element.94), calls=%async_computation | async-start | bytes 4718592 | tf_op jit(solution)/shard_map/all_to_all | solution.py:517
  38.3 12.0 %collective-permute-start.6 = (bf16[2,2,4,64,128]{4,3,2,1,0:T(8,128)(2,1)S(1)}, bf16[2,2,4,64,128]{4,3,2,1,0:T(8,128)(2,1)S(1)}, u32[]{:S(2)}, u32[]{:S(2)}) collective-permute-start(bf16[2,2,4,64,128]{4,3,2,1,0:T(8,128)(2,1)S(1)} %copy-done.38), channel_id=1, source_target_pairs={{0,32},{4,36},{8,40},{12,44},{16,48},{20,52},{24,56},{28,60},{32,6... | collective-permute-start | bytes 786440 | tf_op jit(solution)/shard_map/ppermute | solution.py:459
  40.0 10.3 %collective-permute-start.7 = (bf16[2,2,4,64,128]{4,3,2,1,0:T(8,128)(2,1)S(1)}, bf16[2,2,4,64,128]{4,3,2,1,0:T(8,128)(2,1)S(1)}, u32[]{:S(2)}, u32[]{:S(2)}) collective-permute-start(bf16[2,2,4,64,128]{4,3,2,1,0:T(8,128)(2,1)S(1)} %copy-done.35), channel_id=1, source_target_pairs={{0,224},{4,228},{8,232},{12,236},{16,240},{20,244},{24,248},{28,25... | collective-permute-start | bytes 786440 | tf_op jit(solution)/shard_map/ppermute | solution.py:460
  50.6 8.3 %collective-permute-start.8 = (bf16[2,2,4,64,128]{4,3,2,1,0:T(8,128)(2,1)S(1)}, bf16[2,2,4,64,128]{4,3,2,1,0:T(8,128)(2,1)S(1)}, u32[]{:S(2)}, u32[]{:S(2)}) collective-permute-start(bf16[2,2,4,64,128]{4,3,2,1,0:T(8,128)(2,1)S(1)} %get-tuple-element.88), channel_id=1, source_target_pairs={{0,32},{4,36},{8,40},{12,44},{16,48},{20,52},{24,56},{28,60},{32,6... | collective-permute-start | bytes 786440 | tf_op jit(solution)/shard_map/ppermute | solution.py:459
  50.7 8.2 %collective-permute-start.9 = (bf16[2,2,4,64,128]{4,3,2,1,0:T(8,128)(2,1)S(1)}, bf16[2,2,4,64,128]{4,3,2,1,0:T(8,128)(2,1)S(1)}, u32[]{:S(2)}, u32[]{:S(2)}) collective-permute-start(bf16[2,2,4,64,128]{4,3,2,1,0:T(8,128)(2,1)S(1)} %get-tuple-element.89), channel_id=1, source_target_pairs={{0,224},{4,228},{8,232},{12,236},{16,240},{20,244},{24,248},{28,25... | collective-permute-start | bytes 786440 | tf_op jit(solution)/shard_map/ppermute | solution.py:460
  59.1 7.5 %collective-permute-start.10 = (bf16[2,2,4,64,128]{4,3,2,1,0:T(8,128)(2,1)S(1)}, bf16[2,2,4,64,128]{4,3,2,1,0:T(8,128)(2,1)S(1)}, u32[]{:S(2)}, u32[]{:S(2)}) collective-permute-start(bf16[2,2,4,64,128]{4,3,2,1,0:T(8,128)(2,1)S(1)} %get-tuple-element.90), channel_id=1, source_target_pairs={{0,32},{4,36},{8,40},{12,44},{16,48},{20,52},{24,56},{28,60},{32,6... | collective-permute-start | bytes 786440 | tf_op jit(solution)/shard_map/ppermute | solution.py:459
  60.1 6.6 %collective-permute-start.11 = (bf16[2,2,4,64,128]{4,3,2,1,0:T(8,128)(2,1)S(1)}, bf16[2,2,4,64,128]{4,3,2,1,0:T(8,128)(2,1)S(1)}, u32[]{:S(2)}, u32[]{:S(2)}) collective-permute-start(bf16[2,2,4,64,128]{4,3,2,1,0:T(8,128)(2,1)S(1)} %get-tuple-element.91), channel_id=1, source_target_pairs={{0,224},{4,228},{8,232},{12,236},{16,240},{20,244},{24,248},{28,25... | collective-permute-start | bytes 786440 | tf_op jit(solution)/shard_map/ppermute | solution.py:460
  66.9 5.2 %collective-permute-start.12 = (bf16[2,4,64,128]{3,2,1,0:T(8,128)(2,1)S(1)}, bf16[2,4,64,128]{3,2,1,0:T(8,128)(2,1)S(1)}, u32[]{:S(2)}, u32[]{:S(2)}) collective-permute-start(bf16[2,4,64,128]{3,2,1,0:T(8,128)(2,1)S(1)} %get-tuple-element.92), channel_id=1, source_target_pairs={{0,32},{4,36},{8,40},{12,44},{16,48},{20,52},{24,56},{28,60},{32,6... | collective-permute-start | bytes 393224 | tf_op jit(solution)/shard_map/ppermute | solution.py:464
  67.8 4.3 %collective-permute-start.13 = (bf16[2,4,64,128]{3,2,1,0:T(8,128)(2,1)S(1)}, bf16[2,4,64,128]{3,2,1,0:T(8,128)(2,1)S(1)}, u32[]{:S(2)}, u32[]{:S(2)}) collective-permute-start(bf16[2,4,64,128]{3,2,1,0:T(8,128)(2,1)S(1)} %get-tuple-element.93), channel_id=1, source_target_pairs={{0,224},{4,228},{8,232},{12,236},{16,240},{20,244},{24,248},{28,25... | collective-permute-start | bytes 393224 | tf_op jit(solution)/shard_map/ppermute | solution.py:465
  72.1 21.8 %all-to-all-start.1 = ((bf16[8,288,128]{2,1,0:T(8,128)(2,1)}), bf16[8,288,128]{2,1,0:T(8,128)(2,1)S(1)}, u32[]{:S(2)}, u32[]{:S(2)}) async-start(bf16[8,288,128]{2,1,0:T(8,128)(2,1)} %sum_y.3), calls=%async_computation.1 | async-start | bytes 1179648 | tf_op jit(solution)/shard_map/all_to_all | solution.py:526
  77.8 5.0 %collective-permute-start.14 = (bf16[4,64,128]{2,1,0:T(8,128)(2,1)S(1)}, bf16[4,64,128]{2,1,0:T(8,128)(2,1)S(1)}, u32[]{:S(2)}, u32[]{:S(2)}) collective-permute-start(bf16[4,64,128]{2,1,0:T(8,128)(2,1)S(1)} %get-tuple-element.100), channel_id=1, source_target_pairs={{0,8},{4,12},{8,16},{12,20},{16,24},{20,28},{24,0},{28,4},{32,40},... | collective-permute-start | bytes 196616 | tf_op jit(solution)/shard_map/ppermute | solution.py:527
  78.2 4.7 %collective-permute-start.15 = (bf16[4,64,128]{2,1,0:T(8,128)(2,1)S(1)}, bf16[4,64,128]{2,1,0:T(8,128)(2,1)S(1)}, u32[]{:S(2)}, u32[]{:S(2)}) collective-permute-start(bf16[4,64,128]{2,1,0:T(8,128)(2,1)S(1)} %get-tuple-element.101), channel_id=1, source_target_pairs={{0,16},{4,20},{8,24},{12,28},{16,0},{20,4},{24,8},{28,12},{32,48},... | collective-permute-start | bytes 196616 | tf_op jit(solution)/shard_map/ppermute | solution.py:527
  80.2 3.3 %collective-permute-start.16 = (bf16[4,64,128]{2,1,0:T(8,128)(2,1)S(1)}, bf16[4,64,128]{2,1,0:T(8,128)(2,1)S(1)}, u32[]{:S(2)}, u32[]{:S(2)}) collective-permute-start(bf16[4,64,128]{2,1,0:T(8,128)(2,1)S(1)} %get-tuple-element.102), channel_id=1, source_target_pairs={{0,24},{4,28},{8,0},{12,4},{16,8},{20,12},{24,16},{28,20},{32,56},... | collective-permute-start | bytes 196616 | tf_op jit(solution)/shard_map/ppermute | solution.py:527
  95.0 6.5 %collective-permute-start.17 = (bf16[4,128,128]{2,1,0:T(8,128)(2,1)S(1)}, bf16[4,128,128]{2,1,0:T(8,128)(2,1)S(1)}, u32[]{:S(2)}, u32[]{:S(2)}) collective-permute-start(bf16[4,128,128]{2,1,0:T(8,128)(2,1)S(1)} %get-tuple-element.104.s0.refs_1_), channel_id=1, source_target_pairs={{0,1},{1,2},{2,3},{3,0},{4,5},{5,6},{6,7},{7,4},{8,9},{9,10},{10,1... | collective-permute-start | bytes 393224 | tf_op jit(solution)/shard_map/ppermute | solution.py:592
  95.4 6.1 %collective-permute-start.18 = (bf16[4,128,128]{2,1,0:T(8,128)(2,1)S(1)}, bf16[4,128,128]{2,1,0:T(8,128)(2,1)S(1)}, u32[]{:S(2)}, u32[]{:S(2)}) collective-permute-start(bf16[4,128,128]{2,1,0:T(8,128)(2,1)S(1)} %get-tuple-element.104.s0.refs_1_), channel_id=1, source_target_pairs={{0,2},{1,3},{2,0},{3,1},{4,6},{5,7},{6,4},{7,5},{8,10},{9,11},{10,... | collective-permute-start | bytes 393224 | tf_op jit(solution)/shard_map/ppermute | solution.py:592
  96.2 6.0 %collective-permute-start.19 = (bf16[4,128,128]{2,1,0:T(8,128)(2,1)S(1)}, bf16[4,128,128]{2,1,0:T(8,128)(2,1)S(1)}, u32[]{:S(2)}, u32[]{:S(2)}) collective-permute-start(bf16[4,128,128]{2,1,0:T(8,128)(2,1)S(1)} %get-tuple-element.104.s0.refs_1_), channel_id=1, source_target_pairs={{0,3},{1,0},{2,1},{3,2},{4,7},{5,4},{6,5},{7,6},{8,11},{9,8},{10,9... | collective-permute-start | bytes 393224 | tf_op jit(solution)/shard_map/ppermute | solution.py:592
  102.4 7.3 %collective-permute-start.20 = (bf16[4,128,128]{2,1,0:T(8,128)(2,1)S(1)}, bf16[4,128,128]{2,1,0:T(8,128)(2,1)S(1)}, u32[]{:S(2)}, u32[]{:S(2)}) collective-permute-start(bf16[4,128,128]{2,1,0:T(8,128)(2,1)S(1)} %upstream.4.own_ref), channel_id=1, source_target_pairs={{0,4},{4,0},{8,12},{12,8},{16,20},{20,16},{24,28},{28,24},{32,36},... | collective-permute-start | bytes 393224 | tf_op jit(solution)/shard_map/ppermute | solution.py:597
  123.0 30.7 %copy-start.20 = (bf16[2,2,4,64,128]{4,3,2,1,0:T(8,128)(2,1)S(1)}, bf16[2,2,4,64,128]{4,3,2,1,0:T(8,128)(2,1)}, u32[]{:S(2)}) copy-start(bf16[2,2,4,64,128]{4,3,2,1,0:T(8,128)(2,1)} %get-tuple-element.107.q_up) | copy-start | bytes 786436
  123.0 30.6 %copy-start.21 = (bf16[2,2,4,64,128]{4,3,2,1,0:T(8,128)(2,1)S(1)}, bf16[2,2,4,64,128]{4,3,2,1,0:T(8,128)(2,1)}, u32[]{:S(2)}) copy-start(bf16[2,2,4,64,128]{4,3,2,1,0:T(8,128)(2,1)} %get-tuple-element.108.q_down) | copy-start | bytes 786436
  123.0 38.7 %copy-start.14 = (bf16[2,2,4,64,128]{4,3,2,1,0:T(8,128)(2,1)S(1)}, bf16[2,2,4,64,128]{4,3,2,1,0:T(8,128)(2,1)}, u32[]{:S(2)}) copy-start(bf16[2,2,4,64,128]{4,3,2,1,0:T(8,128)(2,1)} %get-tuple-element.106.q_down) | copy-start | bytes 786436
  123.1 38.7 %copy-start.15 = (bf16[2,2,4,64,128]{4,3,2,1,0:T(8,128)(2,1)S(1)}, bf16[2,2,4,64,128]{4,3,2,1,0:T(8,128)(2,1)}, u32[]{:S(2)}) copy-start(bf16[2,2,4,64,128]{4,3,2,1,0:T(8,128)(2,1)} %get-tuple-element.105.q_up) | copy-start | bytes 786436
  123.1 41.7 %all-to-all-start.2 = ((bf16[4,8,288,128]{3,2,1,0:T(8,128)(2,1)}), bf16[4,8,288,128]{3,2,1,0:T(8,128)(2,1)}, u32[]{:S(2)}, u32[]{:S(2)}) async-start(bf16[4,8,288,128]{3,2,1,0:T(8,128)(2,1)} %get-tuple-element.119), calls=%async_computation.2 | async-start | bytes 4718592 | tf_op jit(solution)/shard_map/all_to_all | solution.py:517
  127.8 9.3 %collective-permute-start.21 = (bf16[2,2,4,64,128]{4,3,2,1,0:T(8,128)(2,1)S(1)}, bf16[2,2,4,64,128]{4,3,2,1,0:T(8,128)(2,1)S(1)}, u32[]{:S(2)}, u32[]{:S(2)}) collective-permute-start(bf16[2,2,4,64,128]{4,3,2,1,0:T(8,128)(2,1)S(1)} %copy-done.39), channel_id=1, source_target_pairs={{0,32},{4,36},{8,40},{12,44},{16,48},{20,52},{24,56},{28,60},{32,6... | collective-permute-start | bytes 786440 | tf_op jit(solution)/shard_map/ppermute | solution.py:459
  128.1 8.9 %collective-permute-start.22 = (bf16[2,2,4,64,128]{4,3,2,1,0:T(8,128)(2,1)S(1)}, bf16[2,2,4,64,128]{4,3,2,1,0:T(8,128)(2,1)S(1)}, u32[]{:S(2)}, u32[]{:S(2)}) collective-permute-start(bf16[2,2,4,64,128]{4,3,2,1,0:T(8,128)(2,1)S(1)} %copy-done.36), channel_id=1, source_target_pairs={{0,224},{4,228},{8,232},{12,236},{16,240},{20,244},{24,248},{28,25... | collective-permute-start | bytes 786440 | tf_op jit(solution)/shard_map/ppermute | solution.py:460
  137.3 11.4 %collective-permute-start.23 = (bf16[2,2,4,64,128]{4,3,2,1,0:T(8,128)(2,1)S(1)}, bf16[2,2,4,64,128]{4,3,2,1,0:T(8,128)(2,1)S(1)}, u32[]{:S(2)}, u32[]{:S(2)}) collective-permute-start(bf16[2,2,4,64,128]{4,3,2,1,0:T(8,128)(2,1)S(1)} %get-tuple-element.113), channel_id=1, source_target_pairs={{0,32},{4,36},{8,40},{12,44},{16,48},{20,52},{24,56},{28,60},{32,6... | collective-permute-start | bytes 786440 | tf_op jit(solution)/shard_map/ppermute | solution.py:459
  137.4 16.3 %collective-permute-start.24 = (bf16[2,2,4,64,128]{4,3,2,1,0:T(8,128)(2,1)S(1)}, bf16[2,2,4,64,128]{4,3,2,1,0:T(8,128)(2,1)S(1)}, u32[]{:S(2)}, u32[]{:S(2)}) collective-permute-start(bf16[2,2,4,64,128]{4,3,2,1,0:T(8,128)(2,1)S(1)} %get-tuple-element.114), channel_id=1, source_target_pairs={{0,224},{4,228},{8,232},{12,236},{16,240},{20,244},{24,248},{28,25... | collective-permute-start | bytes 786440 | tf_op jit(solution)/shard_map/ppermute | solution.py:460
  153.9 7.8 %collective-permute-start.25 = (bf16[2,2,4,64,128]{4,3,2,1,0:T(8,128)(2,1)S(1)}, bf16[2,2,4,64,128]{4,3,2,1,0:T(8,128)(2,1)S(1)}, u32[]{:S(2)}, u32[]{:S(2)}) collective-permute-start(bf16[2,2,4,64,128]{4,3,2,1,0:T(8,128)(2,1)S(1)} %get-tuple-element.115), channel_id=1, source_target_pairs={{0,32},{4,36},{8,40},{12,44},{16,48},{20,52},{24,56},{28,60},{32,6... | collective-permute-start | bytes 786440 | tf_op jit(solution)/shard_map/ppermute | solution.py:459
  154.0 7.7 %collective-permute-start.26 = (bf16[2,2,4,64,128]{4,3,2,1,0:T(8,128)(2,1)S(1)}, bf16[2,2,4,64,128]{4,3,2,1,0:T(8,128)(2,1)S(1)}, u32[]{:S(2)}, u32[]{:S(2)}) collective-permute-start(bf16[2,2,4,64,128]{4,3,2,1,0:T(8,128)(2,1)S(1)} %get-tuple-element.116), channel_id=1, source_target_pairs={{0,224},{4,228},{8,232},{12,236},{16,240},{20,244},{24,248},{28,25... | collective-permute-start | bytes 786440 | tf_op jit(solution)/shard_map/ppermute | solution.py:460
  162.0 5.2 %collective-permute-start.27 = (bf16[2,4,64,128]{3,2,1,0:T(8,128)(2,1)S(1)}, bf16[2,4,64,128]{3,2,1,0:T(8,128)(2,1)S(1)}, u32[]{:S(2)}, u32[]{:S(2)}) collective-permute-start(bf16[2,4,64,128]{3,2,1,0:T(8,128)(2,1)S(1)} %get-tuple-element.117), channel_id=1, source_target_pairs={{0,32},{4,36},{8,40},{12,44},{16,48},{20,52},{24,56},{28,60},{32,6... | collective-permute-start | bytes 393224 | tf_op jit(solution)/shard_map/ppermute | solution.py:464
  162.1 5.1 %collective-permute-start.28 = (bf16[2,4,64,128]{3,2,1,0:T(8,128)(2,1)S(1)}, bf16[2,4,64,128]{3,2,1,0:T(8,128)(2,1)S(1)}, u32[]{:S(2)}, u32[]{:S(2)}) collective-permute-start(bf16[2,4,64,128]{3,2,1,0:T(8,128)(2,1)S(1)} %get-tuple-element.118), channel_id=1, source_target_pairs={{0,224},{4,228},{8,232},{12,236},{16,240},{20,244},{24,248},{28,25... | collective-permute-start | bytes 393224 | tf_op jit(solution)/shard_map/ppermute | solution.py:465
  167.2 18.6 %all-to-all-start.3 = ((bf16[8,288,128]{2,1,0:T(8,128)(2,1)}), bf16[8,288,128]{2,1,0:T(8,128)(2,1)S(1)}, u32[]{:S(2)}, u32[]{:S(2)}) async-start(bf16[8,288,128]{2,1,0:T(8,128)(2,1)} %sum_y.4), calls=%async_computation.3 | async-start | bytes 1179648 | tf_op jit(solution)/shard_map/all_to_all | solution.py:526
  171.1 5.9 %collective-permute-start.29 = (bf16[4,64,128]{2,1,0:T(8,128)(2,1)S(1)}, bf16[4,64,128]{2,1,0:T(8,128)(2,1)S(1)}, u32[]{:S(2)}, u32[]{:S(2)}) collective-permute-start(bf16[4,64,128]{2,1,0:T(8,128)(2,1)S(1)} %get-tuple-element.125), channel_id=1, source_target_pairs={{0,8},{4,12},{8,16},{12,20},{16,24},{20,28},{24,0},{28,4},{32,40},... | collective-permute-start | bytes 196616 | tf_op jit(solution)/shard_map/ppermute | solution.py:527
  171.2 5.7 %collective-permute-start.30 = (bf16[4,64,128]{2,1,0:T(8,128)(2,1)S(1)}, bf16[4,64,128]{2,1,0:T(8,128)(2,1)S(1)}, u32[]{:S(2)}, u32[]{:S(2)}) collective-permute-start(bf16[4,64,128]{2,1,0:T(8,128)(2,1)S(1)} %get-tuple-element.126), channel_id=1, source_target_pairs={{0,16},{4,20},{8,24},{12,28},{16,0},{20,4},{24,8},{28,12},{32,48},... | collective-permute-start | bytes 196616 | tf_op jit(solution)/shard_map/ppermute | solution.py:527
  173.9 3.1 %collective-permute-start.31 = (bf16[4,64,128]{2,1,0:T(8,128)(2,1)S(1)}, bf16[4,64,128]{2,1,0:T(8,128)(2,1)S(1)}, u32[]{:S(2)}, u32[]{:S(2)}) collective-permute-start(bf16[4,64,128]{2,1,0:T(8,128)(2,1)S(1)} %get-tuple-element.127), channel_id=1, source_target_pairs={{0,24},{4,28},{8,0},{12,4},{16,8},{20,12},{24,16},{28,20},{32,56},... | collective-permute-start | bytes 196616 | tf_op jit(solution)/shard_map/ppermute | solution.py:527
  186.9 5.1 %collective-permute-start.32 = (bf16[4,128,128]{2,1,0:T(8,128)(2,1)S(1)}, bf16[4,128,128]{2,1,0:T(8,128)(2,1)S(1)}, u32[]{:S(2)}, u32[]{:S(2)}) collective-permute-start(bf16[4,128,128]{2,1,0:T(8,128)(2,1)S(1)} %get-tuple-element.129.s0.refs_1_), channel_id=1, source_target_pairs={{0,1},{1,2},{2,3},{3,0},{4,5},{5,6},{6,7},{7,4},{8,9},{9,10},{10,1... | collective-permute-start | bytes 393224 | tf_op jit(solution)/shard_map/ppermute | solution.py:592
  187.6 6.7 %collective-permute-start.33 = (bf16[4,128,128]{2,1,0:T(8,128)(2,1)S(1)}, bf16[4,128,128]{2,1,0:T(8,128)(2,1)S(1)}, u32[]{:S(2)}, u32[]{:S(2)}) collective-permute-start(bf16[4,128,128]{2,1,0:T(8,128)(2,1)S(1)} %get-tuple-element.129.s0.refs_1_), channel_id=1, source_target_pairs={{0,2},{1,3},{2,0},{3,1},{4,6},{5,7},{6,4},{7,5},{8,10},{9,11},{10,... | collective-permute-start | bytes 393224 | tf_op jit(solution)/shard_map/ppermute | solution.py:592
  190.5 3.8 %collective-permute-start.34 = (bf16[4,128,128]{2,1,0:T(8,128)(2,1)S(1)}, bf16[4,128,128]{2,1,0:T(8,128)(2,1)S(1)}, u32[]{:S(2)}, u32[]{:S(2)}) collective-permute-start(bf16[4,128,128]{2,1,0:T(8,128)(2,1)S(1)} %get-tuple-element.129.s0.refs_1_), channel_id=1, source_target_pairs={{0,3},{1,0},{2,1},{3,2},{4,7},{5,4},{6,5},{7,6},{8,11},{9,8},{10,9... | collective-permute-start | bytes 393224 | tf_op jit(solution)/shard_map/ppermute | solution.py:592
  194.7 9.0 %collective-permute-start.35 = (bf16[4,128,128]{2,1,0:T(8,128)(2,1)S(1)}, bf16[4,128,128]{2,1,0:T(8,128)(2,1)S(1)}, u32[]{:S(2)}, u32[]{:S(2)}) collective-permute-start(bf16[4,128,128]{2,1,0:T(8,128)(2,1)S(1)} %upstream.5.own_ref), channel_id=1, source_target_pairs={{0,4},{4,0},{8,12},{12,8},{16,20},{20,16},{24,28},{28,24},{32,36},... | collective-permute-start | bytes 393224 | tf_op jit(solution)/shard_map/ppermute | solution.py:597
  217.0 30.7 %copy-start.10 = (bf16[2,2,4,64,128]{4,3,2,1,0:T(8,128)(2,1)S(1)}, bf16[2,2,4,64,128]{4,3,2,1,0:T(8,128)(2,1)}, u32[]{:S(2)}) copy-start(bf16[2,2,4,64,128]{4,3,2,1,0:T(8,128)(2,1)} %get-tuple-element.131.q_down) | copy-start | bytes 786436
  217.0 30.7 %copy-start.11 = (bf16[2,2,4,64,128]{4,3,2,1,0:T(8,128)(2,1)S(1)}, bf16[2,2,4,64,128]{4,3,2,1,0:T(8,128)(2,1)}, u32[]{:S(2)}) copy-start(bf16[2,2,4,64,128]{4,3,2,1,0:T(8,128)(2,1)} %get-tuple-element.130.q_up) | copy-start | bytes 786436
  217.0 34.0 %all-to-all-start.4 = ((bf16[4,8,288,128]{3,2,1,0:T(8,128)(2,1)}), bf16[4,8,288,128]{3,2,1,0:T(8,128)(2,1)}, u32[]{:S(2)}, u32[]{:S(2)}) async-start(bf16[4,8,288,128]{3,2,1,0:T(8,128)(2,1)} %get-tuple-element.144), calls=%async_computation.4 | async-start | bytes 4718592 | tf_op jit(solution)/shard_map/all_to_all | solution.py:517
  221.7 9.3 %collective-permute-start.36 = (bf16[2,2,4,64,128]{4,3,2,1,0:T(8,128)(2,1)S(1)}, bf16[2,2,4,64,128]{4,3,2,1,0:T(8,128)(2,1)S(1)}, u32[]{:S(2)}, u32[]{:S(2)}) collective-permute-start(bf16[2,2,4,64,128]{4,3,2,1,0:T(8,128)(2,1)S(1)} %copy-done.37), channel_id=1, source_target_pairs={{0,32},{4,36},{8,40},{12,44},{16,48},{20,52},{24,56},{28,60},{32,6... | collective-permute-start | bytes 786440 | tf_op jit(solution)/shard_map/ppermute | solution.py:459
  222.0 8.9 %collective-permute-start.37 = (bf16[2,2,4,64,128]{4,3,2,1,0:T(8,128)(2,1)S(1)}, bf16[2,2,4,64,128]{4,3,2,1,0:T(8,128)(2,1)S(1)}, u32[]{:S(2)}, u32[]{:S(2)}) collective-permute-start(bf16[2,2,4,64,128]{4,3,2,1,0:T(8,128)(2,1)S(1)} %copy-done.34), channel_id=1, source_target_pairs={{0,224},{4,228},{8,232},{12,236},{16,240},{20,244},{24,248},{28,25... | collective-permute-start | bytes 786440 | tf_op jit(solution)/shard_map/ppermute | solution.py:460
  231.2 8.5 %collective-permute-start.38 = (bf16[2,2,4,64,128]{4,3,2,1,0:T(8,128)(2,1)S(1)}, bf16[2,2,4,64,128]{4,3,2,1,0:T(8,128)(2,1)S(1)}, u32[]{:S(2)}, u32[]{:S(2)}) collective-permute-start(bf16[2,2,4,64,128]{4,3,2,1,0:T(8,128)(2,1)S(1)} %get-tuple-element.138), channel_id=1, source_target_pairs={{0,32},{4,36},{8,40},{12,44},{16,48},{20,52},{24,56},{28,60},{32,6... | collective-permute-start | bytes 786440 | tf_op jit(solution)/shard_map/ppermute | solution.py:459
  231.3 8.4 %collective-permute-start.39 = (bf16[2,2,4,64,128]{4,3,2,1,0:T(8,128)(2,1)S(1)}, bf16[2,2,4,64,128]{4,3,2,1,0:T(8,128)(2,1)S(1)}, u32[]{:S(2)}, u32[]{:S(2)}) collective-permute-start(bf16[2,2,4,64,128]{4,3,2,1,0:T(8,128)(2,1)S(1)} %get-tuple-element.139), channel_id=1, source_target_pairs={{0,224},{4,228},{8,232},{12,236},{16,240},{20,244},{24,248},{28,25... | collective-permute-start | bytes 786440 | tf_op jit(solution)/shard_map/ppermute | solution.py:460
  240.0 7.7 %collective-permute-start.40 = (bf16[2,2,4,64,128]{4,3,2,1,0:T(8,128)(2,1)S(1)}, bf16[2,2,4,64,128]{4,3,2,1,0:T(8,128)(2,1)S(1)}, u32[]{:S(2)}, u32[]{:S(2)}) collective-permute-start(bf16[2,2,4,64,128]{4,3,2,1,0:T(8,128)(2,1)S(1)} %get-tuple-element.140), channel_id=1, source_target_pairs={{0,32},{4,36},{8,40},{12,44},{16,48},{20,52},{24,56},{28,60},{32,6... | collective-permute-start | bytes 786440 | tf_op jit(solution)/shard_map/ppermute | solution.py:459
  240.1 7.6 %collective-permute-start.41 = (bf16[2,2,4,64,128]{4,3,2,1,0:T(8,128)(2,1)S(1)}, bf16[2,2,4,64,128]{4,3,2,1,0:T(8,128)(2,1)S(1)}, u32[]{:S(2)}, u32[]{:S(2)}) collective-permute-start(bf16[2,2,4,64,128]{4,3,2,1,0:T(8,128)(2,1)S(1)} %get-tuple-element.141), channel_id=1, source_target_pairs={{0,224},{4,228},{8,232},{12,236},{16,240},{20,244},{24,248},{28,25... | collective-permute-start | bytes 786440 | tf_op jit(solution)/shard_map/ppermute | solution.py:460
  247.9 5.5 %collective-permute-start.42 = (bf16[2,4,64,128]{3,2,1,0:T(8,128)(2,1)S(1)}, bf16[2,4,64,128]{3,2,1,0:T(8,128)(2,1)S(1)}, u32[]{:S(2)}, u32[]{:S(2)}) collective-permute-start(bf16[2,4,64,128]{3,2,1,0:T(8,128)(2,1)S(1)} %get-tuple-element.142), channel_id=1, source_target_pairs={{0,32},{4,36},{8,40},{12,44},{16,48},{20,52},{24,56},{28,60},{32,6... | collective-permute-start | bytes 393224 | tf_op jit(solution)/shard_map/ppermute | solution.py:464
  248.0 5.4 %collective-permute-start.43 = (bf16[2,4,64,128]{3,2,1,0:T(8,128)(2,1)S(1)}, bf16[2,4,64,128]{3,2,1,0:T(8,128)(2,1)S(1)}, u32[]{:S(2)}, u32[]{:S(2)}) collective-permute-start(bf16[2,4,64,128]{3,2,1,0:T(8,128)(2,1)S(1)} %get-tuple-element.143), channel_id=1, source_target_pairs={{0,224},{4,228},{8,232},{12,236},{16,240},{20,244},{24,248},{28,25... | collective-permute-start | bytes 393224 | tf_op jit(solution)/shard_map/ppermute | solution.py:465
  271.3 6.6 %collective-permute-start.47 = (f32[48,128]{1,0:T(8,128)S(1)}, f32[48,128]{1,0:T(8,128)S(1)}, u32[]{:S(2)}, u32[]{:S(2)}) collective-permute-start(f32[48,128]{1,0:T(8,128)S(1)} %pad_maximum_fusion.a_ref), channel_id=1, source_target_pairs={{0,4},{4,0},{8,12},{12,8},{16,20},{20,16},{24,28},{28,24},{32,36},... | collective-permute-start | bytes 73736 | tf_op jit(solution)/shard_map/ppermute | solution.py:197
  280.0 18.3 %all-to-all-start.6 = ((bf16[32,48,128]{2,1,0:T(8,128)(2,1)}), bf16[32,48,128]{2,1,0:T(8,128)(2,1)S(1)}, u32[]{:S(2)}, u32[]{:S(2)}) async-start(bf16[32,48,128]{2,1,0:T(8,128)(2,1)} %spread.1), calls=%async_computation.6 | async-start | bytes 786432 | tf_op jit(solution)/shard_map/all_to_all | solution.py:212
  283.9 5.3 %collective-permute-start.44 = (bf16[4,64,128]{2,1,0:T(8,128)(2,1)S(1)}, bf16[4,64,128]{2,1,0:T(8,128)(2,1)S(1)}, u32[]{:S(2)}, u32[]{:S(2)}) collective-permute-start(bf16[4,64,128]{2,1,0:T(8,128)(2,1)S(1)} %get-tuple-element.150), channel_id=1, source_target_pairs={{0,8},{4,12},{8,16},{12,20},{16,24},{20,28},{24,0},{28,4},{32,40},... | collective-permute-start | bytes 196616 | tf_op jit(solution)/shard_map/ppermute | solution.py:527
  285.1 6.8 %collective-permute-start.45 = (bf16[4,64,128]{2,1,0:T(8,128)(2,1)S(1)}, bf16[4,64,128]{2,1,0:T(8,128)(2,1)S(1)}, u32[]{:S(2)}, u32[]{:S(2)}) collective-permute-start(bf16[4,64,128]{2,1,0:T(8,128)(2,1)S(1)} %get-tuple-element.151), channel_id=1, source_target_pairs={{0,16},{4,20},{8,24},{12,28},{16,0},{20,4},{24,8},{28,12},{32,48},... | collective-permute-start | bytes 196616 | tf_op jit(solution)/shard_map/ppermute | solution.py:527
  287.5 5.8 %collective-permute-start.46 = (bf16[4,64,128]{2,1,0:T(8,128)(2,1)S(1)}, bf16[4,64,128]{2,1,0:T(8,128)(2,1)S(1)}, u32[]{:S(2)}, u32[]{:S(2)}) collective-permute-start(bf16[4,64,128]{2,1,0:T(8,128)(2,1)S(1)} %get-tuple-element.152), channel_id=1, source_target_pairs={{0,24},{4,28},{8,0},{12,4},{16,8},{20,12},{24,16},{28,20},{32,56},... | collective-permute-start | bytes 196616 | tf_op jit(solution)/shard_map/ppermute | solution.py:527
  (31 other events, 280.2 us)
where the time goes:
time: 305 us; the launch traced here: 300 us
  starting transfers between devices  116 us (38%)
  waiting for transfers between devices  87.4 us (29%)
  Pallas kernels  63.4 us (21%)
  blocking collectives  17.8 us (6%)
  local copies, waits for them, and re-layouts  9.85 us (3%)
    ppermute x9, waiting for transfers between devices, ring(): got_up = lax.ppermute(up, 'dp', ahead)  44.6 us
    pallas_call x3, Pallas kernels, messages_of(): pl.pallas_call(message_kernel, out_shape=(jax.ShapeDtypeStruct((NY, NZ, R...  37.8 us
    ppermute x9, starting transfers between devices, ring(): got_down = lax.ppermute(down, 'dp', back)  33.6 us
    all_to_all x2, waiting for transfers between devices, exchange(): lax.all_to_all(made['sums'], 'dp', 0, 0, axis_index_groups=Z_GROUPS, tile...  19.1 us
    all_to_all x1, blocking collectives, exchange(): lax.all_to_all(made['sums'], 'dp', 0, 0, axis_index_groups=Z_GROUPS, tile...  17.8 us
    all_to_all x3, starting transfers between devices, exchange(): lax.all_to_all(out_a, 'dp', 0, 0, axis_index_groups=Y_GROUPS, tiled=True)  14 us
    ppermute x3, starting transfers between devices, on_device(): sibling = lax.ppermute(own, 'dp', shift(dc=1))  12.2 us
    ppermute x9, starting transfers between devices, exchange(): lax.ppermute(x, 'dp', shift(dy=d + 1))  11.4 us
  transfers between devices with their start and end apart: 54, of which 25 were waited for; matrix products, arithmetic and copies ran while one was open for 2% of the time, Pallas kernels for 8%

commit v1 on v0

--- a/solution.py
+++ b/solution.py
@@ -15,8 +15,10 @@
 SLOTS = NZ * NY * NB
 EDGES = 256
 UNROLL = 8
+CHUNKS = 8
 ITEMS = 264
 HALF = 64
+REST = BLK - HALF
 
 bf16 = jnp.bfloat16
 f32 = jnp.float32
@@ -41,7 +43,7 @@
 
 
 YZ_GROUPS = [[index_of(z, y, c) for z in range(NZ) for y in range(NY)] for c in range(NC)]
-PAIR = (2, NY // 2, NB, HALF, BLK)
+PAIR = (2, NY // 2, NB, REST, BLK)
 SUM_Y_COST = 1
 SUMS = 512 // (NZ * NY)
 ROWS = NB * HALF + 2 * SUMS
@@ -217,11 +219,22 @@
 def message_kernel(table, own_ref, sib_ref, a_own, a_sib, weight_ref, out_a, *rest):
     out_b = rest[:NZ]
     edges, acc, up, stage, stage_b, sems, out_sems, out_b_sems = rest[NZ:]
+    many = EDGES // 2 // CHUNKS
     copies = [
-        pltpu.make_async_copy(a_own, edges.at[pl.ds(0, EDGES // 2)], sems.at[0]),
-        pltpu.make_async_copy(a_sib, edges.at[pl.ds(EDGES // 2, EDGES // 2)], sems.at[1]),
+        pltpu.make_async_copy(
+            source.at[pl.ds(i * many, many)],
+            edges.at[pl.ds(side * (EDGES // 2) + i * many, many)],
+            sems.at[side * CHUNKS + i],
+        )
+        for side, source in enumerate((a_own, a_sib))
+        for i in range(CHUNKS)
     ]
-    copies[0].start()
+    for copy in copies:
+        copy.start()
+    weight_copy = pltpu.make_async_copy(
+        weight_ref, out_a.at[:, :, pl.ds(NB * HALF, 2 * SUMS)], sems.at[2 * CHUNKS]
+    )
+    weight_copy.start()
     up[0:NB] = own_ref[...]
     up[NB : 2 * NB] = sib_ref[...]
     up[2 * NB] = jnp.zeros((BLK, BLK), bf16)
@@ -244,14 +257,11 @@
             acc[slot] = acc[slot] + sums[j]
 
     early = n_own // UNROLL
-    copies[0].wait()
-    copies[1].start()
-    weight_copy = pltpu.make_async_copy(
-        weight_ref, out_a.at[:, :, pl.ds(NB * HALF, 2 * SUMS)], sems.at[2]
-    )
-    weight_copy.start()
+    for copy in copies[:CHUNKS]:
+        copy.wait()
     pl.loop(0, early)(add_items)
-    copies[1].wait()
+    for copy in copies[CHUNKS:]:
+        copy.wait()
     pl.loop(early, (n_items + UNROLL - 1) // UNROLL)(add_items)
 
     z, y = table[5 * ITEMS + 1], table[5 * ITEMS + 2]
@@ -288,7 +298,7 @@
         message_kernel,
         out_shape=(jax.ShapeDtypeStruct((NY, NZ, ROWS, BLK), bf16),)
         + (jax.ShapeDtypeStruct(PAIR, bf16),) * NZ,
-        in_specs=[pl.BlockSpec(memory_space=pltpu.SMEM), vmem(), vmem(), hbm, hbm, hbm],
+        in_specs=[pl.BlockSpec(memory_space=pltpu.SMEM), vmem(), vmem(), hbm, hbm, vmem()],
         out_specs=(hbm,) * (NZ + 1),
         scratch_shapes=[
             pltpu.VMEM((EDGES, BLK, BLK), bf16),
@@ -296,7 +306,7 @@
             pltpu.VMEM((2 * NB + 1, BLK, BLK), bf16),
             pltpu.VMEM((NZ, NY, NB * HALF, BLK), bf16),
             pltpu.VMEM((NZ,) + PAIR, bf16),
-            pltpu.SemaphoreType.DMA((3,)),
+            pltpu.SemaphoreType.DMA((2 * CHUNKS + 1,)),
             pltpu.SemaphoreType.DMA((NZ * NY,)),
             pltpu.SemaphoreType.DMA((NZ,)),
         ],
@@ -438,7 +448,7 @@
 
 
 def ring_end(keep, last_up, last_down):
-    shape = (NB, HALF, BLK)
+    shape = (NB, REST, BLK)
     return pl.pallas_call(
         ring_end_kernel,
         out_shape=(jax.ShapeDtypeStruct(shape, f32),)

time: 305 us -> 294 us (0.964)
  Pallas kernels: 63.4 us -> 51.3 us
    pallas_call x3, Pallas kernels: 37.8 us -> 25.7 us  [messages_of(): pl.pallas_call(message_kernel, out_shape=(jax.ShapeDtypeStruct((NY, NZ, R...]
  transfers between devices with their start and end apart: 54 -> 54, of which waited for: 25 -> 24; matrix products, arithmetic and copies ran while one was open for 2% -> 2% of each run, Pallas kernels for 8% -> 8%
where the time goes in v1:
time: 294 us; the launch traced here: 288 us
  starting transfers between devices  118 us (40%)
  waiting for transfers between devices  86.2 us (29%)
  Pallas kernels  51.3 us (17%)
  blocking collectives  17.8 us (6%)
  local copies, waits for them, and re-layouts  9.85 us (3%)
    ppermute x9, waiting for transfers between devices, ring(): got_up = lax.ppermute(up, 'dp', ahead)  44.7 us
    ppermute x9, starting transfers between devices, ring(): got_down = lax.ppermute(down, 'dp', back)  31.8 us
    pallas_call x3, Pallas kernels, messages_of(): pl.pallas_call(message_kernel, out_shape=(jax.ShapeDtypeStruct((NY, NZ, R...  25.7 us
    all_to_all x2, waiting for transfers between devices, exchange(): lax.all_to_all(made['sums'], 'dp', 0, 0, axis_index_groups=Z_GROUPS, tile...  18.9 us
    all_to_all x1, blocking collectives, exchange(): lax.all_to_all(made['sums'], 'dp', 0, 0, axis_index_groups=Z_GROUPS, tile...  17.8 us
    all_to_all x3, starting transfers between devices, exchange(): lax.all_to_all(out_a, 'dp', 0, 0, axis_index_groups=Y_GROUPS, tiled=True)  14 us
    ppermute x3, starting transfers between devices, on_device(): sibling = lax.ppermute(own, 'dp', shift(dc=1))  12.2 us
    ppermute x9, starting transfers between devices, exchange(): lax.ppermute(x, 'dp', shift(dy=d + 1))  12.2 us
  transfers between devices with their start and end apart: 54, of which 24 were waited for; matrix products, arithmetic and copies ran while one was open for 2% of the time, Pallas kernels for 8%

profile of v1, /device:TPU:1, one launch (start us, length us, event | category | flops | bytes accessed | tf_op | source)
XLA Modules:
  0.0 288.1 jit_solution(13207913201473180314)
XLA Ops:
  0.7 3.3 %collective-permute-start.5 = (bf16[128,128,128]{2,1,0:T(8,128)(2,1)}, bf16[128,128,128]{2,1,0:T(8,128)(2,1)}, u32[]{:S(2)}, u32[]{:S(2)}) collective-permute-start(bf16[128,128,128]{2,1,0:T(8,128)(2,1)} %a_own.5), channel_id=1, source_target_pairs={{0,4},{4,0},{8,12},{12,8},{16,20},{20,16},{24,28},{28,24},{32,36},... | collective-permute-start | bytes 12582920 | tf_op jit(solution)/shard_map/ppermute | solution.py:591
  4.0 2.2 first_slopes.1
  6.2 1.9 collective-permute-start.2
  9.9 1.3 gather_fusion
  13.3 2.1 weight_part.3.weight_ref
  18.2 2.0 concatenate.102.table
  20.9 8.6 %messages.3 = (bf16[4,8,288,128]{3,2,1,0:T(8,128)(2,1)}, bf16[2,2,4,64,128]{4,3,2,1,0:T(8,128)(2,1)}, bf16[2,2,4,64,128]{4,3,2,1,0:T(8,128)(2,1)}, bf16[2,2,4,64...) custom-call(s32[1324]{0:T(1024)} %concatenate.102.table, ...), custom_call_target="tpu_custom_call" | custom-call | bytes 19800000 | tf_op jit(solution)/shard_map/messages/pallas_call | solution.py:297
  29.6 4.7 %all-to-all-start = ((bf16[4,8,288,128]{3,2,1,0:T(8,128)(2,1)}), bf16[4,8,288,128]{3,2,1,0:T(8,128)(2,1)}, u32[]{:S(2)}, u32[]{:S(2)}) async-start(bf16[4,8,288,128]{3,2,1,0:T(8,128)(2,1)} %get-tuple-element.94), calls=%async_computation | async-start | bytes 4718592 | tf_op jit(solution)/shard_map/all_to_all | solution.py:527
  34.3 2.0 collective-permute-start.6
  36.2 3.8 %collective-permute-start.7 = (bf16[2,2,4,64,128]{4,3,2,1,0:T(8,128)(2,1)S(1)}, bf16[2,2,4,64,128]{4,3,2,1,0:T(8,128)(2,1)S(1)}, u32[]{:S(2)}, u32[]{:S(2)}) collective-permute-start(bf16[2,2,4,64,128]{4,3,2,1,0:T(8,128)(2,1)S(1)} %copy-done.35), channel_id=1, source_target_pairs={{0,224},{4,228},{8,232},{12,236},{16,240},{20,244},{24,248},{28,25... | collective-permute-start | bytes 786440 | tf_op jit(solution)/shard_map/ppermute | solution.py:470
  40.0 6.3 %collective-permute-done.6.got_up = bf16[2,2,4,64,128]{4,3,2,1,0:T(8,128)(2,1)S(1)} collective-permute-done((bf16[2,2,4,64,128]{4,3,2,1,0:T(8,128)(2,1)S(1)}, bf16[2,2,4,64,128]{4,3,2,1,0:T(8,128)(2,1)S(1)}, u32[]{:S(2)}, u32[]{:S(2)}) %collective-permute-start.6) | collective-permute-done | bytes 262176 | tf_op jit(solution)/shard_map/ppermute | solution.py:469
  46.7 2.7 collective-permute-start.9
  49.3 5.6 %collective-permute-done.8.got_up = bf16[2,2,4,64,128]{4,3,2,1,0:T(8,128)(2,1)S(1)} collective-permute-done((bf16[2,2,4,64,128]{4,3,2,1,0:T(8,128)(2,1)S(1)}, bf16[2,2,4,64,128]{4,3,2,1,0:T(8,128)(2,1)S(1)}, u32[]{:S(2)}, u32[]{:S(2)}) %collective-permute-start.8) | collective-permute-done | bytes 262176 | tf_op jit(solution)/shard_map/ppermute | solution.py:469
  55.2 1.6 collective-permute-start.10
  56.7 1.4 collective-permute-start.11
  58.1 4.5 %collective-permute-done.10.got_up = bf16[2,2,4,64,128]{4,3,2,1,0:T(8,128)(2,1)S(1)} collective-permute-done((bf16[2,2,4,64,128]{4,3,2,1,0:T(8,128)(2,1)S(1)}, bf16[2,2,4,64,128]{4,3,2,1,0:T(8,128)(2,1)S(1)}, u32[]{:S(2)}, u32[]{:S(2)}) %collective-permute-start.10) | collective-permute-done | bytes 262176 | tf_op jit(solution)/shard_map/ppermute | solution.py:469
  62.9 1.7 collective-permute-start.12
  65.7 2.4 sum_y.3
  68.4 6.0 %all-to-all-start.1 = ((bf16[8,288,128]{2,1,0:T(8,128)(2,1)}), bf16[8,288,128]{2,1,0:T(8,128)(2,1)S(1)}, u32[]{:S(2)}, u32[]{:S(2)}) async-start(bf16[8,288,128]{2,1,0:T(8,128)(2,1)} %sum_y.3), calls=%async_computation.1 | async-start | bytes 1179648 | tf_op jit(solution)/shard_map/all_to_all | solution.py:536
  74.6 2.0 collective-permute-start.15
  76.6 1.6 collective-permute-start.16
  78.2 2.1 factors.2.refs_5_
  80.4 10.2 %all-to-all-done.1.from_z = bf16[8,288,128]{2,1,0:T(8,128)(2,1)S(1)} async-done(((bf16[8,288,128]{2,1,0:T(8,128)(2,1)}), bf16[8,288,128]{2,1,0:T(8,128)(2,1)S(1)}, u32[]{:S(2)}, u32[]{:S(2)}) %all-to-all-start.1) | async-done | bytes 589856 | tf_op jit(solution)/shard_map/all_to_all | solution.py:536
  92.0 1.8 collective-permute-start.18
  95.1 3.0 %collective-permute-done.17.s1 = bf16[4,128,128]{2,1,0:T(8,128)(2,1)S(1)} collective-permute-done((bf16[4,128,128]{2,1,0:T(8,128)(2,1)S(1)}, bf16[4,128,128]{2,1,0:T(8,128)(2,1)S(1)}, u32[]{:S(2)}, u32[]{:S(2)}) %collective-permute-start.17) | collective-permute-done | bytes 131104 | tf_op jit(solution)/shard_map/ppermute | solution.py:602
  99.0 5.2 %collective-permute-start.20 = (bf16[4,128,128]{2,1,0:T(8,128)(2,1)S(1)}, bf16[4,128,128]{2,1,0:T(8,128)(2,1)S(1)}, u32[]{:S(2)}, u32[]{:S(2)}) collective-permute-start(bf16[4,128,128]{2,1,0:T(8,128)(2,1)S(1)} %upstream.4.own_ref), channel_id=1, source_target_pairs={{0,4},{4,0},{8,12},{12,8},{16,20},{20,16},{24,28},{28,24},{32,36},... | collective-permute-start | bytes 393224 | tf_op jit(solution)/shard_map/ppermute | solution.py:607
  104.3 2.1 weight_part.4.weight_ref
  107.0 8.5 %messages.4 = (bf16[4,8,288,128]{3,2,1,0:T(8,128)(2,1)}, bf16[2,2,4,64,128]{4,3,2,1,0:T(8,128)(2,1)}, bf16[2,2,4,64,128]{4,3,2,1,0:T(8,128)(2,1)}, bf16[2,2,4,64...) custom-call(s32[1324]{0:T(1024)} %concatenate.102.table, ...), custom_call_target="tpu_custom_call" | custom-call | bytes 19800000 | tf_op jit(solution)/shard_map/messages/pallas_call | solution.py:297
  115.7 4.7 %all-to-all-start.2 = ((bf16[4,8,288,128]{3,2,1,0:T(8,128)(2,1)}), bf16[4,8,288,128]{3,2,1,0:T(8,128)(2,1)}, u32[]{:S(2)}, u32[]{:S(2)}) async-start(bf16[4,8,288,128]{3,2,1,0:T(8,128)(2,1)} %get-tuple-element.119), calls=%async_computation.2 | async-start | bytes 4718592 | tf_op jit(solution)/shard_map/all_to_all | solution.py:527
  121.0 2.1 collective-permute-start.22
  123.1 6.6 %collective-permute-done.21.got_up = bf16[2,2,4,64,128]{4,3,2,1,0:T(8,128)(2,1)S(1)} collective-permute-done((bf16[2,2,4,64,128]{4,3,2,1,0:T(8,128)(2,1)S(1)}, bf16[2,2,4,64,128]{4,3,2,1,0:T(8,128)(2,1)S(1)}, u32[]{:S(2)}, u32[]{:S(2)}) %collective-permute-start.21) | collective-permute-done | bytes 262176 | tf_op jit(solution)/shard_map/ppermute | solution.py:469
  130.0 11.4 %collective-permute-start.24 = (bf16[2,2,4,64,128]{4,3,2,1,0:T(8,128)(2,1)S(1)}, bf16[2,2,4,64,128]{4,3,2,1,0:T(8,128)(2,1)S(1)}, u32[]{:S(2)}, u32[]{:S(2)}) collective-permute-start(bf16[2,2,4,64,128]{4,3,2,1,0:T(8,128)(2,1)S(1)} %get-tuple-element.114), channel_id=1, source_target_pairs={{0,224},{4,228},{8,232},{12,236},{16,240},{20,244},{24,248},{28,25... | collective-permute-start | bytes 786440 | tf_op jit(solution)/shard_map/ppermute | solution.py:470
  141.4 4.9 %collective-permute-done.24.got_down = bf16[2,2,4,64,128]{4,3,2,1,0:T(8,128)(2,1)S(1)} collective-permute-done((bf16[2,2,4,64,128]{4,3,2,1,0:T(8,128)(2,1)S(1)}, bf16[2,2,4,64,128]{4,3,2,1,0:T(8,128)(2,1)S(1)}, u32[]{:S(2)}, u32[]{:S(2)}) %collective-permute-start.24) | collective-permute-done | bytes 262176 | tf_op jit(solution)/shard_map/ppermute | solution.py:470
  146.9 2.9 collective-permute-start.26
  149.8 4.6 %collective-permute-done.25.got_up = bf16[2,2,4,64,128]{4,3,2,1,0:T(8,128)(2,1)S(1)} collective-permute-done((bf16[2,2,4,64,128]{4,3,2,1,0:T(8,128)(2,1)S(1)}, bf16[2,2,4,64,128]{4,3,2,1,0:T(8,128)(2,1)S(1)}, u32[]{:S(2)}, u32[]{:S(2)}) %collective-permute-start.25) | collective-permute-done | bytes 262176 | tf_op jit(solution)/shard_map/ppermute | solution.py:469
  154.7 2.7 collective-permute-start.28
  157.3 2.4 sum_y.4
  159.8 3.9 %all-to-all-start.3 = ((bf16[8,288,128]{2,1,0:T(8,128)(2,1)}), bf16[8,288,128]{2,1,0:T(8,128)(2,1)S(1)}, u32[]{:S(2)}, u32[]{:S(2)}) async-start(bf16[8,288,128]{2,1,0:T(8,128)(2,1)} %sum_y.4), calls=%async_computation.3 | async-start | bytes 1179648 | tf_op jit(solution)/shard_map/all_to_all | solution.py:536
  163.9 2.7 collective-permute-start.30
  167.4 2.1 factors.3.refs_5_
  169.7 8.7 %all-to-all-done.3.from_z = bf16[8,288,128]{2,1,0:T(8,128)(2,1)S(1)} async-done(((bf16[8,288,128]{2,1,0:T(8,128)(2,1)}), bf16[8,288,128]{2,1,0:T(8,128)(2,1)S(1)}, u32[]{:S(2)}, u32[]{:S(2)}) %all-to-all-start.3) | async-done | bytes 589856 | tf_op jit(solution)/shard_map/all_to_all | solution.py:536
  180.2 3.0 %collective-permute-start.33 = (bf16[4,128,128]{2,1,0:T(8,128)(2,1)S(1)}, bf16[4,128,128]{2,1,0:T(8,128)(2,1)S(1)}, u32[]{:S(2)}, u32[]{:S(2)}) collective-permute-start(bf16[4,128,128]{2,1,0:T(8,128)(2,1)S(1)} %get-tuple-element.129.s0.refs_1_), channel_id=1, source_target_pairs={{0,2},{1,3},{2,0},{3,1},{4,6},{5,7},{6,4},{7,5},{8,10},{9,11},{10,... | collective-permute-start | bytes 393224 | tf_op jit(solution)/shard_map/ppermute | solution.py:602
  183.2 1.4 collective-permute-done.32.s1
  184.6 2.3 collective-permute-done.33.s2
  187.3 6.9 %collective-permute-start.35 = (bf16[4,128,128]{2,1,0:T(8,128)(2,1)S(1)}, bf16[4,128,128]{2,1,0:T(8,128)(2,1)S(1)}, u32[]{:S(2)}, u32[]{:S(2)}) collective-permute-start(bf16[4,128,128]{2,1,0:T(8,128)(2,1)S(1)} %upstream.5.own_ref), channel_id=1, source_target_pairs={{0,4},{4,0},{8,12},{12,8},{16,20},{20,16},{24,28},{28,24},{32,36},... | collective-permute-start | bytes 393224 | tf_op jit(solution)/shard_map/ppermute | solution.py:607
  194.2 2.1 weight_part.5.weight_ref
  197.0 8.5 %messages.5 = (bf16[4,8,288,128]{3,2,1,0:T(8,128)(2,1)}, bf16[2,2,4,64,128]{4,3,2,1,0:T(8,128)(2,1)}, bf16[2,2,4,64,128]{4,3,2,1,0:T(8,128)(2,1)}, bf16[2,2,4,64...) custom-call(s32[1324]{0:T(1024)} %concatenate.102.table, ...), custom_call_target="tpu_custom_call" | custom-call | bytes 19800000 | tf_op jit(solution)/shard_map/messages/pallas_call | solution.py:297
  205.6 4.6 %all-to-all-start.4 = ((bf16[4,8,288,128]{3,2,1,0:T(8,128)(2,1)}), bf16[4,8,288,128]{3,2,1,0:T(8,128)(2,1)}, u32[]{:S(2)}, u32[]{:S(2)}) async-start(bf16[4,8,288,128]{3,2,1,0:T(8,128)(2,1)} %get-tuple-element.144), calls=%async_computation.4 | async-start | bytes 4718592 | tf_op jit(solution)/shard_map/all_to_all | solution.py:527
  210.9 2.3 collective-permute-start.37
  213.2 6.4 %collective-permute-done.36.got_up = bf16[2,2,4,64,128]{4,3,2,1,0:T(8,128)(2,1)S(1)} collective-permute-done((bf16[2,2,4,64,128]{4,3,2,1,0:T(8,128)(2,1)S(1)}, bf16[2,2,4,64,128]{4,3,2,1,0:T(8,128)(2,1)S(1)}, u32[]{:S(2)}, u32[]{:S(2)}) %collective-permute-start.36) | collective-permute-done | bytes 262176 | tf_op jit(solution)/shard_map/ppermute | solution.py:469
  219.9 2.6 collective-permute-start.39
  222.6 5.8 %collective-permute-done.38.got_up = bf16[2,2,4,64,128]{4,3,2,1,0:T(8,128)(2,1)S(1)} collective-permute-done((bf16[2,2,4,64,128]{4,3,2,1,0:T(8,128)(2,1)S(1)}, bf16[2,2,4,64,128]{4,3,2,1,0:T(8,128)(2,1)S(1)}, u32[]{:S(2)}, u32[]{:S(2)}) %collective-permute-start.38) | collective-permute-done | bytes 262176 | tf_op jit(solution)/shard_map/ppermute | solution.py:469
  228.7 2.7 collective-permute-start.41
  231.4 5.0 %collective-permute-done.40.got_up = bf16[2,2,4,64,128]{4,3,2,1,0:T(8,128)(2,1)S(1)} collective-permute-done((bf16[2,2,4,64,128]{4,3,2,1,0:T(8,128)(2,1)S(1)}, bf16[2,2,4,64,128]{4,3,2,1,0:T(8,128)(2,1)S(1)}, u32[]{:S(2)}, u32[]{:S(2)}) %collective-permute-start.40) | collective-permute-done | bytes 262176 | tf_op jit(solution)/shard_map/ppermute | solution.py:469
  236.7 2.7 collective-permute-start.43
  239.6 2.4 sum_y.5
  242.0 17.8 %all_to_all.35.from_z = bf16[8,288,128]{2,1,0:T(8,128)(2,1)S(1)} all-to-all(bf16[8,288,128]{2,1,0:T(8,128)(2,1)} %sum_y.5), channel_id=1, replica_groups={{0,32,64,96,128,160,192,224},{4,36,68,100,132,164,196,228},{8,40,72,104..., dimensions={0} | all-to-all | bytes 1179648 | tf_op jit(solution)/shard_map/all_to_all | solution.py:536
  259.9 5.7 %collective-permute-start.47 = (f32[48,128]{1,0:T(8,128)S(1)}, f32[48,128]{1,0:T(8,128)S(1)}, u32[]{:S(2)}, u32[]{:S(2)}) collective-permute-start(f32[48,128]{1,0:T(8,128)S(1)} %pad_maximum_fusion.a_ref), channel_id=1, source_target_pairs={{0,4},{4,0},{8,12},{12,8},{16,20},{20,16},{24,28},{28,24},{32,36},... | collective-permute-start | bytes 73736 | tf_op jit(solution)/shard_map/ppermute | solution.py:199
  267.1 1.5 spread.1
  268.6 3.9 %all-to-all-start.6 = ((bf16[32,48,128]{2,1,0:T(8,128)(2,1)}), bf16[32,48,128]{2,1,0:T(8,128)(2,1)S(1)}, u32[]{:S(2)}, u32[]{:S(2)}) async-start(bf16[32,48,128]{2,1,0:T(8,128)(2,1)} %spread.1), calls=%async_computation.6 | async-start | bytes 786432 | tf_op jit(solution)/shard_map/all_to_all | solution.py:214
  273.7 2.4 collective-permute-start.45
  277.8 2.7 collective-permute-done.45.refs_2_
  280.5 1.4 collective-permute-done.46.refs_3_
  282.8 4.1 %all-to-all-done.6 = bf16[32,48,128]{2,1,0:T(8,128)(2,1)S(1)} async-done(((bf16[32,48,128]{2,1,0:T(8,128)(2,1)}), bf16[32,48,128]{2,1,0:T(8,128)(2,1)S(1)}, u32[]{:S(2)}, u32[]{:S(2)}) %all-to-all-start.6) | async-done | bytes 393248 | tf_op jit(solution)/shard_map/all_to_all | solution.py:214
  (185 shorter events, 27.2 us)
Async XLA Ops:
  0.7 19.6 %collective-permute-start.5 = (bf16[128,128,128]{2,1,0:T(8,128)(2,1)}, bf16[128,128,128]{2,1,0:T(8,128)(2,1)}, u32[]{:S(2)}, u32[]{:S(2)}) collective-permute-start(bf16[128,128,128]{2,1,0:T(8,128)(2,1)} %a_own.5), channel_id=1, source_target_pairs={{0,4},{4,0},{8,12},{12,8},{16,20},{20,16},{24,28},{28,24},{32,36},... | collective-permute-start | bytes 12582920 | tf_op jit(solution)/shard_map/ppermute | solution.py:591
  6.2 10.9 %collective-permute-start.1 = (bf16[4,128,128]{2,1,0:T(8,128)(2,1)}, bf16[4,128,128]{2,1,0:T(8,128)(2,1)S(1)}, u32[]{:S(2)}, u32[]{:S(2)}) collective-permute-start(bf16[4,128,128]{2,1,0:T(8,128)(2,1)} %get-tuple-element.79.s0.refs_1_), channel_id=1, source_target_pairs={{0,1},{1,2},{2,3},{3,0},{4,5},{5,6},{6,7},{7,4},{8,9},{9,10},{10,1... | collective-permute-start | bytes 393224 | tf_op jit(solution)/shard_map/ppermute | solution.py:602
  6.2 10.9 %collective-permute-start.2 = (bf16[4,128,128]{2,1,0:T(8,128)(2,1)}, bf16[4,128,128]{2,1,0:T(8,128)(2,1)S(1)}, u32[]{:S(2)}, u32[]{:S(2)}) collective-permute-start(bf16[4,128,128]{2,1,0:T(8,128)(2,1)} %get-tuple-element.79.s0.refs_1_), channel_id=1, source_target_pairs={{0,2},{1,3},{2,0},{3,1},{4,6},{5,7},{6,4},{7,5},{8,10},{9,11},{10,... | collective-permute-start | bytes 393224 | tf_op jit(solution)/shard_map/ppermute | solution.py:602
  8.1 9.0 %collective-permute-start.3 = (bf16[4,128,128]{2,1,0:T(8,128)(2,1)}, bf16[4,128,128]{2,1,0:T(8,128)(2,1)S(1)}, u32[]{:S(2)}, u32[]{:S(2)}) collective-permute-start(bf16[4,128,128]{2,1,0:T(8,128)(2,1)} %get-tuple-element.79.s0.refs_1_), channel_id=1, source_target_pairs={{0,3},{1,0},{2,1},{3,2},{4,7},{5,4},{6,5},{7,6},{8,11},{9,8},{10,9... | collective-permute-start | bytes 393224 | tf_op jit(solution)/shard_map/ppermute | solution.py:602
  11.2 4.1 %collective-permute-start = (s32[2,128]{1,0:T(2,128)S(1)}, s32[2,128]{1,0:T(2,128)S(1)}, u32[]{:S(2)}, u32[]{:S(2)}) collective-permute-start(s32[2,128]{1,0:T(2,128)S(1)} %pad_add_fusion), channel_id=1, source_target_pairs={{0,4},{4,0},{8,12},{12,8},{16,20},{20,16},{24,28},{28,24},{32,36},... | collective-permute-start | bytes 3080 | tf_op jit(solution)/shard_map/ppermute | solution.py:545
  17.4 2.8 collective-permute-start.4
  29.5 25.4 %copy-start.18 = (bf16[2,2,4,64,128]{4,3,2,1,0:T(8,128)(2,1)S(1)}, bf16[2,2,4,64,128]{4,3,2,1,0:T(8,128)(2,1)}, u32[]{:S(2)}) copy-start(bf16[2,2,4,64,128]{4,3,2,1,0:T(8,128)(2,1)} %get-tuple-element.82.q_up) | copy-start | bytes 786436
  29.5 25.4 %copy-start.19 = (bf16[2,2,4,64,128]{4,3,2,1,0:T(8,128)(2,1)S(1)}, bf16[2,2,4,64,128]{4,3,2,1,0:T(8,128)(2,1)}, u32[]{:S(2)}) copy-start(bf16[2,2,4,64,128]{4,3,2,1,0:T(8,128)(2,1)} %get-tuple-element.83.q_down) | copy-start | bytes 786436
  29.6 33.1 %copy-start.12 = (bf16[2,2,4,64,128]{4,3,2,1,0:T(8,128)(2,1)S(1)}, bf16[2,2,4,64,128]{4,3,2,1,0:T(8,128)(2,1)}, u32[]{:S(2)}) copy-start(bf16[2,2,4,64,128]{4,3,2,1,0:T(8,128)(2,1)} %get-tuple-element.81.q_down) | copy-start | bytes 786436
  29.6 33.1 %copy-start.13 = (bf16[2,2,4,64,128]{4,3,2,1,0:T(8,128)(2,1)S(1)}, bf16[2,2,4,64,128]{4,3,2,1,0:T(8,128)(2,1)}, u32[]{:S(2)}) copy-start(bf16[2,2,4,64,128]{4,3,2,1,0:T(8,128)(2,1)} %get-tuple-element.80.q_up) | copy-start | bytes 786436
  29.6 36.1 %all-to-all-start = ((bf16[4,8,288,128]{3,2,1,0:T(8,128)(2,1)}), bf16[4,8,288,128]{3,2,1,0:T(8,128)(2,1)}, u32[]{:S(2)}, u32[]{:S(2)}) async-start(bf16[4,8,288,128]{3,2,1,0:T(8,128)(2,1)} %get-tuple-element.94), calls=%async_computation | async-start | bytes 4718592 | tf_op jit(solution)/shard_map/all_to_all | solution.py:527
  34.3 12.0 %collective-permute-start.6 = (bf16[2,2,4,64,128]{4,3,2,1,0:T(8,128)(2,1)S(1)}, bf16[2,2,4,64,128]{4,3,2,1,0:T(8,128)(2,1)S(1)}, u32[]{:S(2)}, u32[]{:S(2)}) collective-permute-start(bf16[2,2,4,64,128]{4,3,2,1,0:T(8,128)(2,1)S(1)} %copy-done.38), channel_id=1, source_target_pairs={{0,32},{4,36},{8,40},{12,44},{16,48},{20,52},{24,56},{28,60},{32,6... | collective-permute-start | bytes 786440 | tf_op jit(solution)/shard_map/ppermute | solution.py:469
  36.2 10.1 %collective-permute-start.7 = (bf16[2,2,4,64,128]{4,3,2,1,0:T(8,128)(2,1)S(1)}, bf16[2,2,4,64,128]{4,3,2,1,0:T(8,128)(2,1)S(1)}, u32[]{:S(2)}, u32[]{:S(2)}) collective-permute-start(bf16[2,2,4,64,128]{4,3,2,1,0:T(8,128)(2,1)S(1)} %copy-done.35), channel_id=1, source_target_pairs={{0,224},{4,228},{8,232},{12,236},{16,240},{20,244},{24,248},{28,25... | collective-permute-start | bytes 786440 | tf_op jit(solution)/shard_map/ppermute | solution.py:470
  46.6 8.3 %collective-permute-start.8 = (bf16[2,2,4,64,128]{4,3,2,1,0:T(8,128)(2,1)S(1)}, bf16[2,2,4,64,128]{4,3,2,1,0:T(8,128)(2,1)S(1)}, u32[]{:S(2)}, u32[]{:S(2)}) collective-permute-start(bf16[2,2,4,64,128]{4,3,2,1,0:T(8,128)(2,1)S(1)} %get-tuple-element.88), channel_id=1, source_target_pairs={{0,32},{4,36},{8,40},{12,44},{16,48},{20,52},{24,56},{28,60},{32,6... | collective-permute-start | bytes 786440 | tf_op jit(solution)/shard_map/ppermute | solution.py:469
  46.7 8.3 %collective-permute-start.9 = (bf16[2,2,4,64,128]{4,3,2,1,0:T(8,128)(2,1)S(1)}, bf16[2,2,4,64,128]{4,3,2,1,0:T(8,128)(2,1)S(1)}, u32[]{:S(2)}, u32[]{:S(2)}) collective-permute-start(bf16[2,2,4,64,128]{4,3,2,1,0:T(8,128)(2,1)S(1)} %get-tuple-element.89), channel_id=1, source_target_pairs={{0,224},{4,228},{8,232},{12,236},{16,240},{20,244},{24,248},{28,25... | collective-permute-start | bytes 786440 | tf_op jit(solution)/shard_map/ppermute | solution.py:470
  55.2 7.5 %collective-permute-start.10 = (bf16[2,2,4,64,128]{4,3,2,1,0:T(8,128)(2,1)S(1)}, bf16[2,2,4,64,128]{4,3,2,1,0:T(8,128)(2,1)S(1)}, u32[]{:S(2)}, u32[]{:S(2)}) collective-permute-start(bf16[2,2,4,64,128]{4,3,2,1,0:T(8,128)(2,1)S(1)} %get-tuple-element.90), channel_id=1, source_target_pairs={{0,32},{4,36},{8,40},{12,44},{16,48},{20,52},{24,56},{28,60},{32,6... | collective-permute-start | bytes 786440 | tf_op jit(solution)/shard_map/ppermute | solution.py:469
  56.7 6.0 %collective-permute-start.11 = (bf16[2,2,4,64,128]{4,3,2,1,0:T(8,128)(2,1)S(1)}, bf16[2,2,4,64,128]{4,3,2,1,0:T(8,128)(2,1)S(1)}, u32[]{:S(2)}, u32[]{:S(2)}) collective-permute-start(bf16[2,2,4,64,128]{4,3,2,1,0:T(8,128)(2,1)S(1)} %get-tuple-element.91), channel_id=1, source_target_pairs={{0,224},{4,228},{8,232},{12,236},{16,240},{20,244},{24,248},{28,25... | collective-permute-start | bytes 786440 | tf_op jit(solution)/shard_map/ppermute | solution.py:470
  62.9 5.2 %collective-permute-start.12 = (bf16[2,4,64,128]{3,2,1,0:T(8,128)(2,1)S(1)}, bf16[2,4,64,128]{3,2,1,0:T(8,128)(2,1)S(1)}, u32[]{:S(2)}, u32[]{:S(2)}) collective-permute-start(bf16[2,4,64,128]{3,2,1,0:T(8,128)(2,1)S(1)} %get-tuple-element.92), channel_id=1, source_target_pairs={{0,32},{4,36},{8,40},{12,44},{16,48},{20,52},{24,56},{28,60},{32,6... | collective-permute-start | bytes 393224 | tf_op jit(solution)/shard_map/ppermute | solution.py:474
  64.6 3.8 %collective-permute-start.13 = (bf16[2,4,64,128]{3,2,1,0:T(8,128)(2,1)S(1)}, bf16[2,4,64,128]{3,2,1,0:T(8,128)(2,1)S(1)}, u32[]{:S(2)}, u32[]{:S(2)}) collective-permute-start(bf16[2,4,64,128]{3,2,1,0:T(8,128)(2,1)S(1)} %get-tuple-element.93), channel_id=1, source_target_pairs={{0,224},{4,228},{8,232},{12,236},{16,240},{20,244},{24,248},{28,25... | collective-permute-start | bytes 393224 | tf_op jit(solution)/shard_map/ppermute | solution.py:475
  68.4 22.2 %all-to-all-start.1 = ((bf16[8,288,128]{2,1,0:T(8,128)(2,1)}), bf16[8,288,128]{2,1,0:T(8,128)(2,1)S(1)}, u32[]{:S(2)}, u32[]{:S(2)}) async-start(bf16[8,288,128]{2,1,0:T(8,128)(2,1)} %sum_y.3), calls=%async_computation.1 | async-start | bytes 1179648 | tf_op jit(solution)/shard_map/all_to_all | solution.py:536
  74.5 5.9 %collective-permute-start.14 = (bf16[4,64,128]{2,1,0:T(8,128)(2,1)S(1)}, bf16[4,64,128]{2,1,0:T(8,128)(2,1)S(1)}, u32[]{:S(2)}, u32[]{:S(2)}) collective-permute-start(bf16[4,64,128]{2,1,0:T(8,128)(2,1)S(1)} %get-tuple-element.100), channel_id=1, source_target_pairs={{0,8},{4,12},{8,16},{12,20},{16,24},{20,28},{24,0},{28,4},{32,40},... | collective-permute-start | bytes 196616 | tf_op jit(solution)/shard_map/ppermute | solution.py:537
  74.6 5.8 %collective-permute-start.15 = (bf16[4,64,128]{2,1,0:T(8,128)(2,1)S(1)}, bf16[4,64,128]{2,1,0:T(8,128)(2,1)S(1)}, u32[]{:S(2)}, u32[]{:S(2)}) collective-permute-start(bf16[4,64,128]{2,1,0:T(8,128)(2,1)S(1)} %get-tuple-element.101), channel_id=1, source_target_pairs={{0,16},{4,20},{8,24},{12,28},{16,0},{20,4},{24,8},{28,12},{32,48},... | collective-permute-start | bytes 196616 | tf_op jit(solution)/shard_map/ppermute | solution.py:537
  76.6 3.8 %collective-permute-start.16 = (bf16[4,64,128]{2,1,0:T(8,128)(2,1)S(1)}, bf16[4,64,128]{2,1,0:T(8,128)(2,1)S(1)}, u32[]{:S(2)}, u32[]{:S(2)}) collective-permute-start(bf16[4,64,128]{2,1,0:T(8,128)(2,1)S(1)} %get-tuple-element.102), channel_id=1, source_target_pairs={{0,24},{4,28},{8,0},{12,4},{16,8},{20,12},{24,16},{28,20},{32,56},... | collective-permute-start | bytes 196616 | tf_op jit(solution)/shard_map/ppermute | solution.py:537
  91.6 6.5 %collective-permute-start.17 = (bf16[4,128,128]{2,1,0:T(8,128)(2,1)S(1)}, bf16[4,128,128]{2,1,0:T(8,128)(2,1)S(1)}, u32[]{:S(2)}, u32[]{:S(2)}) collective-permute-start(bf16[4,128,128]{2,1,0:T(8,128)(2,1)S(1)} %get-tuple-element.104.s0.refs_1_), channel_id=1, source_target_pairs={{0,1},{1,2},{2,3},{3,0},{4,5},{5,6},{6,7},{7,4},{8,9},{9,10},{10,1... | collective-permute-start | bytes 393224 | tf_op jit(solution)/shard_map/ppermute | solution.py:602
  92.0 6.1 %collective-permute-start.18 = (bf16[4,128,128]{2,1,0:T(8,128)(2,1)S(1)}, bf16[4,128,128]{2,1,0:T(8,128)(2,1)S(1)}, u32[]{:S(2)}, u32[]{:S(2)}) collective-permute-start(bf16[4,128,128]{2,1,0:T(8,128)(2,1)S(1)} %get-tuple-element.104.s0.refs_1_), channel_id=1, source_target_pairs={{0,2},{1,3},{2,0},{3,1},{4,6},{5,7},{6,4},{7,5},{8,10},{9,11},{10,... | collective-permute-start | bytes 393224 | tf_op jit(solution)/shard_map/ppermute | solution.py:602
  93.8 4.9 %collective-permute-start.19 = (bf16[4,128,128]{2,1,0:T(8,128)(2,1)S(1)}, bf16[4,128,128]{2,1,0:T(8,128)(2,1)S(1)}, u32[]{:S(2)}, u32[]{:S(2)}) collective-permute-start(bf16[4,128,128]{2,1,0:T(8,128)(2,1)S(1)} %get-tuple-element.104.s0.refs_1_), channel_id=1, source_target_pairs={{0,3},{1,0},{2,1},{3,2},{4,7},{5,4},{6,5},{7,6},{8,11},{9,8},{10,9... | collective-permute-start | bytes 393224 | tf_op jit(solution)/shard_map/ppermute | solution.py:602
  99.0 7.3 %collective-permute-start.20 = (bf16[4,128,128]{2,1,0:T(8,128)(2,1)S(1)}, bf16[4,128,128]{2,1,0:T(8,128)(2,1)S(1)}, u32[]{:S(2)}, u32[]{:S(2)}) collective-permute-start(bf16[4,128,128]{2,1,0:T(8,128)(2,1)S(1)} %upstream.4.own_ref), channel_id=1, source_target_pairs={{0,4},{4,0},{8,12},{12,8},{16,20},{20,16},{24,28},{28,24},{32,36},... | collective-permute-start | bytes 393224 | tf_op jit(solution)/shard_map/ppermute | solution.py:607
  115.6 30.7 %copy-start.20 = (bf16[2,2,4,64,128]{4,3,2,1,0:T(8,128)(2,1)S(1)}, bf16[2,2,4,64,128]{4,3,2,1,0:T(8,128)(2,1)}, u32[]{:S(2)}) copy-start(bf16[2,2,4,64,128]{4,3,2,1,0:T(8,128)(2,1)} %get-tuple-element.107.q_up) | copy-start | bytes 786436
  115.6 30.7 %copy-start.21 = (bf16[2,2,4,64,128]{4,3,2,1,0:T(8,128)(2,1)S(1)}, bf16[2,2,4,64,128]{4,3,2,1,0:T(8,128)(2,1)}, u32[]{:S(2)}) copy-start(bf16[2,2,4,64,128]{4,3,2,1,0:T(8,128)(2,1)} %get-tuple-element.108.q_down) | copy-start | bytes 786436
  115.6 38.7 %copy-start.14 = (bf16[2,2,4,64,128]{4,3,2,1,0:T(8,128)(2,1)S(1)}, bf16[2,2,4,64,128]{4,3,2,1,0:T(8,128)(2,1)}, u32[]{:S(2)}) copy-start(bf16[2,2,4,64,128]{4,3,2,1,0:T(8,128)(2,1)} %get-tuple-element.106.q_down) | copy-start | bytes 786436
  115.7 38.7 %copy-start.15 = (bf16[2,2,4,64,128]{4,3,2,1,0:T(8,128)(2,1)S(1)}, bf16[2,2,4,64,128]{4,3,2,1,0:T(8,128)(2,1)}, u32[]{:S(2)}) copy-start(bf16[2,2,4,64,128]{4,3,2,1,0:T(8,128)(2,1)} %get-tuple-element.105.q_up) | copy-start | bytes 786436
  115.7 41.7 %all-to-all-start.2 = ((bf16[4,8,288,128]{3,2,1,0:T(8,128)(2,1)}), bf16[4,8,288,128]{3,2,1,0:T(8,128)(2,1)}, u32[]{:S(2)}, u32[]{:S(2)}) async-start(bf16[4,8,288,128]{3,2,1,0:T(8,128)(2,1)} %get-tuple-element.119), calls=%async_computation.2 | async-start | bytes 4718592 | tf_op jit(solution)/shard_map/all_to_all | solution.py:527
  120.4 9.3 %collective-permute-start.21 = (bf16[2,2,4,64,128]{4,3,2,1,0:T(8,128)(2,1)S(1)}, bf16[2,2,4,64,128]{4,3,2,1,0:T(8,128)(2,1)S(1)}, u32[]{:S(2)}, u32[]{:S(2)}) collective-permute-start(bf16[2,2,4,64,128]{4,3,2,1,0:T(8,128)(2,1)S(1)} %copy-done.39), channel_id=1, source_target_pairs={{0,32},{4,36},{8,40},{12,44},{16,48},{20,52},{24,56},{28,60},{32,6... | collective-permute-start | bytes 786440 | tf_op jit(solution)/shard_map/ppermute | solution.py:469
  121.0 8.7 %collective-permute-start.22 = (bf16[2,2,4,64,128]{4,3,2,1,0:T(8,128)(2,1)S(1)}, bf16[2,2,4,64,128]{4,3,2,1,0:T(8,128)(2,1)S(1)}, u32[]{:S(2)}, u32[]{:S(2)}) collective-permute-start(bf16[2,2,4,64,128]{4,3,2,1,0:T(8,128)(2,1)S(1)} %copy-done.36), channel_id=1, source_target_pairs={{0,224},{4,228},{8,232},{12,236},{16,240},{20,244},{24,248},{28,25... | collective-permute-start | bytes 786440 | tf_op jit(solution)/shard_map/ppermute | solution.py:470
  129.9 11.5 %collective-permute-start.23 = (bf16[2,2,4,64,128]{4,3,2,1,0:T(8,128)(2,1)S(1)}, bf16[2,2,4,64,128]{4,3,2,1,0:T(8,128)(2,1)S(1)}, u32[]{:S(2)}, u32[]{:S(2)}) collective-permute-start(bf16[2,2,4,64,128]{4,3,2,1,0:T(8,128)(2,1)S(1)} %get-tuple-element.113), channel_id=1, source_target_pairs={{0,32},{4,36},{8,40},{12,44},{16,48},{20,52},{24,56},{28,60},{32,6... | collective-permute-start | bytes 786440 | tf_op jit(solution)/shard_map/ppermute | solution.py:469
  130.0 16.3 %collective-permute-start.24 = (bf16[2,2,4,64,128]{4,3,2,1,0:T(8,128)(2,1)S(1)}, bf16[2,2,4,64,128]{4,3,2,1,0:T(8,128)(2,1)S(1)}, u32[]{:S(2)}, u32[]{:S(2)}) collective-permute-start(bf16[2,2,4,64,128]{4,3,2,1,0:T(8,128)(2,1)S(1)} %get-tuple-element.114), channel_id=1, source_target_pairs={{0,224},{4,228},{8,232},{12,236},{16,240},{20,244},{24,248},{28,25... | collective-permute-start | bytes 786440 | tf_op jit(solution)/shard_map/ppermute | solution.py:470
  146.5 7.8 %collective-permute-start.25 = (bf16[2,2,4,64,128]{4,3,2,1,0:T(8,128)(2,1)S(1)}, bf16[2,2,4,64,128]{4,3,2,1,0:T(8,128)(2,1)S(1)}, u32[]{:S(2)}, u32[]{:S(2)}) collective-permute-start(bf16[2,2,4,64,128]{4,3,2,1,0:T(8,128)(2,1)S(1)} %get-tuple-element.115), channel_id=1, source_target_pairs={{0,32},{4,36},{8,40},{12,44},{16,48},{20,52},{24,56},{28,60},{32,6... | collective-permute-start | bytes 786440 | tf_op jit(solution)/shard_map/ppermute | solution.py:469
  146.9 7.4 %collective-permute-start.26 = (bf16[2,2,4,64,128]{4,3,2,1,0:T(8,128)(2,1)S(1)}, bf16[2,2,4,64,128]{4,3,2,1,0:T(8,128)(2,1)S(1)}, u32[]{:S(2)}, u32[]{:S(2)}) collective-permute-start(bf16[2,2,4,64,128]{4,3,2,1,0:T(8,128)(2,1)S(1)} %get-tuple-element.116), channel_id=1, source_target_pairs={{0,224},{4,228},{8,232},{12,236},{16,240},{20,244},{24,248},{28,25... | collective-permute-start | bytes 786440 | tf_op jit(solution)/shard_map/ppermute | solution.py:470
  154.6 5.2 %collective-permute-start.27 = (bf16[2,4,64,128]{3,2,1,0:T(8,128)(2,1)S(1)}, bf16[2,4,64,128]{3,2,1,0:T(8,128)(2,1)S(1)}, u32[]{:S(2)}, u32[]{:S(2)}) collective-permute-start(bf16[2,4,64,128]{3,2,1,0:T(8,128)(2,1)S(1)} %get-tuple-element.117), channel_id=1, source_target_pairs={{0,32},{4,36},{8,40},{12,44},{16,48},{20,52},{24,56},{28,60},{32,6... | collective-permute-start | bytes 393224 | tf_op jit(solution)/shard_map/ppermute | solution.py:474
  154.7 5.1 %collective-permute-start.28 = (bf16[2,4,64,128]{3,2,1,0:T(8,128)(2,1)S(1)}, bf16[2,4,64,128]{3,2,1,0:T(8,128)(2,1)S(1)}, u32[]{:S(2)}, u32[]{:S(2)}) collective-permute-start(bf16[2,4,64,128]{3,2,1,0:T(8,128)(2,1)S(1)} %get-tuple-element.118), channel_id=1, source_target_pairs={{0,224},{4,228},{8,232},{12,236},{16,240},{20,244},{24,248},{28,25... | collective-permute-start | bytes 393224 | tf_op jit(solution)/shard_map/ppermute | solution.py:475
  159.8 18.6 %all-to-all-start.3 = ((bf16[8,288,128]{2,1,0:T(8,128)(2,1)}), bf16[8,288,128]{2,1,0:T(8,128)(2,1)S(1)}, u32[]{:S(2)}, u32[]{:S(2)}) async-start(bf16[8,288,128]{2,1,0:T(8,128)(2,1)} %sum_y.4), calls=%async_computation.3 | async-start | bytes 1179648 | tf_op jit(solution)/shard_map/all_to_all | solution.py:536
  163.7 5.9 %collective-permute-start.29 = (bf16[4,64,128]{2,1,0:T(8,128)(2,1)S(1)}, bf16[4,64,128]{2,1,0:T(8,128)(2,1)S(1)}, u32[]{:S(2)}, u32[]{:S(2)}) collective-permute-start(bf16[4,64,128]{2,1,0:T(8,128)(2,1)S(1)} %get-tuple-element.125), channel_id=1, source_target_pairs={{0,8},{4,12},{8,16},{12,20},{16,24},{20,28},{24,0},{28,4},{32,40},... | collective-permute-start | bytes 196616 | tf_op jit(solution)/shard_map/ppermute | solution.py:537
  163.9 5.7 %collective-permute-start.30 = (bf16[4,64,128]{2,1,0:T(8,128)(2,1)S(1)}, bf16[4,64,128]{2,1,0:T(8,128)(2,1)S(1)}, u32[]{:S(2)}, u32[]{:S(2)}) collective-permute-start(bf16[4,64,128]{2,1,0:T(8,128)(2,1)S(1)} %get-tuple-element.126), channel_id=1, source_target_pairs={{0,16},{4,20},{8,24},{12,28},{16,0},{20,4},{24,8},{28,12},{32,48},... | collective-permute-start | bytes 196616 | tf_op jit(solution)/shard_map/ppermute | solution.py:537
  166.6 3.1 %collective-permute-start.31 = (bf16[4,64,128]{2,1,0:T(8,128)(2,1)S(1)}, bf16[4,64,128]{2,1,0:T(8,128)(2,1)S(1)}, u32[]{:S(2)}, u32[]{:S(2)}) collective-permute-start(bf16[4,64,128]{2,1,0:T(8,128)(2,1)S(1)} %get-tuple-element.127), channel_id=1, source_target_pairs={{0,24},{4,28},{8,0},{12,4},{16,8},{20,12},{24,16},{28,20},{32,56},... | collective-permute-start | bytes 196616 | tf_op jit(solution)/shard_map/ppermute | solution.py:537
  179.5 5.1 %collective-permute-start.32 = (bf16[4,128,128]{2,1,0:T(8,128)(2,1)S(1)}, bf16[4,128,128]{2,1,0:T(8,128)(2,1)S(1)}, u32[]{:S(2)}, u32[]{:S(2)}) collective-permute-start(bf16[4,128,128]{2,1,0:T(8,128)(2,1)S(1)} %get-tuple-element.129.s0.refs_1_), channel_id=1, source_target_pairs={{0,1},{1,2},{2,3},{3,0},{4,5},{5,6},{6,7},{7,4},{8,9},{9,10},{10,1... | collective-permute-start | bytes 393224 | tf_op jit(solution)/shard_map/ppermute | solution.py:602
  180.2 6.7 %collective-permute-start.33 = (bf16[4,128,128]{2,1,0:T(8,128)(2,1)S(1)}, bf16[4,128,128]{2,1,0:T(8,128)(2,1)S(1)}, u32[]{:S(2)}, u32[]{:S(2)}) collective-permute-start(bf16[4,128,128]{2,1,0:T(8,128)(2,1)S(1)} %get-tuple-element.129.s0.refs_1_), channel_id=1, source_target_pairs={{0,2},{1,3},{2,0},{3,1},{4,6},{5,7},{6,4},{7,5},{8,10},{9,11},{10,... | collective-permute-start | bytes 393224 | tf_op jit(solution)/shard_map/ppermute | solution.py:602
  183.2 3.8 %collective-permute-start.34 = (bf16[4,128,128]{2,1,0:T(8,128)(2,1)S(1)}, bf16[4,128,128]{2,1,0:T(8,128)(2,1)S(1)}, u32[]{:S(2)}, u32[]{:S(2)}) collective-permute-start(bf16[4,128,128]{2,1,0:T(8,128)(2,1)S(1)} %get-tuple-element.129.s0.refs_1_), channel_id=1, source_target_pairs={{0,3},{1,0},{2,1},{3,2},{4,7},{5,4},{6,5},{7,6},{8,11},{9,8},{10,9... | collective-permute-start | bytes 393224 | tf_op jit(solution)/shard_map/ppermute | solution.py:602
  187.3 9.0 %collective-permute-start.35 = (bf16[4,128,128]{2,1,0:T(8,128)(2,1)S(1)}, bf16[4,128,128]{2,1,0:T(8,128)(2,1)S(1)}, u32[]{:S(2)}, u32[]{:S(2)}) collective-permute-start(bf16[4,128,128]{2,1,0:T(8,128)(2,1)S(1)} %upstream.5.own_ref), channel_id=1, source_target_pairs={{0,4},{4,0},{8,12},{12,8},{16,20},{20,16},{24,28},{28,24},{32,36},... | collective-permute-start | bytes 393224 | tf_op jit(solution)/shard_map/ppermute | solution.py:607
  205.6 30.8 %copy-start.10 = (bf16[2,2,4,64,128]{4,3,2,1,0:T(8,128)(2,1)S(1)}, bf16[2,2,4,64,128]{4,3,2,1,0:T(8,128)(2,1)}, u32[]{:S(2)}) copy-start(bf16[2,2,4,64,128]{4,3,2,1,0:T(8,128)(2,1)} %get-tuple-element.131.q_down) | copy-start | bytes 786436
  205.6 30.8 %copy-start.11 = (bf16[2,2,4,64,128]{4,3,2,1,0:T(8,128)(2,1)S(1)}, bf16[2,2,4,64,128]{4,3,2,1,0:T(8,128)(2,1)}, u32[]{:S(2)}) copy-start(bf16[2,2,4,64,128]{4,3,2,1,0:T(8,128)(2,1)} %get-tuple-element.130.q_up) | copy-start | bytes 786436
  205.6 34.0 %all-to-all-start.4 = ((bf16[4,8,288,128]{3,2,1,0:T(8,128)(2,1)}), bf16[4,8,288,128]{3,2,1,0:T(8,128)(2,1)}, u32[]{:S(2)}, u32[]{:S(2)}) async-start(bf16[4,8,288,128]{3,2,1,0:T(8,128)(2,1)} %get-tuple-element.144), calls=%async_computation.4 | async-start | bytes 4718592 | tf_op jit(solution)/shard_map/all_to_all | solution.py:527
  210.3 9.3 %collective-permute-start.36 = (bf16[2,2,4,64,128]{4,3,2,1,0:T(8,128)(2,1)S(1)}, bf16[2,2,4,64,128]{4,3,2,1,0:T(8,128)(2,1)S(1)}, u32[]{:S(2)}, u32[]{:S(2)}) collective-permute-start(bf16[2,2,4,64,128]{4,3,2,1,0:T(8,128)(2,1)S(1)} %copy-done.37), channel_id=1, source_target_pairs={{0,32},{4,36},{8,40},{12,44},{16,48},{20,52},{24,56},{28,60},{32,6... | collective-permute-start | bytes 786440 | tf_op jit(solution)/shard_map/ppermute | solution.py:469
  210.9 8.7 %collective-permute-start.37 = (bf16[2,2,4,64,128]{4,3,2,1,0:T(8,128)(2,1)S(1)}, bf16[2,2,4,64,128]{4,3,2,1,0:T(8,128)(2,1)S(1)}, u32[]{:S(2)}, u32[]{:S(2)}) collective-permute-start(bf16[2,2,4,64,128]{4,3,2,1,0:T(8,128)(2,1)S(1)} %copy-done.34), channel_id=1, source_target_pairs={{0,224},{4,228},{8,232},{12,236},{16,240},{20,244},{24,248},{28,25... | collective-permute-start | bytes 786440 | tf_op jit(solution)/shard_map/ppermute | solution.py:470
  219.8 8.5 %collective-permute-start.38 = (bf16[2,2,4,64,128]{4,3,2,1,0:T(8,128)(2,1)S(1)}, bf16[2,2,4,64,128]{4,3,2,1,0:T(8,128)(2,1)S(1)}, u32[]{:S(2)}, u32[]{:S(2)}) collective-permute-start(bf16[2,2,4,64,128]{4,3,2,1,0:T(8,128)(2,1)S(1)} %get-tuple-element.138), channel_id=1, source_target_pairs={{0,32},{4,36},{8,40},{12,44},{16,48},{20,52},{24,56},{28,60},{32,6... | collective-permute-start | bytes 786440 | tf_op jit(solution)/shard_map/ppermute | solution.py:469
  219.9 8.4 %collective-permute-start.39 = (bf16[2,2,4,64,128]{4,3,2,1,0:T(8,128)(2,1)S(1)}, bf16[2,2,4,64,128]{4,3,2,1,0:T(8,128)(2,1)S(1)}, u32[]{:S(2)}, u32[]{:S(2)}) collective-permute-start(bf16[2,2,4,64,128]{4,3,2,1,0:T(8,128)(2,1)S(1)} %get-tuple-element.139), channel_id=1, source_target_pairs={{0,224},{4,228},{8,232},{12,236},{16,240},{20,244},{24,248},{28,25... | collective-permute-start | bytes 786440 | tf_op jit(solution)/shard_map/ppermute | solution.py:470
  228.6 7.7 %collective-permute-start.40 = (bf16[2,2,4,64,128]{4,3,2,1,0:T(8,128)(2,1)S(1)}, bf16[2,2,4,64,128]{4,3,2,1,0:T(8,128)(2,1)S(1)}, u32[]{:S(2)}, u32[]{:S(2)}) collective-permute-start(bf16[2,2,4,64,128]{4,3,2,1,0:T(8,128)(2,1)S(1)} %get-tuple-element.140), channel_id=1, source_target_pairs={{0,32},{4,36},{8,40},{12,44},{16,48},{20,52},{24,56},{28,60},{32,6... | collective-permute-start | bytes 786440 | tf_op jit(solution)/shard_map/ppermute | solution.py:469
  228.7 7.6 %collective-permute-start.41 = (bf16[2,2,4,64,128]{4,3,2,1,0:T(8,128)(2,1)S(1)}, bf16[2,2,4,64,128]{4,3,2,1,0:T(8,128)(2,1)S(1)}, u32[]{:S(2)}, u32[]{:S(2)}) collective-permute-start(bf16[2,2,4,64,128]{4,3,2,1,0:T(8,128)(2,1)S(1)} %get-tuple-element.141), channel_id=1, source_target_pairs={{0,224},{4,228},{8,232},{12,236},{16,240},{20,244},{24,248},{28,25... | collective-permute-start | bytes 786440 | tf_op jit(solution)/shard_map/ppermute | solution.py:470
  236.6 5.5 %collective-permute-start.42 = (bf16[2,4,64,128]{3,2,1,0:T(8,128)(2,1)S(1)}, bf16[2,4,64,128]{3,2,1,0:T(8,128)(2,1)S(1)}, u32[]{:S(2)}, u32[]{:S(2)}) collective-permute-start(bf16[2,4,64,128]{3,2,1,0:T(8,128)(2,1)S(1)} %get-tuple-element.142), channel_id=1, source_target_pairs={{0,32},{4,36},{8,40},{12,44},{16,48},{20,52},{24,56},{28,60},{32,6... | collective-permute-start | bytes 393224 | tf_op jit(solution)/shard_map/ppermute | solution.py:474
  236.7 5.4 %collective-permute-start.43 = (bf16[2,4,64,128]{3,2,1,0:T(8,128)(2,1)S(1)}, bf16[2,4,64,128]{3,2,1,0:T(8,128)(2,1)S(1)}, u32[]{:S(2)}, u32[]{:S(2)}) collective-permute-start(bf16[2,4,64,128]{3,2,1,0:T(8,128)(2,1)S(1)} %get-tuple-element.143), channel_id=1, source_target_pairs={{0,224},{4,228},{8,232},{12,236},{16,240},{20,244},{24,248},{28,25... | collective-permute-start | bytes 393224 | tf_op jit(solution)/shard_map/ppermute | solution.py:475
  259.9 6.6 %collective-permute-start.47 = (f32[48,128]{1,0:T(8,128)S(1)}, f32[48,128]{1,0:T(8,128)S(1)}, u32[]{:S(2)}, u32[]{:S(2)}) collective-permute-start(f32[48,128]{1,0:T(8,128)S(1)} %pad_maximum_fusion.a_ref), channel_id=1, source_target_pairs={{0,4},{4,0},{8,12},{12,8},{16,20},{20,16},{24,28},{28,24},{32,36},... | collective-permute-start | bytes 73736 | tf_op jit(solution)/shard_map/ppermute | solution.py:199
  268.6 18.3 %all-to-all-start.6 = ((bf16[32,48,128]{2,1,0:T(8,128)(2,1)}), bf16[32,48,128]{2,1,0:T(8,128)(2,1)S(1)}, u32[]{:S(2)}, u32[]{:S(2)}) async-start(bf16[32,48,128]{2,1,0:T(8,128)(2,1)} %spread.1), calls=%async_computation.6 | async-start | bytes 786432 | tf_op jit(solution)/shard_map/all_to_all | solution.py:214
  272.5 5.3 %collective-permute-start.44 = (bf16[4,64,128]{2,1,0:T(8,128)(2,1)S(1)}, bf16[4,64,128]{2,1,0:T(8,128)(2,1)S(1)}, u32[]{:S(2)}, u32[]{:S(2)}) collective-permute-start(bf16[4,64,128]{2,1,0:T(8,128)(2,1)S(1)} %get-tuple-element.150), channel_id=1, source_target_pairs={{0,8},{4,12},{8,16},{12,20},{16,24},{20,28},{24,0},{28,4},{32,40},... | collective-permute-start | bytes 196616 | tf_op jit(solution)/shard_map/ppermute | solution.py:537
  273.7 6.8 %collective-permute-start.45 = (bf16[4,64,128]{2,1,0:T(8,128)(2,1)S(1)}, bf16[4,64,128]{2,1,0:T(8,128)(2,1)S(1)}, u32[]{:S(2)}, u32[]{:S(2)}) collective-permute-start(bf16[4,64,128]{2,1,0:T(8,128)(2,1)S(1)} %get-tuple-element.151), channel_id=1, source_target_pairs={{0,16},{4,20},{8,24},{12,28},{16,0},{20,4},{24,8},{28,12},{32,48},... | collective-permute-start | bytes 196616 | tf_op jit(solution)/shard_map/ppermute | solution.py:537
  276.2 5.8 %collective-permute-start.46 = (bf16[4,64,128]{2,1,0:T(8,128)(2,1)S(1)}, bf16[4,64,128]{2,1,0:T(8,128)(2,1)S(1)}, u32[]{:S(2)}, u32[]{:S(2)}) collective-permute-start(bf16[4,64,128]{2,1,0:T(8,128)(2,1)S(1)} %get-tuple-element.152), channel_id=1, source_target_pairs={{0,24},{4,28},{8,0},{12,4},{16,8},{20,12},{24,16},{28,20},{32,56},... | collective-permute-start | bytes 196616 | tf_op jit(solution)/shard_map/ppermute | solution.py:537
  (31 other events, 281.1 us)

commit v2 on v1

--- a/solution.py
+++ b/solution.py
@@ -184,7 +184,7 @@
         ],
         out_specs=pl.BlockSpec(shape, lambda i: (0, 0, 0, 0)),
         compiler_params=params(60 * MB),
-        cost_estimate=cost(1),
+        cost_estimate=cost(4),
         name="weight_part",
     )(saved, slopes)
 
@@ -204,7 +204,7 @@
         grid=(1,),
         in_specs=[pl.BlockSpec(mine.shape, lambda i: (0, 0))] * 2,
         out_specs=pl.BlockSpec(shape, lambda i: (0, 0, 0)),
-        compiler_params=params(60 * MB),
+        compiler_params=params(8 * MB),
         cost_estimate=cost(0.5),
         name="spread",
     )(mine, theirs)
@@ -603,6 +603,7 @@
             for d in range(1, NX)
         ]
         weight = weight_part(saved_inputs, slopes, hop, scale)
+        pieces[-1], weight = lax.optimization_barrier((pieces[-1], weight))
         own = upstream_of(member, my_rows[hop], pieces)
         sibling = lax.ppermute(own, "dp", shift(dc=1))
         out_a, *out_b = messages_of(table, own, sibling, edge_values, edges_sib, weight)

time: 294 us -> 292 us (level)
  transfers between devices with their start and end apart: 54 -> 54, of which waited for: 24 -> 27; matrix products, arithmetic and copies ran while one was open for 2% -> 2% of each run, Pallas kernels for 8% -> 8%
where the time goes in v2:
time: 292 us; the launch traced here: 286 us
  starting transfers between devices  116 us (40%)
  waiting for transfers between devices  86.5 us (30%)
  Pallas kernels  50.6 us (17%)
  blocking collectives  17.8 us (6%)
  local copies, waits for them, and re-layouts  11.1 us (4%)
    ppermute x9, waiting for transfers between devices, ring(): got_up = lax.ppermute(up, 'dp', ahead)  43.3 us
    ppermute x9, starting transfers between devices, ring(): got_down = lax.ppermute(down, 'dp', back)  32.6 us
    pallas_call x3, Pallas kernels, messages_of(): pl.pallas_call(message_kernel, out_shape=(jax.ShapeDtypeStruct((NY, NZ, R...  25.7 us
    all_to_all x2, waiting for transfers between devices, exchange(): lax.all_to_all(made['sums'], 'dp', 0, 0, axis_index_groups=Z_GROUPS, tile...  19.1 us
    all_to_all x1, blocking collectives, exchange(): lax.all_to_all(made['sums'], 'dp', 0, 0, axis_index_groups=Z_GROUPS, tile...  17.8 us
    all_to_all x3, starting transfers between devices, exchange(): lax.all_to_all(out_a, 'dp', 0, 0, axis_index_groups=Y_GROUPS, tiled=True)  14 us
    ppermute x3, starting transfers between devices, on_device(): sibling = lax.ppermute(own, 'dp', shift(dc=1))  12.5 us
    ppermute x9, starting transfers between devices, exchange(): lax.ppermute(x, 'dp', shift(dy=d + 1))  11.3 us
  transfers between devices with their start and end apart: 54, of which 27 were waited for; matrix products, arithmetic and copies ran while one was open for 2% of the time, Pallas kernels for 8%

profile of v2, /device:TPU:1, one launch (start us, length us, event | category | flops | bytes accessed | tf_op | source)
XLA Modules:
  0.0 286.3 jit_solution(2693739382311887486)
XLA Ops:
  0.7 3.3 %collective-permute-start.5 = (bf16[128,128,128]{2,1,0:T(8,128)(2,1)}, bf16[128,128,128]{2,1,0:T(8,128)(2,1)}, u32[]{:S(2)}, u32[]{:S(2)}) collective-permute-start(bf16[128,128,128]{2,1,0:T(8,128)(2,1)} %a_own.5), channel_id=1, source_target_pairs={{0,4},{4,0},{8,12},{12,8},{16,20},{20,16},{24,28},{28,24},{32,36},... | collective-permute-start | bytes 12582920 | tf_op jit(solution)/shard_map/ppermute | solution.py:591
  4.0 2.2 first_slopes.1
  6.2 1.9 collective-permute-start.2
  8.1 1.2 collective-permute-start.3
  9.9 1.3 gather_fusion
  13.3 2.1 weight_part.3.weight_ref
  18.2 2.0 concatenate.102.table
  20.9 8.6 %messages.3 = (bf16[4,8,288,128]{3,2,1,0:T(8,128)(2,1)}, bf16[2,2,4,64,128]{4,3,2,1,0:T(8,128)(2,1)}, bf16[2,2,4,64,128]{4,3,2,1,0:T(8,128)(2,1)}, bf16[2,2,4,64...) custom-call(s32[1324]{0:T(1024)} %concatenate.102.table, ...), custom_call_target="tpu_custom_call" | custom-call | bytes 19800000 | tf_op jit(solution)/shard_map/messages/pallas_call | solution.py:297
  29.6 4.7 %all-to-all-start = ((bf16[4,8,288,128]{3,2,1,0:T(8,128)(2,1)}), bf16[4,8,288,128]{3,2,1,0:T(8,128)(2,1)}, u32[]{:S(2)}, u32[]{:S(2)}) async-start(bf16[4,8,288,128]{3,2,1,0:T(8,128)(2,1)} %get-tuple-element.102), calls=%async_computation | async-start | bytes 4718592 | tf_op jit(solution)/shard_map/all_to_all | solution.py:527
  34.3 1.7 collective-permute-start.6
  36.0 3.7 %collective-permute-start.7 = (bf16[2,2,4,64,128]{4,3,2,1,0:T(8,128)(2,1)S(1)}, bf16[2,2,4,64,128]{4,3,2,1,0:T(8,128)(2,1)S(1)}, u32[]{:S(2)}, u32[]{:S(2)}) collective-permute-start(bf16[2,2,4,64,128]{4,3,2,1,0:T(8,128)(2,1)S(1)} %copy-done.35), channel_id=1, source_target_pairs={{0,224},{4,228},{8,232},{12,236},{16,240},{20,244},{24,248},{28,25... | collective-permute-start | bytes 786440 | tf_op jit(solution)/shard_map/ppermute | solution.py:470
  39.7 5.9 %collective-permute-done.6.got_up = bf16[2,2,4,64,128]{4,3,2,1,0:T(8,128)(2,1)S(1)} collective-permute-done((bf16[2,2,4,64,128]{4,3,2,1,0:T(8,128)(2,1)S(1)}, bf16[2,2,4,64,128]{4,3,2,1,0:T(8,128)(2,1)S(1)}, u32[]{:S(2)}, u32[]{:S(2)}) %collective-permute-start.6) | collective-permute-done | bytes 262176 | tf_op jit(solution)/shard_map/ppermute | solution.py:469
  46.0 2.7 collective-permute-start.9
  48.7 5.2 %collective-permute-done.8.got_up = bf16[2,2,4,64,128]{4,3,2,1,0:T(8,128)(2,1)S(1)} collective-permute-done((bf16[2,2,4,64,128]{4,3,2,1,0:T(8,128)(2,1)S(1)}, bf16[2,2,4,64,128]{4,3,2,1,0:T(8,128)(2,1)S(1)}, u32[]{:S(2)}, u32[]{:S(2)}) %collective-permute-start.8) | collective-permute-done | bytes 262176 | tf_op jit(solution)/shard_map/ppermute | solution.py:469
  54.2 1.9 collective-permute-start.10
  57.1 4.2 %collective-permute-done.10.got_up = bf16[2,2,4,64,128]{4,3,2,1,0:T(8,128)(2,1)S(1)} collective-permute-done((bf16[2,2,4,64,128]{4,3,2,1,0:T(8,128)(2,1)S(1)}, bf16[2,2,4,64,128]{4,3,2,1,0:T(8,128)(2,1)S(1)}, u32[]{:S(2)}, u32[]{:S(2)}) %collective-permute-start.10) | collective-permute-done | bytes 262176 | tf_op jit(solution)/shard_map/ppermute | solution.py:469
  62.1 1.7 collective-permute-start.12
  64.9 2.4 sum_y.3
  67.6 6.0 %all-to-all-start.1 = ((bf16[8,288,128]{2,1,0:T(8,128)(2,1)}), bf16[8,288,128]{2,1,0:T(8,128)(2,1)S(1)}, u32[]{:S(2)}, u32[]{:S(2)}) async-start(bf16[8,288,128]{2,1,0:T(8,128)(2,1)} %sum_y.3), calls=%async_computation.1 | async-start | bytes 1179648 | tf_op jit(solution)/shard_map/all_to_all | solution.py:536
  74.0 2.1 collective-permute-start.15
  76.5 2.1 factors.2.refs_5_
  79.4 10.5 %all-to-all-done.1.from_z = bf16[8,288,128]{2,1,0:T(8,128)(2,1)S(1)} async-done(((bf16[8,288,128]{2,1,0:T(8,128)(2,1)}), bf16[8,288,128]{2,1,0:T(8,128)(2,1)S(1)}, u32[]{:S(2)}, u32[]{:S(2)}) %all-to-all-start.1) | async-done | bytes 589856 | tf_op jit(solution)/shard_map/all_to_all | solution.py:536
  91.0 1.5 collective-permute-start.17
  93.1 2.1 weight_part.4.weight_ref
  96.1 1.7 collective-permute-done.18.s2
  99.0 5.7 %collective-permute-start.20 = (bf16[4,128,128]{2,1,0:T(8,128)(2,1)S(1)}, bf16[4,128,128]{2,1,0:T(8,128)(2,1)S(1)}, u32[]{:S(2)}, u32[]{:S(2)}) collective-permute-start(bf16[4,128,128]{2,1,0:T(8,128)(2,1)S(1)} %upstream.4.own_ref), channel_id=1, source_target_pairs={{0,4},{4,0},{8,12},{12,8},{16,20},{20,16},{24,28},{28,24},{32,36},... | collective-permute-start | bytes 393224 | tf_op jit(solution)/shard_map/ppermute | solution.py:608
  106.4 8.5 %messages.4 = (bf16[4,8,288,128]{3,2,1,0:T(8,128)(2,1)}, bf16[2,2,4,64,128]{4,3,2,1,0:T(8,128)(2,1)}, bf16[2,2,4,64,128]{4,3,2,1,0:T(8,128)(2,1)}, bf16[2,2,4,64...) custom-call(s32[1324]{0:T(1024)} %concatenate.102.table, ...), custom_call_target="tpu_custom_call" | custom-call | bytes 19800000 | tf_op jit(solution)/shard_map/messages/pallas_call | solution.py:297
  115.0 4.7 %all-to-all-start.2 = ((bf16[4,8,288,128]{3,2,1,0:T(8,128)(2,1)}), bf16[4,8,288,128]{3,2,1,0:T(8,128)(2,1)}, u32[]{:S(2)}, u32[]{:S(2)}) async-start(bf16[4,8,288,128]{3,2,1,0:T(8,128)(2,1)} %get-tuple-element.129), calls=%async_computation.2 | async-start | bytes 4718592 | tf_op jit(solution)/shard_map/all_to_all | solution.py:527
  120.1 2.4 collective-permute-start.22
  122.5 6.5 %collective-permute-done.21.got_up = bf16[2,2,4,64,128]{4,3,2,1,0:T(8,128)(2,1)S(1)} collective-permute-done((bf16[2,2,4,64,128]{4,3,2,1,0:T(8,128)(2,1)S(1)}, bf16[2,2,4,64,128]{4,3,2,1,0:T(8,128)(2,1)S(1)}, u32[]{:S(2)}, u32[]{:S(2)}) %collective-permute-start.21) | collective-permute-done | bytes 262176 | tf_op jit(solution)/shard_map/ppermute | solution.py:469
  129.3 11.4 %collective-permute-start.24 = (bf16[2,2,4,64,128]{4,3,2,1,0:T(8,128)(2,1)S(1)}, bf16[2,2,4,64,128]{4,3,2,1,0:T(8,128)(2,1)S(1)}, u32[]{:S(2)}, u32[]{:S(2)}) collective-permute-start(bf16[2,2,4,64,128]{4,3,2,1,0:T(8,128)(2,1)S(1)} %get-tuple-element.124), channel_id=1, source_target_pairs={{0,224},{4,228},{8,232},{12,236},{16,240},{20,244},{24,248},{28,25... | collective-permute-start | bytes 786440 | tf_op jit(solution)/shard_map/ppermute | solution.py:470
  140.8 4.8 %collective-permute-done.24.got_down = bf16[2,2,4,64,128]{4,3,2,1,0:T(8,128)(2,1)S(1)} collective-permute-done((bf16[2,2,4,64,128]{4,3,2,1,0:T(8,128)(2,1)S(1)}, bf16[2,2,4,64,128]{4,3,2,1,0:T(8,128)(2,1)S(1)}, u32[]{:S(2)}, u32[]{:S(2)}) %collective-permute-start.24) | collective-permute-done | bytes 262176 | tf_op jit(solution)/shard_map/ppermute | solution.py:470
  145.9 3.3 %collective-permute-start.26 = (bf16[2,2,4,64,128]{4,3,2,1,0:T(8,128)(2,1)S(1)}, bf16[2,2,4,64,128]{4,3,2,1,0:T(8,128)(2,1)S(1)}, u32[]{:S(2)}, u32[]{:S(2)}) collective-permute-start(bf16[2,2,4,64,128]{4,3,2,1,0:T(8,128)(2,1)S(1)} %get-tuple-element.126), channel_id=1, source_target_pairs={{0,224},{4,228},{8,232},{12,236},{16,240},{20,244},{24,248},{28,25... | collective-permute-start | bytes 786440 | tf_op jit(solution)/shard_map/ppermute | solution.py:470
  149.1 4.6 %collective-permute-done.25.got_up = bf16[2,2,4,64,128]{4,3,2,1,0:T(8,128)(2,1)S(1)} collective-permute-done((bf16[2,2,4,64,128]{4,3,2,1,0:T(8,128)(2,1)S(1)}, bf16[2,2,4,64,128]{4,3,2,1,0:T(8,128)(2,1)S(1)}, u32[]{:S(2)}, u32[]{:S(2)}) %collective-permute-start.25) | collective-permute-done | bytes 262176 | tf_op jit(solution)/shard_map/ppermute | solution.py:469
  154.0 2.7 collective-permute-start.28
  156.7 2.4 sum_y.4
  159.1 3.9 %all-to-all-start.3 = ((bf16[8,288,128]{2,1,0:T(8,128)(2,1)}), bf16[8,288,128]{2,1,0:T(8,128)(2,1)S(1)}, u32[]{:S(2)}, u32[]{:S(2)}) async-start(bf16[8,288,128]{2,1,0:T(8,128)(2,1)} %sum_y.4), calls=%async_computation.3 | async-start | bytes 1179648 | tf_op jit(solution)/shard_map/all_to_all | solution.py:536
  163.2 2.7 collective-permute-start.30
  166.8 2.1 factors.3.refs_5_
  169.0 8.7 %all-to-all-done.3.from_z = bf16[8,288,128]{2,1,0:T(8,128)(2,1)S(1)} async-done(((bf16[8,288,128]{2,1,0:T(8,128)(2,1)}), bf16[8,288,128]{2,1,0:T(8,128)(2,1)S(1)}, u32[]{:S(2)}, u32[]{:S(2)}) %all-to-all-start.3) | async-done | bytes 589856 | tf_op jit(solution)/shard_map/all_to_all | solution.py:536
  178.8 1.9 collective-permute-start.34
  180.7 1.3 collective-permute-start.33
  182.0 2.1 weight_part.5.weight_ref
  184.1 3.0 %collective-permute-done.32.s1 = bf16[4,128,128]{2,1,0:T(8,128)(2,1)S(1)} collective-permute-done((bf16[4,128,128]{2,1,0:T(8,128)(2,1)S(1)}, bf16[4,128,128]{2,1,0:T(8,128)(2,1)S(1)}, u32[]{:S(2)}, u32[]{:S(2)}) %collective-permute-start.32) | collective-permute-done | bytes 131104 | tf_op jit(solution)/shard_map/ppermute | solution.py:602
  188.4 6.7 %collective-permute-start.35 = (bf16[4,128,128]{2,1,0:T(8,128)(2,1)S(1)}, bf16[4,128,128]{2,1,0:T(8,128)(2,1)S(1)}, u32[]{:S(2)}, u32[]{:S(2)}) collective-permute-start(bf16[4,128,128]{2,1,0:T(8,128)(2,1)S(1)} %upstream.5.own_ref), channel_id=1, source_target_pairs={{0,4},{4,0},{8,12},{12,8},{16,20},{20,16},{24,28},{28,24},{32,36},... | collective-permute-start | bytes 393224 | tf_op jit(solution)/shard_map/ppermute | solution.py:608
  196.7 8.5 %messages.5 = (bf16[4,8,288,128]{3,2,1,0:T(8,128)(2,1)}, bf16[2,2,4,64,128]{4,3,2,1,0:T(8,128)(2,1)}, bf16[2,2,4,64,128]{4,3,2,1,0:T(8,128)(2,1)}, bf16[2,2,4,64...) custom-call(s32[1324]{0:T(1024)} %concatenate.102.table, ...), custom_call_target="tpu_custom_call" | custom-call | bytes 19800000 | tf_op jit(solution)/shard_map/messages/pallas_call | solution.py:297
  205.3 4.6 %all-to-all-start.4 = ((bf16[4,8,288,128]{3,2,1,0:T(8,128)(2,1)}), bf16[4,8,288,128]{3,2,1,0:T(8,128)(2,1)}, u32[]{:S(2)}, u32[]{:S(2)}) async-start(bf16[4,8,288,128]{3,2,1,0:T(8,128)(2,1)} %get-tuple-element.156), calls=%async_computation.4 | async-start | bytes 4718592 | tf_op jit(solution)/shard_map/all_to_all | solution.py:527
  210.3 2.6 collective-permute-start.37
  213.0 6.2 %collective-permute-done.36.got_up = bf16[2,2,4,64,128]{4,3,2,1,0:T(8,128)(2,1)S(1)} collective-permute-done((bf16[2,2,4,64,128]{4,3,2,1,0:T(8,128)(2,1)S(1)}, bf16[2,2,4,64,128]{4,3,2,1,0:T(8,128)(2,1)S(1)}, u32[]{:S(2)}, u32[]{:S(2)}) %collective-permute-start.36) | collective-permute-done | bytes 262176 | tf_op jit(solution)/shard_map/ppermute | solution.py:469
  219.5 2.7 collective-permute-start.39
  222.2 5.7 %collective-permute-done.38.got_up = bf16[2,2,4,64,128]{4,3,2,1,0:T(8,128)(2,1)S(1)} collective-permute-done((bf16[2,2,4,64,128]{4,3,2,1,0:T(8,128)(2,1)S(1)}, bf16[2,2,4,64,128]{4,3,2,1,0:T(8,128)(2,1)S(1)}, u32[]{:S(2)}, u32[]{:S(2)}) %collective-permute-start.38) | collective-permute-done | bytes 262176 | tf_op jit(solution)/shard_map/ppermute | solution.py:469
  228.3 2.7 collective-permute-start.41
  230.9 4.9 %collective-permute-done.40.got_up = bf16[2,2,4,64,128]{4,3,2,1,0:T(8,128)(2,1)S(1)} collective-permute-done((bf16[2,2,4,64,128]{4,3,2,1,0:T(8,128)(2,1)S(1)}, bf16[2,2,4,64,128]{4,3,2,1,0:T(8,128)(2,1)S(1)}, u32[]{:S(2)}, u32[]{:S(2)}) %collective-permute-start.40) | collective-permute-done | bytes 262176 | tf_op jit(solution)/shard_map/ppermute | solution.py:469
  236.2 2.7 collective-permute-start.43
  239.2 2.4 sum_y.5
  241.7 17.8 %all_to_all.35.from_z = bf16[8,288,128]{2,1,0:T(8,128)(2,1)S(1)} all-to-all(bf16[8,288,128]{2,1,0:T(8,128)(2,1)} %sum_y.5), channel_id=1, replica_groups={{0,32,64,96,128,160,192,224},{4,36,68,100,132,164,196,228},{8,40,72,104..., dimensions={0} | all-to-all | bytes 1179648 | tf_op jit(solution)/shard_map/all_to_all | solution.py:536
  259.5 5.6 %collective-permute-start.47 = (f32[48,128]{1,0:T(8,128)S(1)}, f32[48,128]{1,0:T(8,128)S(1)}, u32[]{:S(2)}, u32[]{:S(2)}) collective-permute-start(f32[48,128]{1,0:T(8,128)S(1)} %pad_maximum_fusion.a_ref), channel_id=1, source_target_pairs={{0,4},{4,0},{8,12},{12,8},{16,20},{20,16},{24,28},{28,24},{32,36},... | collective-permute-start | bytes 73736 | tf_op jit(solution)/shard_map/ppermute | solution.py:199
  266.7 3.9 %all-to-all-start.6 = ((bf16[32,48,128]{2,1,0:T(8,128)(2,1)}), bf16[32,48,128]{2,1,0:T(8,128)(2,1)S(1)}, u32[]{:S(2)}, u32[]{:S(2)}) async-start(bf16[32,48,128]{2,1,0:T(8,128)(2,1)} %spread.1), calls=%async_computation.6 | async-start | bytes 786432 | tf_op jit(solution)/shard_map/all_to_all | solution.py:214
  270.7 1.2 collective-permute-start.44
  271.9 2.4 collective-permute-start.45
  274.3 1.2 collective-permute-start.46
  276.0 2.7 collective-permute-done.45.refs_2_
  278.6 1.4 collective-permute-done.46.refs_3_
  280.9 4.1 %all-to-all-done.6 = bf16[32,48,128]{2,1,0:T(8,128)(2,1)S(1)} async-done(((bf16[32,48,128]{2,1,0:T(8,128)(2,1)}), bf16[32,48,128]{2,1,0:T(8,128)(2,1)S(1)}, u32[]{:S(2)}, u32[]{:S(2)}) %all-to-all-start.6) | async-done | bytes 393248 | tf_op jit(solution)/shard_map/all_to_all | solution.py:214
  (185 shorter events, 28.6 us)
Async XLA Ops:
  0.7 19.6 %collective-permute-start.5 = (bf16[128,128,128]{2,1,0:T(8,128)(2,1)}, bf16[128,128,128]{2,1,0:T(8,128)(2,1)}, u32[]{:S(2)}, u32[]{:S(2)}) collective-permute-start(bf16[128,128,128]{2,1,0:T(8,128)(2,1)} %a_own.5), channel_id=1, source_target_pairs={{0,4},{4,0},{8,12},{12,8},{16,20},{20,16},{24,28},{28,24},{32,36},... | collective-permute-start | bytes 12582920 | tf_op jit(solution)/shard_map/ppermute | solution.py:591
  6.2 10.9 %collective-permute-start.1 = (bf16[4,128,128]{2,1,0:T(8,128)(2,1)}, bf16[4,128,128]{2,1,0:T(8,128)(2,1)S(1)}, u32[]{:S(2)}, u32[]{:S(2)}) collective-permute-start(bf16[4,128,128]{2,1,0:T(8,128)(2,1)} %get-tuple-element.85.refs_1_.s0), channel_id=1, source_target_pairs={{0,1},{1,2},{2,3},{3,0},{4,5},{5,6},{6,7},{7,4},{8,9},{9,10},{10,1... | collective-permute-start | bytes 393224 | tf_op jit(solution)/shard_map/ppermute | solution.py:602
  6.2 10.9 %collective-permute-start.2 = (bf16[4,128,128]{2,1,0:T(8,128)(2,1)}, bf16[4,128,128]{2,1,0:T(8,128)(2,1)S(1)}, u32[]{:S(2)}, u32[]{:S(2)}) collective-permute-start(bf16[4,128,128]{2,1,0:T(8,128)(2,1)} %get-tuple-element.85.refs_1_.s0), channel_id=1, source_target_pairs={{0,2},{1,3},{2,0},{3,1},{4,6},{5,7},{6,4},{7,5},{8,10},{9,11},{10,... | collective-permute-start | bytes 393224 | tf_op jit(solution)/shard_map/ppermute | solution.py:602
  8.1 9.0 %collective-permute-start.3 = (bf16[4,128,128]{2,1,0:T(8,128)(2,1)}, bf16[4,128,128]{2,1,0:T(8,128)(2,1)S(1)}, u32[]{:S(2)}, u32[]{:S(2)}) collective-permute-start(bf16[4,128,128]{2,1,0:T(8,128)(2,1)} %get-tuple-element.85.refs_1_.s0), channel_id=1, source_target_pairs={{0,3},{1,0},{2,1},{3,2},{4,7},{5,4},{6,5},{7,6},{8,11},{9,8},{10,9... | collective-permute-start | bytes 393224 | tf_op jit(solution)/shard_map/ppermute | solution.py:602
  11.2 4.1 %collective-permute-start = (s32[2,128]{1,0:T(2,128)S(1)}, s32[2,128]{1,0:T(2,128)S(1)}, u32[]{:S(2)}, u32[]{:S(2)}) collective-permute-start(s32[2,128]{1,0:T(2,128)S(1)} %pad_add_fusion), channel_id=1, source_target_pairs={{0,4},{4,0},{8,12},{12,8},{16,20},{20,16},{24,28},{28,24},{32,36},... | collective-permute-start | bytes 3080 | tf_op jit(solution)/shard_map/ppermute | solution.py:545
  17.4 2.8 collective-permute-start.4
  29.5 24.4 %copy-start.20 = (bf16[2,2,4,64,128]{4,3,2,1,0:T(8,128)(2,1)S(1)}, bf16[2,2,4,64,128]{4,3,2,1,0:T(8,128)(2,1)}, u32[]{:S(2)}) copy-start(bf16[2,2,4,64,128]{4,3,2,1,0:T(8,128)(2,1)} %get-tuple-element.90.q_up) | copy-start | bytes 786436
  29.5 24.4 %copy-start.21 = (bf16[2,2,4,64,128]{4,3,2,1,0:T(8,128)(2,1)S(1)}, bf16[2,2,4,64,128]{4,3,2,1,0:T(8,128)(2,1)}, u32[]{:S(2)}) copy-start(bf16[2,2,4,64,128]{4,3,2,1,0:T(8,128)(2,1)} %get-tuple-element.91.q_down) | copy-start | bytes 786436
  29.6 32.4 %copy-start.14 = (bf16[2,2,4,64,128]{4,3,2,1,0:T(8,128)(2,1)S(1)}, bf16[2,2,4,64,128]{4,3,2,1,0:T(8,128)(2,1)}, u32[]{:S(2)}) copy-start(bf16[2,2,4,64,128]{4,3,2,1,0:T(8,128)(2,1)} %get-tuple-element.89.q_down) | copy-start | bytes 786436
  29.6 32.3 %copy-start.15 = (bf16[2,2,4,64,128]{4,3,2,1,0:T(8,128)(2,1)S(1)}, bf16[2,2,4,64,128]{4,3,2,1,0:T(8,128)(2,1)}, u32[]{:S(2)}) copy-start(bf16[2,2,4,64,128]{4,3,2,1,0:T(8,128)(2,1)} %get-tuple-element.88.q_up) | copy-start | bytes 786436
  29.6 35.3 %all-to-all-start = ((bf16[4,8,288,128]{3,2,1,0:T(8,128)(2,1)}), bf16[4,8,288,128]{3,2,1,0:T(8,128)(2,1)}, u32[]{:S(2)}, u32[]{:S(2)}) async-start(bf16[4,8,288,128]{3,2,1,0:T(8,128)(2,1)} %get-tuple-element.102), calls=%async_computation | async-start | bytes 4718592 | tf_op jit(solution)/shard_map/all_to_all | solution.py:527
  34.3 11.4 %collective-permute-start.6 = (bf16[2,2,4,64,128]{4,3,2,1,0:T(8,128)(2,1)S(1)}, bf16[2,2,4,64,128]{4,3,2,1,0:T(8,128)(2,1)S(1)}, u32[]{:S(2)}, u32[]{:S(2)}) collective-permute-start(bf16[2,2,4,64,128]{4,3,2,1,0:T(8,128)(2,1)S(1)} %copy-done.38), channel_id=1, source_target_pairs={{0,32},{4,36},{8,40},{12,44},{16,48},{20,52},{24,56},{28,60},{32,6... | collective-permute-start | bytes 786440 | tf_op jit(solution)/shard_map/ppermute | solution.py:469
  36.0 9.7 %collective-permute-start.7 = (bf16[2,2,4,64,128]{4,3,2,1,0:T(8,128)(2,1)S(1)}, bf16[2,2,4,64,128]{4,3,2,1,0:T(8,128)(2,1)S(1)}, u32[]{:S(2)}, u32[]{:S(2)}) collective-permute-start(bf16[2,2,4,64,128]{4,3,2,1,0:T(8,128)(2,1)S(1)} %copy-done.35), channel_id=1, source_target_pairs={{0,224},{4,228},{8,232},{12,236},{16,240},{20,244},{24,248},{28,25... | collective-permute-start | bytes 786440 | tf_op jit(solution)/shard_map/ppermute | solution.py:470
  45.9 8.0 %collective-permute-start.8 = (bf16[2,2,4,64,128]{4,3,2,1,0:T(8,128)(2,1)S(1)}, bf16[2,2,4,64,128]{4,3,2,1,0:T(8,128)(2,1)S(1)}, u32[]{:S(2)}, u32[]{:S(2)}) collective-permute-start(bf16[2,2,4,64,128]{4,3,2,1,0:T(8,128)(2,1)S(1)} %get-tuple-element.96), channel_id=1, source_target_pairs={{0,32},{4,36},{8,40},{12,44},{16,48},{20,52},{24,56},{28,60},{32,6... | collective-permute-start | bytes 786440 | tf_op jit(solution)/shard_map/ppermute | solution.py:469
  46.0 7.9 %collective-permute-start.9 = (bf16[2,2,4,64,128]{4,3,2,1,0:T(8,128)(2,1)S(1)}, bf16[2,2,4,64,128]{4,3,2,1,0:T(8,128)(2,1)S(1)}, u32[]{:S(2)}, u32[]{:S(2)}) collective-permute-start(bf16[2,2,4,64,128]{4,3,2,1,0:T(8,128)(2,1)S(1)} %get-tuple-element.97), channel_id=1, source_target_pairs={{0,224},{4,228},{8,232},{12,236},{16,240},{20,244},{24,248},{28,25... | collective-permute-start | bytes 786440 | tf_op jit(solution)/shard_map/ppermute | solution.py:470
  54.2 7.2 %collective-permute-start.10 = (bf16[2,2,4,64,128]{4,3,2,1,0:T(8,128)(2,1)S(1)}, bf16[2,2,4,64,128]{4,3,2,1,0:T(8,128)(2,1)S(1)}, u32[]{:S(2)}, u32[]{:S(2)}) collective-permute-start(bf16[2,2,4,64,128]{4,3,2,1,0:T(8,128)(2,1)S(1)} %get-tuple-element.98), channel_id=1, source_target_pairs={{0,32},{4,36},{8,40},{12,44},{16,48},{20,52},{24,56},{28,60},{32,6... | collective-permute-start | bytes 786440 | tf_op jit(solution)/shard_map/ppermute | solution.py:469
  56.0 5.9 %collective-permute-start.11 = (bf16[2,2,4,64,128]{4,3,2,1,0:T(8,128)(2,1)S(1)}, bf16[2,2,4,64,128]{4,3,2,1,0:T(8,128)(2,1)S(1)}, u32[]{:S(2)}, u32[]{:S(2)}) collective-permute-start(bf16[2,2,4,64,128]{4,3,2,1,0:T(8,128)(2,1)S(1)} %get-tuple-element.99), channel_id=1, source_target_pairs={{0,224},{4,228},{8,232},{12,236},{16,240},{20,244},{24,248},{28,25... | collective-permute-start | bytes 786440 | tf_op jit(solution)/shard_map/ppermute | solution.py:470
  62.1 5.2 %collective-permute-start.12 = (bf16[2,4,64,128]{3,2,1,0:T(8,128)(2,1)S(1)}, bf16[2,4,64,128]{3,2,1,0:T(8,128)(2,1)S(1)}, u32[]{:S(2)}, u32[]{:S(2)}) collective-permute-start(bf16[2,4,64,128]{3,2,1,0:T(8,128)(2,1)S(1)} %get-tuple-element.100), channel_id=1, source_target_pairs={{0,32},{4,36},{8,40},{12,44},{16,48},{20,52},{24,56},{28,60},{32,6... | collective-permute-start | bytes 393224 | tf_op jit(solution)/shard_map/ppermute | solution.py:474
  63.8 3.8 %collective-permute-start.13 = (bf16[2,4,64,128]{3,2,1,0:T(8,128)(2,1)S(1)}, bf16[2,4,64,128]{3,2,1,0:T(8,128)(2,1)S(1)}, u32[]{:S(2)}, u32[]{:S(2)}) collective-permute-start(bf16[2,4,64,128]{3,2,1,0:T(8,128)(2,1)S(1)} %get-tuple-element.101), channel_id=1, source_target_pairs={{0,224},{4,228},{8,232},{12,236},{16,240},{20,244},{24,248},{28,25... | collective-permute-start | bytes 393224 | tf_op jit(solution)/shard_map/ppermute | solution.py:475
  67.6 22.2 %all-to-all-start.1 = ((bf16[8,288,128]{2,1,0:T(8,128)(2,1)}), bf16[8,288,128]{2,1,0:T(8,128)(2,1)S(1)}, u32[]{:S(2)}, u32[]{:S(2)}) async-start(bf16[8,288,128]{2,1,0:T(8,128)(2,1)} %sum_y.3), calls=%async_computation.1 | async-start | bytes 1179648 | tf_op jit(solution)/shard_map/all_to_all | solution.py:536
  73.7 5.1 %collective-permute-start.14 = (bf16[4,64,128]{2,1,0:T(8,128)(2,1)S(1)}, bf16[4,64,128]{2,1,0:T(8,128)(2,1)S(1)}, u32[]{:S(2)}, u32[]{:S(2)}) collective-permute-start(bf16[4,64,128]{2,1,0:T(8,128)(2,1)S(1)} %get-tuple-element.108), channel_id=1, source_target_pairs={{0,8},{4,12},{8,16},{12,20},{16,24},{20,28},{24,0},{28,4},{32,40},... | collective-permute-start | bytes 196616 | tf_op jit(solution)/shard_map/ppermute | solution.py:537
  74.0 4.7 %collective-permute-start.15 = (bf16[4,64,128]{2,1,0:T(8,128)(2,1)S(1)}, bf16[4,64,128]{2,1,0:T(8,128)(2,1)S(1)}, u32[]{:S(2)}, u32[]{:S(2)}) collective-permute-start(bf16[4,64,128]{2,1,0:T(8,128)(2,1)S(1)} %get-tuple-element.109), channel_id=1, source_target_pairs={{0,16},{4,20},{8,24},{12,28},{16,0},{20,4},{24,8},{28,12},{32,48},... | collective-permute-start | bytes 196616 | tf_op jit(solution)/shard_map/ppermute | solution.py:537
  76.2 3.2 %collective-permute-start.16 = (bf16[4,64,128]{2,1,0:T(8,128)(2,1)S(1)}, bf16[4,64,128]{2,1,0:T(8,128)(2,1)S(1)}, u32[]{:S(2)}, u32[]{:S(2)}) collective-permute-start(bf16[4,64,128]{2,1,0:T(8,128)(2,1)S(1)} %get-tuple-element.110), channel_id=1, source_target_pairs={{0,24},{4,28},{8,0},{12,4},{16,8},{20,12},{24,16},{28,20},{32,56},... | collective-permute-start | bytes 196616 | tf_op jit(solution)/shard_map/ppermute | solution.py:537
  90.9 4.3 %collective-permute-start.19 = (bf16[4,128,128]{2,1,0:T(8,128)(2,1)S(1)}, bf16[4,128,128]{2,1,0:T(8,128)(2,1)S(1)}, u32[]{:S(2)}, u32[]{:S(2)}) collective-permute-start(bf16[4,128,128]{2,1,0:T(8,128)(2,1)S(1)} %get-tuple-element.112.refs_1_.s0), channel_id=1, source_target_pairs={{0,3},{1,0},{2,1},{3,2},{4,7},{5,4},{6,5},{7,6},{8,11},{9,8},{10,9... | collective-permute-start | bytes 393224 | tf_op jit(solution)/shard_map/ppermute | solution.py:602
  91.0 5.1 %collective-permute-start.17 = (bf16[4,128,128]{2,1,0:T(8,128)(2,1)S(1)}, bf16[4,128,128]{2,1,0:T(8,128)(2,1)S(1)}, u32[]{:S(2)}, u32[]{:S(2)}) collective-permute-start(bf16[4,128,128]{2,1,0:T(8,128)(2,1)S(1)} %get-tuple-element.112.refs_1_.s0), channel_id=1, source_target_pairs={{0,1},{1,2},{2,3},{3,0},{4,5},{5,6},{6,7},{7,4},{8,9},{9,10},{10,1... | collective-permute-start | bytes 393224 | tf_op jit(solution)/shard_map/ppermute | solution.py:602
  92.5 5.3 %collective-permute-start.18 = (bf16[4,128,128]{2,1,0:T(8,128)(2,1)S(1)}, bf16[4,128,128]{2,1,0:T(8,128)(2,1)S(1)}, u32[]{:S(2)}, u32[]{:S(2)}) collective-permute-start(bf16[4,128,128]{2,1,0:T(8,128)(2,1)S(1)} %get-tuple-element.112.refs_1_.s0), channel_id=1, source_target_pairs={{0,2},{1,3},{2,0},{3,1},{4,6},{5,7},{6,4},{7,5},{8,10},{9,11},{10,... | collective-permute-start | bytes 393224 | tf_op jit(solution)/shard_map/ppermute | solution.py:602
  99.0 6.7 %collective-permute-start.20 = (bf16[4,128,128]{2,1,0:T(8,128)(2,1)S(1)}, bf16[4,128,128]{2,1,0:T(8,128)(2,1)S(1)}, u32[]{:S(2)}, u32[]{:S(2)}) collective-permute-start(bf16[4,128,128]{2,1,0:T(8,128)(2,1)S(1)} %upstream.4.own_ref), channel_id=1, source_target_pairs={{0,4},{4,0},{8,12},{12,8},{16,20},{20,16},{24,28},{28,24},{32,36},... | collective-permute-start | bytes 393224 | tf_op jit(solution)/shard_map/ppermute | solution.py:608
  115.0 30.6 %copy-start.22 = (bf16[2,2,4,64,128]{4,3,2,1,0:T(8,128)(2,1)S(1)}, bf16[2,2,4,64,128]{4,3,2,1,0:T(8,128)(2,1)}, u32[]{:S(2)}) copy-start(bf16[2,2,4,64,128]{4,3,2,1,0:T(8,128)(2,1)} %get-tuple-element.117.q_up) | copy-start | bytes 786436
  115.0 30.6 %copy-start.23 = (bf16[2,2,4,64,128]{4,3,2,1,0:T(8,128)(2,1)S(1)}, bf16[2,2,4,64,128]{4,3,2,1,0:T(8,128)(2,1)}, u32[]{:S(2)}) copy-start(bf16[2,2,4,64,128]{4,3,2,1,0:T(8,128)(2,1)} %get-tuple-element.118.q_down) | copy-start | bytes 786436
  115.0 38.7 %copy-start.16 = (bf16[2,2,4,64,128]{4,3,2,1,0:T(8,128)(2,1)S(1)}, bf16[2,2,4,64,128]{4,3,2,1,0:T(8,128)(2,1)}, u32[]{:S(2)}) copy-start(bf16[2,2,4,64,128]{4,3,2,1,0:T(8,128)(2,1)} %get-tuple-element.116.q_down) | copy-start | bytes 786436
  115.0 38.7 %copy-start.17 = (bf16[2,2,4,64,128]{4,3,2,1,0:T(8,128)(2,1)S(1)}, bf16[2,2,4,64,128]{4,3,2,1,0:T(8,128)(2,1)}, u32[]{:S(2)}) copy-start(bf16[2,2,4,64,128]{4,3,2,1,0:T(8,128)(2,1)} %get-tuple-element.115.q_up) | copy-start | bytes 786436
  115.0 41.7 %all-to-all-start.2 = ((bf16[4,8,288,128]{3,2,1,0:T(8,128)(2,1)}), bf16[4,8,288,128]{3,2,1,0:T(8,128)(2,1)}, u32[]{:S(2)}, u32[]{:S(2)}) async-start(bf16[4,8,288,128]{3,2,1,0:T(8,128)(2,1)} %get-tuple-element.129), calls=%async_computation.2 | async-start | bytes 4718592 | tf_op jit(solution)/shard_map/all_to_all | solution.py:527
  119.7 9.3 %collective-permute-start.21 = (bf16[2,2,4,64,128]{4,3,2,1,0:T(8,128)(2,1)S(1)}, bf16[2,2,4,64,128]{4,3,2,1,0:T(8,128)(2,1)S(1)}, u32[]{:S(2)}, u32[]{:S(2)}) collective-permute-start(bf16[2,2,4,64,128]{4,3,2,1,0:T(8,128)(2,1)S(1)} %copy-done.39), channel_id=1, source_target_pairs={{0,32},{4,36},{8,40},{12,44},{16,48},{20,52},{24,56},{28,60},{32,6... | collective-permute-start | bytes 786440 | tf_op jit(solution)/shard_map/ppermute | solution.py:469
  120.1 8.9 %collective-permute-start.22 = (bf16[2,2,4,64,128]{4,3,2,1,0:T(8,128)(2,1)S(1)}, bf16[2,2,4,64,128]{4,3,2,1,0:T(8,128)(2,1)S(1)}, u32[]{:S(2)}, u32[]{:S(2)}) collective-permute-start(bf16[2,2,4,64,128]{4,3,2,1,0:T(8,128)(2,1)S(1)} %copy-done.36), channel_id=1, source_target_pairs={{0,224},{4,228},{8,232},{12,236},{16,240},{20,244},{24,248},{28,25... | collective-permute-start | bytes 786440 | tf_op jit(solution)/shard_map/ppermute | solution.py:470
  129.2 11.5 %collective-permute-start.23 = (bf16[2,2,4,64,128]{4,3,2,1,0:T(8,128)(2,1)S(1)}, bf16[2,2,4,64,128]{4,3,2,1,0:T(8,128)(2,1)S(1)}, u32[]{:S(2)}, u32[]{:S(2)}) collective-permute-start(bf16[2,2,4,64,128]{4,3,2,1,0:T(8,128)(2,1)S(1)} %get-tuple-element.123), channel_id=1, source_target_pairs={{0,32},{4,36},{8,40},{12,44},{16,48},{20,52},{24,56},{28,60},{32,6... | collective-permute-start | bytes 786440 | tf_op jit(solution)/shard_map/ppermute | solution.py:469
  129.3 16.2 %collective-permute-start.24 = (bf16[2,2,4,64,128]{4,3,2,1,0:T(8,128)(2,1)S(1)}, bf16[2,2,4,64,128]{4,3,2,1,0:T(8,128)(2,1)S(1)}, u32[]{:S(2)}, u32[]{:S(2)}) collective-permute-start(bf16[2,2,4,64,128]{4,3,2,1,0:T(8,128)(2,1)S(1)} %get-tuple-element.124), channel_id=1, source_target_pairs={{0,224},{4,228},{8,232},{12,236},{16,240},{20,244},{24,248},{28,25... | collective-permute-start | bytes 786440 | tf_op jit(solution)/shard_map/ppermute | solution.py:470
  145.8 7.9 %collective-permute-start.25 = (bf16[2,2,4,64,128]{4,3,2,1,0:T(8,128)(2,1)S(1)}, bf16[2,2,4,64,128]{4,3,2,1,0:T(8,128)(2,1)S(1)}, u32[]{:S(2)}, u32[]{:S(2)}) collective-permute-start(bf16[2,2,4,64,128]{4,3,2,1,0:T(8,128)(2,1)S(1)} %get-tuple-element.125), channel_id=1, source_target_pairs={{0,32},{4,36},{8,40},{12,44},{16,48},{20,52},{24,56},{28,60},{32,6... | collective-permute-start | bytes 786440 | tf_op jit(solution)/shard_map/ppermute | solution.py:469
  145.9 7.8 %collective-permute-start.26 = (bf16[2,2,4,64,128]{4,3,2,1,0:T(8,128)(2,1)S(1)}, bf16[2,2,4,64,128]{4,3,2,1,0:T(8,128)(2,1)S(1)}, u32[]{:S(2)}, u32[]{:S(2)}) collective-permute-start(bf16[2,2,4,64,128]{4,3,2,1,0:T(8,128)(2,1)S(1)} %get-tuple-element.126), channel_id=1, source_target_pairs={{0,224},{4,228},{8,232},{12,236},{16,240},{20,244},{24,248},{28,25... | collective-permute-start | bytes 786440 | tf_op jit(solution)/shard_map/ppermute | solution.py:470
  153.9 5.2 %collective-permute-start.27 = (bf16[2,4,64,128]{3,2,1,0:T(8,128)(2,1)S(1)}, bf16[2,4,64,128]{3,2,1,0:T(8,128)(2,1)S(1)}, u32[]{:S(2)}, u32[]{:S(2)}) collective-permute-start(bf16[2,4,64,128]{3,2,1,0:T(8,128)(2,1)S(1)} %get-tuple-element.127), channel_id=1, source_target_pairs={{0,32},{4,36},{8,40},{12,44},{16,48},{20,52},{24,56},{28,60},{32,6... | collective-permute-start | bytes 393224 | tf_op jit(solution)/shard_map/ppermute | solution.py:474
  154.0 5.1 %collective-permute-start.28 = (bf16[2,4,64,128]{3,2,1,0:T(8,128)(2,1)S(1)}, bf16[2,4,64,128]{3,2,1,0:T(8,128)(2,1)S(1)}, u32[]{:S(2)}, u32[]{:S(2)}) collective-permute-start(bf16[2,4,64,128]{3,2,1,0:T(8,128)(2,1)S(1)} %get-tuple-element.128), channel_id=1, source_target_pairs={{0,224},{4,228},{8,232},{12,236},{16,240},{20,244},{24,248},{28,25... | collective-permute-start | bytes 393224 | tf_op jit(solution)/shard_map/ppermute | solution.py:475
  159.1 18.6 %all-to-all-start.3 = ((bf16[8,288,128]{2,1,0:T(8,128)(2,1)}), bf16[8,288,128]{2,1,0:T(8,128)(2,1)S(1)}, u32[]{:S(2)}, u32[]{:S(2)}) async-start(bf16[8,288,128]{2,1,0:T(8,128)(2,1)} %sum_y.4), calls=%async_computation.3 | async-start | bytes 1179648 | tf_op jit(solution)/shard_map/all_to_all | solution.py:536
  163.0 5.9 %collective-permute-start.29 = (bf16[4,64,128]{2,1,0:T(8,128)(2,1)S(1)}, bf16[4,64,128]{2,1,0:T(8,128)(2,1)S(1)}, u32[]{:S(2)}, u32[]{:S(2)}) collective-permute-start(bf16[4,64,128]{2,1,0:T(8,128)(2,1)S(1)} %get-tuple-element.135), channel_id=1, source_target_pairs={{0,8},{4,12},{8,16},{12,20},{16,24},{20,28},{24,0},{28,4},{32,40},... | collective-permute-start | bytes 196616 | tf_op jit(solution)/shard_map/ppermute | solution.py:537
  163.2 5.7 %collective-permute-start.30 = (bf16[4,64,128]{2,1,0:T(8,128)(2,1)S(1)}, bf16[4,64,128]{2,1,0:T(8,128)(2,1)S(1)}, u32[]{:S(2)}, u32[]{:S(2)}) collective-permute-start(bf16[4,64,128]{2,1,0:T(8,128)(2,1)S(1)} %get-tuple-element.136), channel_id=1, source_target_pairs={{0,16},{4,20},{8,24},{12,28},{16,0},{20,4},{24,8},{28,12},{32,48},... | collective-permute-start | bytes 196616 | tf_op jit(solution)/shard_map/ppermute | solution.py:537
  165.9 3.1 %collective-permute-start.31 = (bf16[4,64,128]{2,1,0:T(8,128)(2,1)S(1)}, bf16[4,64,128]{2,1,0:T(8,128)(2,1)S(1)}, u32[]{:S(2)}, u32[]{:S(2)}) collective-permute-start(bf16[4,64,128]{2,1,0:T(8,128)(2,1)S(1)} %get-tuple-element.137), channel_id=1, source_target_pairs={{0,24},{4,28},{8,0},{12,4},{16,8},{20,12},{24,16},{28,20},{32,56},... | collective-permute-start | bytes 196616 | tf_op jit(solution)/shard_map/ppermute | solution.py:537
  178.8 5.3 %collective-permute-start.34 = (bf16[4,128,128]{2,1,0:T(8,128)(2,1)S(1)}, bf16[4,128,128]{2,1,0:T(8,128)(2,1)S(1)}, u32[]{:S(2)}, u32[]{:S(2)}) collective-permute-start(bf16[4,128,128]{2,1,0:T(8,128)(2,1)S(1)} %get-tuple-element.139.refs_1_.s0), channel_id=1, source_target_pairs={{0,3},{1,0},{2,1},{3,2},{4,7},{5,4},{6,5},{7,6},{8,11},{9,8},{10,9... | collective-permute-start | bytes 393224 | tf_op jit(solution)/shard_map/ppermute | solution.py:602
  180.7 6.4 %collective-permute-start.32 = (bf16[4,128,128]{2,1,0:T(8,128)(2,1)S(1)}, bf16[4,128,128]{2,1,0:T(8,128)(2,1)S(1)}, u32[]{:S(2)}, u32[]{:S(2)}) collective-permute-start(bf16[4,128,128]{2,1,0:T(8,128)(2,1)S(1)} %get-tuple-element.139.refs_1_.s0), channel_id=1, source_target_pairs={{0,1},{1,2},{2,3},{3,0},{4,5},{5,6},{6,7},{7,4},{8,9},{9,10},{10,1... | collective-permute-start | bytes 393224 | tf_op jit(solution)/shard_map/ppermute | solution.py:602
  180.7 6.4 %collective-permute-start.33 = (bf16[4,128,128]{2,1,0:T(8,128)(2,1)S(1)}, bf16[4,128,128]{2,1,0:T(8,128)(2,1)S(1)}, u32[]{:S(2)}, u32[]{:S(2)}) collective-permute-start(bf16[4,128,128]{2,1,0:T(8,128)(2,1)S(1)} %get-tuple-element.139.refs_1_.s0), channel_id=1, source_target_pairs={{0,2},{1,3},{2,0},{3,1},{4,6},{5,7},{6,4},{7,5},{8,10},{9,11},{10,... | collective-permute-start | bytes 393224 | tf_op jit(solution)/shard_map/ppermute | solution.py:602
  188.4 7.6 %collective-permute-start.35 = (bf16[4,128,128]{2,1,0:T(8,128)(2,1)S(1)}, bf16[4,128,128]{2,1,0:T(8,128)(2,1)S(1)}, u32[]{:S(2)}, u32[]{:S(2)}) collective-permute-start(bf16[4,128,128]{2,1,0:T(8,128)(2,1)S(1)} %upstream.5.own_ref), channel_id=1, source_target_pairs={{0,4},{4,0},{8,12},{12,8},{16,20},{20,16},{24,28},{28,24},{32,36},... | collective-permute-start | bytes 393224 | tf_op jit(solution)/shard_map/ppermute | solution.py:608
  205.3 30.6 %copy-start.12 = (bf16[2,2,4,64,128]{4,3,2,1,0:T(8,128)(2,1)S(1)}, bf16[2,2,4,64,128]{4,3,2,1,0:T(8,128)(2,1)}, u32[]{:S(2)}) copy-start(bf16[2,2,4,64,128]{4,3,2,1,0:T(8,128)(2,1)} %get-tuple-element.143.q_down) | copy-start | bytes 786436
  205.3 30.6 %copy-start.13 = (bf16[2,2,4,64,128]{4,3,2,1,0:T(8,128)(2,1)S(1)}, bf16[2,2,4,64,128]{4,3,2,1,0:T(8,128)(2,1)}, u32[]{:S(2)}) copy-start(bf16[2,2,4,64,128]{4,3,2,1,0:T(8,128)(2,1)} %get-tuple-element.142.q_up) | copy-start | bytes 786436
  205.3 33.9 %all-to-all-start.4 = ((bf16[4,8,288,128]{3,2,1,0:T(8,128)(2,1)}), bf16[4,8,288,128]{3,2,1,0:T(8,128)(2,1)}, u32[]{:S(2)}, u32[]{:S(2)}) async-start(bf16[4,8,288,128]{3,2,1,0:T(8,128)(2,1)} %get-tuple-element.156), calls=%async_computation.4 | async-start | bytes 4718592 | tf_op jit(solution)/shard_map/all_to_all | solution.py:527
  210.0 9.3 %collective-permute-start.36 = (bf16[2,2,4,64,128]{4,3,2,1,0:T(8,128)(2,1)S(1)}, bf16[2,2,4,64,128]{4,3,2,1,0:T(8,128)(2,1)S(1)}, u32[]{:S(2)}, u32[]{:S(2)}) collective-permute-start(bf16[2,2,4,64,128]{4,3,2,1,0:T(8,128)(2,1)S(1)} %copy-done.37), channel_id=1, source_target_pairs={{0,32},{4,36},{8,40},{12,44},{16,48},{20,52},{24,56},{28,60},{32,6... | collective-permute-start | bytes 786440 | tf_op jit(solution)/shard_map/ppermute | solution.py:469
  210.3 8.9 %collective-permute-start.37 = (bf16[2,2,4,64,128]{4,3,2,1,0:T(8,128)(2,1)S(1)}, bf16[2,2,4,64,128]{4,3,2,1,0:T(8,128)(2,1)S(1)}, u32[]{:S(2)}, u32[]{:S(2)}) collective-permute-start(bf16[2,2,4,64,128]{4,3,2,1,0:T(8,128)(2,1)S(1)} %copy-done.34), channel_id=1, source_target_pairs={{0,224},{4,228},{8,232},{12,236},{16,240},{20,244},{24,248},{28,25... | collective-permute-start | bytes 786440 | tf_op jit(solution)/shard_map/ppermute | solution.py:470
  219.5 8.5 %collective-permute-start.38 = (bf16[2,2,4,64,128]{4,3,2,1,0:T(8,128)(2,1)S(1)}, bf16[2,2,4,64,128]{4,3,2,1,0:T(8,128)(2,1)S(1)}, u32[]{:S(2)}, u32[]{:S(2)}) collective-permute-start(bf16[2,2,4,64,128]{4,3,2,1,0:T(8,128)(2,1)S(1)} %get-tuple-element.150), channel_id=1, source_target_pairs={{0,32},{4,36},{8,40},{12,44},{16,48},{20,52},{24,56},{28,60},{32,6... | collective-permute-start | bytes 786440 | tf_op jit(solution)/shard_map/ppermute | solution.py:469
  219.5 8.4 %collective-permute-start.39 = (bf16[2,2,4,64,128]{4,3,2,1,0:T(8,128)(2,1)S(1)}, bf16[2,2,4,64,128]{4,3,2,1,0:T(8,128)(2,1)S(1)}, u32[]{:S(2)}, u32[]{:S(2)}) collective-permute-start(bf16[2,2,4,64,128]{4,3,2,1,0:T(8,128)(2,1)S(1)} %get-tuple-element.151), channel_id=1, source_target_pairs={{0,224},{4,228},{8,232},{12,236},{16,240},{20,244},{24,248},{28,25... | collective-permute-start | bytes 786440 | tf_op jit(solution)/shard_map/ppermute | solution.py:470
  228.2 7.7 %collective-permute-start.40 = (bf16[2,2,4,64,128]{4,3,2,1,0:T(8,128)(2,1)S(1)}, bf16[2,2,4,64,128]{4,3,2,1,0:T(8,128)(2,1)S(1)}, u32[]{:S(2)}, u32[]{:S(2)}) collective-permute-start(bf16[2,2,4,64,128]{4,3,2,1,0:T(8,128)(2,1)S(1)} %get-tuple-element.152), channel_id=1, source_target_pairs={{0,32},{4,36},{8,40},{12,44},{16,48},{20,52},{24,56},{28,60},{32,6... | collective-permute-start | bytes 786440 | tf_op jit(solution)/shard_map/ppermute | solution.py:469
  228.3 7.6 %collective-permute-start.41 = (bf16[2,2,4,64,128]{4,3,2,1,0:T(8,128)(2,1)S(1)}, bf16[2,2,4,64,128]{4,3,2,1,0:T(8,128)(2,1)S(1)}, u32[]{:S(2)}, u32[]{:S(2)}) collective-permute-start(bf16[2,2,4,64,128]{4,3,2,1,0:T(8,128)(2,1)S(1)} %get-tuple-element.153), channel_id=1, source_target_pairs={{0,224},{4,228},{8,232},{12,236},{16,240},{20,244},{24,248},{28,25... | collective-permute-start | bytes 786440 | tf_op jit(solution)/shard_map/ppermute | solution.py:470
  236.1 5.6 %collective-permute-start.42 = (bf16[2,4,64,128]{3,2,1,0:T(8,128)(2,1)S(1)}, bf16[2,4,64,128]{3,2,1,0:T(8,128)(2,1)S(1)}, u32[]{:S(2)}, u32[]{:S(2)}) collective-permute-start(bf16[2,4,64,128]{3,2,1,0:T(8,128)(2,1)S(1)} %get-tuple-element.154), channel_id=1, source_target_pairs={{0,32},{4,36},{8,40},{12,44},{16,48},{20,52},{24,56},{28,60},{32,6... | collective-permute-start | bytes 393224 | tf_op jit(solution)/shard_map/ppermute | solution.py:474
  236.2 5.5 %collective-permute-start.43 = (bf16[2,4,64,128]{3,2,1,0:T(8,128)(2,1)S(1)}, bf16[2,4,64,128]{3,2,1,0:T(8,128)(2,1)S(1)}, u32[]{:S(2)}, u32[]{:S(2)}) collective-permute-start(bf16[2,4,64,128]{3,2,1,0:T(8,128)(2,1)S(1)} %get-tuple-element.155), channel_id=1, source_target_pairs={{0,224},{4,228},{8,232},{12,236},{16,240},{20,244},{24,248},{28,25... | collective-permute-start | bytes 393224 | tf_op jit(solution)/shard_map/ppermute | solution.py:475
  259.5 6.5 %collective-permute-start.47 = (f32[48,128]{1,0:T(8,128)S(1)}, f32[48,128]{1,0:T(8,128)S(1)}, u32[]{:S(2)}, u32[]{:S(2)}) collective-permute-start(f32[48,128]{1,0:T(8,128)S(1)} %pad_maximum_fusion.a_ref), channel_id=1, source_target_pairs={{0,4},{4,0},{8,12},{12,8},{16,20},{20,16},{24,28},{28,24},{32,36},... | collective-permute-start | bytes 73736 | tf_op jit(solution)/shard_map/ppermute | solution.py:199
  266.7 18.3 %all-to-all-start.6 = ((bf16[32,48,128]{2,1,0:T(8,128)(2,1)}), bf16[32,48,128]{2,1,0:T(8,128)(2,1)S(1)}, u32[]{:S(2)}, u32[]{:S(2)}) async-start(bf16[32,48,128]{2,1,0:T(8,128)(2,1)} %spread.1), calls=%async_computation.6 | async-start | bytes 786432 | tf_op jit(solution)/shard_map/all_to_all | solution.py:214
  270.7 5.3 %collective-permute-start.44 = (bf16[4,64,128]{2,1,0:T(8,128)(2,1)S(1)}, bf16[4,64,128]{2,1,0:T(8,128)(2,1)S(1)}, u32[]{:S(2)}, u32[]{:S(2)}) collective-permute-start(bf16[4,64,128]{2,1,0:T(8,128)(2,1)S(1)} %get-tuple-element.162), channel_id=1, source_target_pairs={{0,8},{4,12},{8,16},{12,20},{16,24},{20,28},{24,0},{28,4},{32,40},... | collective-permute-start | bytes 196616 | tf_op jit(solution)/shard_map/ppermute | solution.py:537
  271.9 6.8 %collective-permute-start.45 = (bf16[4,64,128]{2,1,0:T(8,128)(2,1)S(1)}, bf16[4,64,128]{2,1,0:T(8,128)(2,1)S(1)}, u32[]{:S(2)}, u32[]{:S(2)}) collective-permute-start(bf16[4,64,128]{2,1,0:T(8,128)(2,1)S(1)} %get-tuple-element.163), channel_id=1, source_target_pairs={{0,16},{4,20},{8,24},{12,28},{16,0},{20,4},{24,8},{28,12},{32,48},... | collective-permute-start | bytes 196616 | tf_op jit(solution)/shard_map/ppermute | solution.py:537
  274.3 5.8 %collective-permute-start.46 = (bf16[4,64,128]{2,1,0:T(8,128)(2,1)S(1)}, bf16[4,64,128]{2,1,0:T(8,128)(2,1)S(1)}, u32[]{:S(2)}, u32[]{:S(2)}) collective-permute-start(bf16[4,64,128]{2,1,0:T(8,128)(2,1)S(1)} %get-tuple-element.164), channel_id=1, source_target_pairs={{0,24},{4,28},{8,0},{12,4},{16,8},{20,12},{24,16},{28,20},{32,56},... | collective-permute-start | bytes 196616 | tf_op jit(solution)/shard_map/ppermute | solution.py:537
  (31 other events, 249.3 us)
